TPU v7x, 256 devices: a whole 4x4x8 slice. The times are simulated.
256 devices in a mesh: expert: 8 (over z), tensor: 32 (over x, y, core).
Axes of the slice: x: 4, y: 4, z: 8, core: 2. Of those that a mesh axis runs over, the one named last changes fastest.
Arguments:
- tokens: bfloat16 [1024, 7168], P('expert', 'tensor'), may hold values from -48 to 48
- norm_gain: float32 [7168], replicated, may hold values from 0.25 to 1.75
- route_ids: int32 [1024, 2], P('expert'), may hold values from 0 to 7, all different within a row; in each aligned block of 128 rows (0 to 127, 128 to 255, ...) at most 48 rows name the same one
- route_probs: float32 [1024, 2], P('expert'), may hold values from 0.2 to 1
- dense_gate: bfloat16 [4864, 7168], P('tensor'), may hold values from -0.0625 to 0.0625
- dense_up: bfloat16 [4864, 7168], P('tensor'), may hold values from -0.0625 to 0.0625
- dense_down: bfloat16 [4864, 7168], P('tensor'), may hold values from -0.15625 to 0.15625
- expert_gate: bfloat16 [8, 4864, 7168], P('expert', 'tensor'), may hold values from -0.0625 to 0.0625
- expert_up: bfloat16 [8, 4864, 7168], P('expert', 'tensor'), may hold values from -0.0625 to 0.0625
- expert_down: bfloat16 [8, 4864, 7168], P('expert', 'tensor'), may hold values from -0.15625 to 0.15625
Outputs:
- block_out: bfloat16 [1024, 7168], P('expert', 'tensor')
Inputs may be any that keep to these rules, and one draw needn't show every extreme that they name: `route_ids`: in each aligned block of 128 rows (the rows of one index of the expert axis) no expert is named by more than 48 rows, a bound that some block reaches; the 2 ids of a row differ.
All inputs are finite; a program needn't handle non-finite values.
Results may differ from a plain program's by a relative error of at most 0.0064.
Values may be sent and summed in bfloat16 or wider, within the bound.
No kernel may reach another device: no remote copies, remote signals or barrier semaphores. Data moves between devices by JAX's collectives and lax.ppermute only.
A program may use at most 128 MiB of HBM per device.

v0:
```python
import functools

import jax
import jax.numpy as jnp
from jax import lax
from jax.experimental import pallas as pl
from jax.experimental.pallas import tpu as pltpu
from jax.sharding import PartitionSpec as P

SIDE = 4
PAIR = 2
CHIPS = SIDE * SIDE
GROUP = CHIPS * PAIR
F32 = jnp.float32
BF16 = jnp.bfloat16
MIB = 1024 * 1024
MOST = 56 * MIB
CHUNK = 896
SMALL = pl.CostEstimate(flops=MIB, bytes_accessed=MIB, transcendentals=0)


def device_of(x, y, core):
    return (x * SIDE + y) * PAIR + core


def hops(step, first):
    pairs = []
    for x in range(SIDE):
        for y in range(SIDE):
            for core in range(PAIR):
                along_x = (core == 0) == first
                to_x = (x + step) % SIDE if along_x else x
                to_y = y if along_x else (y + step) % SIDE
                pairs.append((device_of(x, y, core), device_of(to_x, to_y, core)))
    return pairs


def sibling(value):
    return lax.ppermute(value, "tensor", [(i, i ^ 1) for i in range(GROUP)])


def piece_index(place, other, sign, outer, inner):
    x, y, core = place[0], place[1], place[2]
    owner = 1 - core if other else core
    move_x = jnp.where(owner == 0, inner, outer)
    move_y = jnp.where(owner == 0, outer, inner)
    at_x = lax.rem(x + sign * move_x + SIDE, SIDE)
    at_y = lax.rem(y + sign * move_y + SIDE, SIDE)
    return device_of(at_x, at_y, owner)


def dispatch_kernel(experts, capacity, ids, probs, tokens, outgoing, combine):
    choose, rows = ids.shape
    slots = experts * capacity
    numbers = lax.broadcasted_iota(jnp.int32, (experts, rows), 0)
    before = lax.broadcasted_iota(jnp.int32, (rows, rows), 0)
    after = lax.broadcasted_iota(jnp.int32, (rows, rows), 1)
    earlier = (before < after).astype(F32).astype(BF16)
    slot_numbers = lax.broadcasted_iota(jnp.int32, (slots, rows), 0)
    taken = jnp.zeros((experts, 1), F32)
    weights = jnp.zeros((slots, rows), F32)
    chosen = jnp.zeros((slots, rows), F32)
    for k in range(choose):
        named = ids[k : k + 1, :]
        onehot = (numbers == named).astype(F32)
        ahead = jnp.dot(onehot.astype(BF16), earlier, preferred_element_type=F32) + taken
        position = jnp.sum(ahead * onehot, axis=0, keepdims=True).astype(jnp.int32)
        hits = slot_numbers == named * capacity + position
        weights = weights + jnp.where(hits, probs[k : k + 1, :], 0.0)
        chosen = chosen + hits.astype(F32)
        taken = taken + jnp.sum(onehot, axis=1, keepdims=True)
    combine[...] = weights
    outgoing[...] = lax.dot_general(
        chosen.astype(BF16), tokens[...], (((1,), (1,)), ((), ())), preferred_element_type=F32
    ).astype(BF16)


def dispatched(ids, probs, tokens, experts, capacity):
    cols, rows = tokens.shape
    return pl.pallas_call(
        functools.partial(dispatch_kernel, experts, capacity),
        out_shape=(
            jax.ShapeDtypeStruct((experts * capacity, cols), BF16),
            jax.ShapeDtypeStruct((experts * capacity, rows), F32),
        ),
        name="dispatch",
    )(ids, probs, tokens)


def up_weights_kernel(cols, gain, gate, up, out):
    for i in range(gate.shape[1] // cols):
        at = slice(i * cols, (i + 1) * cols)
        both = jnp.concatenate([gate[:, at].astype(F32), up[:, at].astype(F32)], axis=0)
        out[i] = (both * gain[:, at]).astype(BF16)


def up_weights(gain, gate, up, cols):
    units, width = gate.shape
    wide = pl.BlockSpec((units, CHUNK), lambda i: (0, i))
    return pl.pallas_call(
        functools.partial(up_weights_kernel, cols),
        out_shape=jax.ShapeDtypeStruct((width // cols, 2 * units, cols), BF16),
        grid=(width // CHUNK,),
        in_specs=[pl.BlockSpec((1, CHUNK), lambda i: (0, i)), wide, wide],
        out_specs=pl.BlockSpec((CHUNK // cols, 2 * units, cols), lambda i: (i, 0, 0)),
        compiler_params=pltpu.CompilerParams(vmem_limit_bytes=MOST),
        cost_estimate=SMALL,
        name="up_weights",
    )(gain, gate, up)


def down_weights_kernel(cols, down, out):
    for i in range(down.shape[1] // cols):
        out[i] = down[:, i * cols : (i + 1) * cols].astype(F32).T.astype(BF16)


def down_weights(down, cols):
    units, width = down.shape
    return pl.pallas_call(
        functools.partial(down_weights_kernel, cols),
        out_shape=jax.ShapeDtypeStruct((width // cols, cols, units), BF16),
        grid=(width // CHUNK,),
        in_specs=[pl.BlockSpec((units, CHUNK), lambda i: (0, i))],
        out_specs=pl.BlockSpec((CHUNK // cols, cols, units), lambda i: (i, 0, 0)),
        compiler_params=pltpu.CompilerParams(vmem_limit_bytes=MOST),
        cost_estimate=SMALL,
        name="down_weights",
    )(down)


def arrive_kernel(dense_rows, count, start, last, width, place, *refs):
    stacks, dense, routed = (refs[i * count : (i + 1) * count] for i in range(3))
    refs = refs[3 * count :]
    if not start:
        carried, refs = refs[:3], refs[3:]
    if last:
        hidden, refs = refs[0], refs[1:]
    dense_sum, routed_sum, squares = refs

    @pl.when(pl.program_id(0) == 0)
    def _():
        for i, ref in enumerate(refs):
            ref[...] = jnp.zeros_like(ref) if start else carried[i][...]

    for stack, dense_weight, routed_weight in zip(stacks, dense, routed):
        block = stack[0]
        dense_sum[...] += jnp.dot(
            dense_weight[0], block[:, :dense_rows], preferred_element_type=F32
        )
        routed_sum[...] += jnp.dot(
            routed_weight[0], block[:, dense_rows:], preferred_element_type=F32
        )
        values = block.astype(F32)
        values = values * values
        squares[...] += jnp.sum(values.reshape(values.shape[0] // 8, 8, values.shape[1]), axis=0)

    if last:

        @pl.when(pl.program_id(0) == pl.num_programs(0) - 1)
        def _():
            scale = lax.rsqrt(jnp.sum(squares[...], axis=0, keepdims=True) / width + 1e-05)
            units = dense_sum.shape[0] // 2
            for sums, span in (
                (dense_sum, slice(0, dense_rows)),
                (routed_sum, slice(dense_rows, scale.shape[1])),
            ):
                gates = sums[:units, :] * scale[:, span]
                ups = sums[units:, :] * scale[:, span]
                hidden[:, span] = (gates / (1.0 + jnp.exp(-gates)) * ups).astype(BF16)


def arrive(place, stage, weights, sums, dense_rows, last=False):
    count = len(stage)
    pieces, cols, rows = stage[0][0].shape
    height = weights[0].shape[1]
    start = sums is None

    def weight(outer, inner, other):
        def index(i, place):
            return piece_index(place, other, -1, outer, inner + i), 0, 0

        return pl.BlockSpec((1, height, cols), index)

    whole = lambda shape: pl.BlockSpec(shape, lambda i, place: (0, 0))
    shapes = [(height, dense_rows), (height, rows - dense_rows), (8, rows)]
    sum_specs = [whole(s) for s in shapes]
    if last:
        out_specs = whole((height // 2, rows))
        out_shape = jax.ShapeDtypeStruct((height // 2, rows), BF16)
        scratch = [pltpu.VMEM(s, F32) for s in shapes]
    else:
        out_specs, scratch = sum_specs, []
        out_shape = [jax.ShapeDtypeStruct(s, F32) for s in shapes]
    return pl.pallas_call(
        functools.partial(arrive_kernel, dense_rows, count, start, last, GROUP * cols),
        out_shape=out_shape,
        grid_spec=pltpu.PrefetchScalarGridSpec(
            num_scalar_prefetch=1,
            grid=(pieces,),
            in_specs=[pl.BlockSpec((1, cols, rows), lambda i, place: (i, 0, 0))] * count
            + [weight(*rest) for _, *rest in stage] * 2
            + ([] if start else sum_specs),
            out_specs=out_specs,
            scratch_shapes=scratch,
        ),
        compiler_params=pltpu.CompilerParams(vmem_limit_bytes=24 * MIB),
        cost_estimate=SMALL,
        name=f"arrive_{stage[-1][1]}_{count}",
    )(
        place,
        *[stack for stack, *_ in stage],
        *[weights[0]] * count,
        *[weights[1]] * count,
        *([] if start else sums),
    )


def down_kernel(dense_rows, place, hidden, *refs):
    mine, others = refs[4:]
    for out, dense, routed in ((mine, refs[0], refs[1]), (others, refs[2], refs[3])):
        for weight, span in (
            (dense, slice(0, dense_rows)),
            (routed, slice(dense_rows, hidden.shape[1])),
        ):
            out[0, :, span] = jnp.dot(
                weight[0], hidden[:, span], preferred_element_type=F32
            ).astype(out.dtype)


def down_pieces(place, hidden, weights, outer, dense_rows):
    units, rows = hidden.shape
    cols = weights[0].shape[1]

    def weight(other):
        def index(i, place):
            return piece_index(place, other, 1, outer, i), 0, 0

        return pl.BlockSpec((1, cols, units), index)

    out = pl.BlockSpec((1, cols, rows), lambda i, place: (i, 0, 0))
    shape = (SIDE, cols, rows)
    return pl.pallas_call(
        functools.partial(down_kernel, dense_rows),
        out_shape=(jax.ShapeDtypeStruct(shape, F32), jax.ShapeDtypeStruct(shape, BF16)),
        grid_spec=pltpu.PrefetchScalarGridSpec(
            num_scalar_prefetch=1,
            grid=(SIDE,),
            in_specs=[pl.BlockSpec((units, rows), lambda i, place: (0, 0))]
            + [weight(False)] * 2
            + [weight(True)] * 2,
            out_specs=(out, out),
        ),
        compiler_params=pltpu.CompilerParams(vmem_limit_bytes=16 * MIB),
        cost_estimate=SMALL,
        name=f"down_pieces_{outer}",
    )(place, hidden, weights[0], weights[1], weights[0], weights[1])


def shards(
    tokens,
    norm_gain,
    route_ids,
    route_probs,
    dense_gate,
    dense_up,
    dense_down,
    expert_gate,
    expert_up,
    expert_down,
):
    experts = lax.axis_size("expert")
    rows, choose = route_ids.shape
    cols = tokens.shape[1]
    capacity = 3 * rows * choose // (2 * experts)
    index = lax.axis_index("tensor")
    place = jnp.stack([index // (SIDE * PAIR), index // PAIR % SIDE, index % PAIR]).astype(jnp.int32)

    gain = norm_gain[None, :]

    outgoing, combine = dispatched(route_ids.T, route_probs.T, tokens.T, experts, capacity)
    received = lax.all_to_all(
        outgoing.reshape(experts, capacity, cols), "expert", 0, 0, tiled=True
    ).reshape(experts * capacity, cols)
    weights = [
        up_weights(gain, dense_gate, dense_up, cols),
        up_weights(gain, expert_gate[0], expert_up[0], cols),
    ]
    received, weights = lax.optimization_barrier((received, weights))
    own = jnp.concatenate([tokens.T, received.T], axis=1)

    def level_one(value, d):
        return lax.ppermute(value, "tensor", hops(d, True))

    def level_two(value, d):
        return lax.ppermute(value, "tensor", hops(d, False))

    arrived = [level_one(own, d) for d in range(1, SIDE)]
    routed_down = down_weights(expert_down[0], cols)
    arrived, routed_down = lax.optimization_barrier((arrived, routed_down))
    stack = jnp.stack([own] + arrived)
    near, far, left = [level_two(stack, d) for d in range(1, SIDE)]
    stack_other = sibling(stack)
    down = [down_weights(dense_down, cols), routed_down]
    add = functools.partial(arrive, place, weights=weights, dense_rows=rows)
    sums = add([(stack, 0, 0, False)], sums=None)
    near, stack_other, sums, down = lax.optimization_barrier((near, stack_other, sums, down))
    near_other = sibling(near)
    sums = add([(stack_other, 0, 0, True), (near, 1, 0, False)], sums=sums)
    far, left, sums = lax.optimization_barrier((far, left, sums))
    far_other, left_other = sibling(far), sibling(left)
    sums = add([(near_other, 1, 0, True), (far, 2, 0, False), (left, 3, 0, False)], sums=sums)
    far_other, left_other, sums = lax.optimization_barrier((far_other, left_other, sums))
    hidden = add([(far_other, 2, 0, True), (left_other, 3, 0, True)], sums=sums, last=True)

    pieces = {}
    for outer in (1, 2, 3, 0):
        mine, others = down_pieces(place, hidden, down, outer, rows)
        if outer > 1:
            pieces[outer - 1], hidden = lax.optimization_barrier((pieces[outer - 1], hidden))
        pieces[outer] = mine + sibling(others).astype(F32)
    level = pieces[0]
    for d in range(1, SIDE):
        level = level + level_two(pieces[d].astype(BF16), d).astype(F32)
    total = level[0]
    for d in range(1, SIDE):
        total = total + level_one(level[d].astype(BF16), d).astype(F32)

    back = total[:, rows:].astype(BF16).T.reshape(experts, capacity, cols)
    returned = lax.all_to_all(back, "expert", 0, 0, tiled=True).reshape(experts * capacity, cols)
    moe_out = jnp.dot(combine.T, returned.astype(F32), precision=lax.Precision.HIGHEST)
    return (total[:, :rows].T + moe_out).astype(BF16)


def solution(mesh):
    in_specs = (
        P("expert", "tensor"),
        P(),
        P("expert", None),
        P("expert", None),
        P("tensor", None),
        P("tensor", None),
        P("tensor", None),
        P("expert", "tensor", None),
        P("expert", "tensor", None),
        P("expert", "tensor", None),
    )
    out_specs = P("expert", "tensor")
    return jax.shard_map(shards, mesh=mesh, in_specs=in_specs, out_specs=out_specs, check_vma=False)
```

profile of v0, /device:TPU:8, one launch (start us, length us, event | category | flops | bytes accessed | tf_op | source)
XLA Modules:
  0.0 140.7 jit_solution(9459109116042605592)
XLA Ops:
  0.0 1.9 %dispatch.1 = (bf16[384,224]{1,0:T(8,128)(2,1)}, f32[384,128]{1,0:T(8,128)}) custom-call(s32[2,128]{1,0:T(2,128)} %bitcast.59, f32[2,128]{1,0:T(2,128)} %bitcast.60, bf16[224,128]{1,0:T(8,128)(2,1)} %bitcast.54), custom_call_target="tpu_custom_call" | custom-call | tf_op jit(solution)/shard_map/dispatch/pallas_call | solution.py:80
  1.9 8.5 %all-to-all-start = ((bf16[8,48,224]{2,1,0:T(8,128)(2,1)}), bf16[8,48,224]{2,1,0:T(8,128)(2,1)S(1)}, u32[]{:S(2)}, u32[]{:S(2)}) async-start(bf16[8,48,224]{2,1,0:T(8,128)(2,1)} %bitcast.56), calls=%async_computation | async-start | bytes 393216 | tf_op jit(solution)/shard_map/all_to_all | solution.py:281
  10.4 7.8 %up_weights.3.refs_2_.refs_4_.refs_5_.refs_6_.refs_7_.refs_8_ = bf16[32,304,224]{2,1,0:T(8,128)(2,1)} custom-call(f32[1,7168]{1,0:T(1,128)} %bitcast.57, bf16[152,7168]{1,0:T(8,128)(2,1)} %bitcast.44, bf16[152,7168]{1,0:T(8,128)(2,1)} %bitcast.45), custom_call_target="tpu_custom_call" | custom-call | flops 1048576 | bytes 1048576 | tf_op jit(solution)/shard_map/up_weights/pallas_call | solution.py:100
  18.2 7.8 %up_weights.2.refs_1_.refs_2_.refs_3_.refs_4_.refs_5_ = bf16[32,304,224]{2,1,0:T(8,128)(2,1)} custom-call(f32[1,7168]{1,0:T(1,128)} %bitcast.58, bf16[152,7168]{1,0:T(8,128)(2,1)} %gate.1, bf16[152,7168]{1,0:T(8,128)(2,1)} %up.1), custom_call_target="tpu_custom_call" | custom-call | flops 1048576 | bytes 1048576 | tf_op jit(solution)/shard_map/up_weights/pallas_call | solution.py:100
  25.9 0.0 all-to-all-done
  25.9 0.1 copy.12
  26.2 3.1 %collective-permute-start.1 = (bf16[224,512]{1,0:T(8,128)(2,1)S(1)}, bf16[224,512]{1,0:T(8,128)(2,1)S(1)}, u32[]{:S(2)}, u32[]{:S(2)}) collective-permute-start(bf16[224,512]{1,0:T(8,128)(2,1)S(1)} %get-tuple-element.105), channel_id=1, source_target_pairs={{0,16},{1,5},{2,18},{3,7},{4,20},{5,1},{6,22},{7,3},{8,24},{9,13},... | collective-permute-start | bytes 688136 | tf_op jit(solution)/shard_map/ppermute | solution.py:292
  29.3 0.6 collective-permute-start
  29.9 2.6 %collective-permute-start.2 = (bf16[224,512]{1,0:T(8,128)(2,1)S(1)}, bf16[224,512]{1,0:T(8,128)(2,1)S(1)}, u32[]{:S(2)}, u32[]{:S(2)}) collective-permute-start(bf16[224,512]{1,0:T(8,128)(2,1)S(1)} %get-tuple-element.105), channel_id=1, source_target_pairs={{0,24},{1,7},{2,26},{3,1},{4,28},{5,3},{6,30},{7,5},{8,0},{9,15},{... | collective-permute-start | bytes 688136 | tf_op jit(solution)/shard_map/ppermute | solution.py:292
  32.5 7.5 %down_weights.2.refs_1_.refs_3_ = bf16[32,224,152]{2,1,0:T(8,128)(2,1)} custom-call(bf16[152,7168]{1,0:T(8,128)(2,1)} %bitcast.46), custom_call_target="tpu_custom_call" | custom-call | flops 1048576 | bytes 1048576 | tf_op jit(solution)/shard_map/down_weights/pallas_call | solution.py:119
  40.0 0.0 collective-permute-done.1
  40.0 0.0 collective-permute-done
  40.0 0.0 collective-permute-done.2
  40.0 0.1 pad_maximum_fusion.refs_0_
  40.1 0.1 collective-permute-start.6
  40.2 1.7 %collective-permute-start.5 = (bf16[4,224,512]{2,1,0:T(8,128)(2,1)S(1)}, bf16[4,224,512]{2,1,0:T(8,128)(2,1)}, u32[]{:S(2)}, u32[]{:S(2)}) collective-permute-start(bf16[4,224,512]{2,1,0:T(8,128)(2,1)S(1)} %pad_maximum_fusion.refs_0_), channel_id=1, source_target_pairs={{0,2},{1,9},{2,4},{3,11},{4,6},{5,13},{6,0},{7,15},{8,10},{9,17},{... | collective-permute-start | bytes 2752520 | tf_op jit(solution)/shard_map/ppermute | solution.py:295
  41.9 0.4 collective-permute-start.4
  42.3 2.3 %collective-permute-start.3 = (bf16[4,224,512]{2,1,0:T(8,128)(2,1)S(1)}, bf16[4,224,512]{2,1,0:T(8,128)(2,1)S(1)}, u32[]{:S(2)}, u32[]{:S(2)}) collective-permute-start(bf16[4,224,512]{2,1,0:T(8,128)(2,1)S(1)} %pad_maximum_fusion.refs_0_), channel_id=1, source_target_pairs={{0,4},{1,17},{2,6},{3,19},{4,0},{5,21},{6,2},{7,23},{8,12},{9,25},... | collective-permute-start | bytes 2752520 | tf_op jit(solution)/shard_map/ppermute | solution.py:295
  44.6 7.4 %down_weights.3.refs_0_.refs_2_ = bf16[32,224,152]{2,1,0:T(8,128)(2,1)} custom-call(bf16[152,7168]{1,0:T(8,128)(2,1)} %down.1), custom_call_target="tpu_custom_call" | custom-call | flops 1048576 | bytes 1048576 | tf_op jit(solution)/shard_map/down_weights/pallas_call | solution.py:119
  52.1 0.1 pad_add_fusion.place
  52.1 2.4 %copy-done = bf16[32,304,224]{2,1,0:T(8,128)(2,1)S(1)} copy-done((bf16[32,304,224]{2,1,0:T(8,128)(2,1)S(1)}, bf16[32,304,224]{2,1,0:T(8,128)(2,1)}, u32[]{:S(2)}) %copy-start) | copy-done | bytes 4358168
  54.6 2.4 %copy-done.1 = bf16[32,304,224]{2,1,0:T(8,128)(2,1)S(1)} copy-done((bf16[32,304,224]{2,1,0:T(8,128)(2,1)S(1)}, bf16[32,304,224]{2,1,0:T(8,128)(2,1)}, u32[]{:S(2)}) %copy-start.1) | copy-done | bytes 4358168
  57.0 1.8 %arrive_0_1.1 = (f32[304,128]{1,0:T(8,128)S(1)}, f32[304,384]{1,0:T(8,128)S(1)}, f32[8,512]{1,0:T(8,128)S(1)}) custom-call(s32[3]{0:T(128)S(1)} %pad_add_fusion.place, bf16[4,224,512]{2,1,0:T(8,128)(2,1)S(1)} %pad_maximum_fusion.refs_0_, bf16[32,304,224]{2,1,0:T(8,128)(2,1)S(1)} %copy-done.1, bf16[32,304,224]{2,1,0:T(8,128)(2,1)S(1)} %copy-done), custom_call_target="tpu_custom_call" | custom-call | flops 1048576 | bytes 1048576 | tf_op jit(solution)/shard_map/arrive_0_1/pallas_call | solution.py:194
  58.8 0.0 collective-permute-done.6.refs_0_
  58.8 5.4 %collective-permute-start.9 = (bf16[4,224,512]{2,1,0:T(8,128)(2,1)}, bf16[4,224,512]{2,1,0:T(8,128)(2,1)S(1)}, u32[]{:S(2)}, u32[]{:S(2)}) collective-permute-start(bf16[4,224,512]{2,1,0:T(8,128)(2,1)} %collective-permute-done.5.refs_1_), channel_id=1, source_target_pairs={{0,1},{1,0},{2,3},{3,2},{4,5},{5,4},{6,7},{7,6},{8,9},{9,8},{10,11... | collective-permute-start | bytes 2752520 | tf_op jit(solution)/shard_map/ppermute | solution.py:39
  64.1 4.0 %arrive_1_2.1 = (f32[304,128]{1,0:T(8,128)S(1)}, f32[304,384]{1,0:T(8,128)S(1)}, f32[8,512]{1,0:T(8,128)S(1)}) custom-call(s32[3]{0:T(128)S(1)} %pad_add_fusion.place, bf16[4,224,512]{2,1,0:T(8,128)(2,1)} %collective-permute-done.6.refs_0_, bf16[4,224,512]{2,1,0:T(8,128)(2,1)} %collective-permute-done.5.refs_1_, bf16[32,304,224]{2,1,0:T(8,128)(2,1)S(1)} %copy-done.1, ...), custom_call_target="tpu_custom_call" | custom-call | flops 1048576 | bytes 1048576 | tf_op jit(solution)/shard_map/arrive_1_2/pallas_call | solution.py:194
  68.2 0.0 collective-permute-done.3.refs_1_
  68.2 0.1 collective-permute-start.7
  68.3 0.5 collective-permute-start.8
  68.8 0.0 collective-permute-done.9.refs_0_
  68.8 2.9 %arrive_3_3.1 = (f32[304,128]{1,0:T(8,128)S(1)}, f32[304,384]{1,0:T(8,128)S(1)}, f32[8,512]{1,0:T(8,128)S(1)}) custom-call(s32[3]{0:T(128)S(1)} %pad_add_fusion.place, bf16[4,224,512]{2,1,0:T(8,128)(2,1)S(1)} %collective-permute-done.9.refs_0_, bf16[4,224,512]{2,1,0:T(8,128)(2,1)S(1)} %collective-permute-done.3.refs_1_, ...), custom_call_target="tpu_custom_call" | custom-call | flops 1048576 | bytes 1048576 | tf_op jit(solution)/shard_map/arrive_3_3/pallas_call | solution.py:194
  71.7 0.4 collective-permute-done.8.refs_1_
  72.1 2.5 %arrive_3_2.1.hidden = bf16[152,512]{1,0:T(8,128)(2,1)S(1)} custom-call(s32[3]{0:T(128)S(1)} %pad_add_fusion.place, bf16[4,224,512]{2,1,0:T(8,128)(2,1)S(1)} %collective-permute-done.7.refs_0_, bf16[4,224,512]{2,1,0:T(8,128)(2,1)S(1)} %collective-permute-done.8.refs_1_, bf16[32,304,224]{2,1,0:T(8,128)(2,1)S(1)} %copy-done.1, ...), custom_call_target="tpu_custom_call" | custom-call | flops 1048576 | bytes 1048576 | tf_op jit(solution)/shard_map/arrive_3_2/pallas_call | solution.py:194
  74.6 0.7 copy-done.3
  75.2 1.9 %down_pieces_1.1 = (f32[4,224,512]{2,1,0:T(8,128)S(1)}, bf16[4,224,512]{2,1,0:T(8,128)(2,1)S(1)}) custom-call(s32[3]{0:T(128)S(1)} %pad_add_fusion.place, bf16[152,512]{1,0:T(8,128)(2,1)S(1)} %arrive_3_2.1.hidden, bf16[32,224,152]{2,1,0:T(8,128)(2,1)S(1)} %copy-done.3, bf16[32,224,152]{2,1,0:T(8,128)(2,1)S(1)} %copy-done.2, ...), custom_call_target="tpu_custom_call" | custom-call | flops 1048576 | bytes 1048576 | tf_op jit(solution)/shard_map/down_pieces_1/pallas_call | solution.py:242
  77.1 0.2 collective-permute-start.11
  77.4 1.9 %down_pieces_2.1 = (f32[4,224,512]{2,1,0:T(8,128)S(1)}, bf16[4,224,512]{2,1,0:T(8,128)(2,1)S(1)}) custom-call(s32[3]{0:T(128)S(1)} %pad_add_fusion.place, bf16[152,512]{1,0:T(8,128)(2,1)S(1)} %arrive_3_2.1.hidden, bf16[32,224,152]{2,1,0:T(8,128)(2,1)S(1)} %copy-done.3, bf16[32,224,152]{2,1,0:T(8,128)(2,1)S(1)} %copy-done.2, ...), custom_call_target="tpu_custom_call" | custom-call | flops 1048576 | bytes 1048576 | tf_op jit(solution)/shard_map/down_pieces_2/pallas_call | solution.py:242
  79.2 0.6 collective-permute-start.10
  79.9 0.0 collective-permute-done.11
  79.9 0.3 convert_add_fusion.1
  80.2 1.9 %down_pieces_3.1 = (f32[4,224,512]{2,1,0:T(8,128)S(1)}, bf16[4,224,512]{2,1,0:T(8,128)(2,1)S(1)}) custom-call(s32[3]{0:T(128)S(1)} %pad_add_fusion.place, bf16[152,512]{1,0:T(8,128)(2,1)S(1)} %arrive_3_2.1.hidden, bf16[32,224,152]{2,1,0:T(8,128)(2,1)S(1)} %copy-done.3, bf16[32,224,152]{2,1,0:T(8,128)(2,1)S(1)} %copy-done.2, ...), custom_call_target="tpu_custom_call" | custom-call | flops 1048576 | bytes 1048576 | tf_op jit(solution)/shard_map/down_pieces_3/pallas_call | solution.py:242
  82.1 0.2 collective-permute-start.15
  82.3 1.5 %collective-permute-start.13 = (bf16[4,224,512]{2,1,0:T(8,128)(2,1)S(1)}, bf16[4,224,512]{2,1,0:T(8,128)(2,1)S(1)}, u32[]{:S(2)}, u32[]{:S(2)}) collective-permute-start(bf16[4,224,512]{2,1,0:T(8,128)(2,1)S(1)} %convert_add_fusion.1), channel_id=1, source_target_pairs={{0,2},{1,9},{2,4},{3,11},{4,6},{5,13},{6,0},{7,15},{8,10},{9,17},{... | collective-permute-start | bytes 2752520 | tf_op jit(solution)/shard_map/ppermute | solution.py:295
  83.9 0.0 collective-permute-done.10
  83.9 0.4 convert_add_fusion.2
  84.2 1.9 %down_pieces_0.1 = (f32[4,224,512]{2,1,0:T(8,128)S(1)}, bf16[4,224,512]{2,1,0:T(8,128)(2,1)S(1)}) custom-call(s32[3]{0:T(128)S(1)} %pad_add_fusion.place, bf16[152,512]{1,0:T(8,128)(2,1)S(1)} %arrive_3_2.1.hidden, bf16[32,224,152]{2,1,0:T(8,128)(2,1)S(1)} %copy-done.3, bf16[32,224,152]{2,1,0:T(8,128)(2,1)S(1)} %copy-done.2, ...), custom_call_target="tpu_custom_call" | custom-call | flops 1048576 | bytes 1048576 | tf_op jit(solution)/shard_map/down_pieces_0/pallas_call | solution.py:242
  86.1 0.1 collective-permute-start.12
  86.2 1.3 collective-permute-start.14
  87.5 0.4 add_convert_fusion
  87.9 2.4 %collective-permute-start.16 = (bf16[4,224,512]{2,1,0:T(8,128)(2,1)S(1)}, bf16[4,224,512]{2,1,0:T(8,128)(2,1)S(1)}, u32[]{:S(2)}, u32[]{:S(2)}) collective-permute-start(bf16[4,224,512]{2,1,0:T(8,128)(2,1)S(1)} %add_convert_fusion), channel_id=1, source_target_pairs={{0,6},{1,25},{2,0},{3,27},{4,2},{5,29},{6,4},{7,31},{8,14},{9,1},{... | collective-permute-start | bytes 2752520 | tf_op jit(solution)/shard_map/ppermute | solution.py:295
  90.3 5.4 %collective-permute-done.13 = bf16[4,224,512]{2,1,0:T(8,128)(2,1)S(1)} collective-permute-done((bf16[4,224,512]{2,1,0:T(8,128)(2,1)S(1)}, bf16[4,224,512]{2,1,0:T(8,128)(2,1)S(1)}, u32[]{:S(2)}, u32[]{:S(2)}) %collective-permute-start.13) | collective-permute-done | bytes 917536 | tf_op jit(solution)/shard_map/ppermute | solution.py:295
  95.7 0.0 collective-permute-done.12
  95.7 5.6 %collective-permute-done.14 = bf16[4,224,512]{2,1,0:T(8,128)(2,1)S(1)} collective-permute-done((bf16[4,224,512]{2,1,0:T(8,128)(2,1)S(1)}, bf16[4,224,512]{2,1,0:T(8,128)(2,1)S(1)}, u32[]{:S(2)}, u32[]{:S(2)}) %collective-permute-start.14) | collective-permute-done | bytes 917536 | tf_op jit(solution)/shard_map/ppermute | solution.py:295
  101.3 9.7 %collective-permute-done.16 = bf16[4,224,512]{2,1,0:T(8,128)(2,1)S(1)} collective-permute-done((bf16[4,224,512]{2,1,0:T(8,128)(2,1)S(1)}, bf16[4,224,512]{2,1,0:T(8,128)(2,1)S(1)}, u32[]{:S(2)}, u32[]{:S(2)}) %collective-permute-start.16) | collective-permute-done | bytes 917536 | tf_op jit(solution)/shard_map/ppermute | solution.py:295
  111.1 0.7 fusion.7
  111.8 0.1 collective-permute-start.17
  111.9 3.2 %collective-permute-start.19 = (bf16[224,512]{1,0:T(8,128)(2,1)S(1)}, bf16[224,512]{1,0:T(8,128)(2,1)S(1)}, u32[]{:S(2)}, u32[]{:S(2)}) collective-permute-start(bf16[224,512]{1,0:T(8,128)(2,1)S(1)} %get-tuple-element.102), channel_id=1, source_target_pairs={{0,24},{1,7},{2,26},{3,1},{4,28},{5,3},{6,30},{7,5},{8,0},{9,15},{... | collective-permute-start | bytes 688136 | tf_op jit(solution)/shard_map/ppermute | solution.py:292
  115.1 4.0 %collective-permute-done.17 = bf16[224,512]{1,0:T(8,128)(2,1)S(1)} collective-permute-done((bf16[224,512]{1,0:T(8,128)(2,1)S(1)}, bf16[224,512]{1,0:T(8,128)(2,1)S(1)}, u32[]{:S(2)}, u32[]{:S(2)}) %collective-permute-start.17) | collective-permute-done | bytes 229408 | tf_op jit(solution)/shard_map/ppermute | solution.py:292
  119.1 2.0 %collective-permute-done.19 = bf16[224,512]{1,0:T(8,128)(2,1)S(1)} collective-permute-done((bf16[224,512]{1,0:T(8,128)(2,1)S(1)}, bf16[224,512]{1,0:T(8,128)(2,1)S(1)}, u32[]{:S(2)}, u32[]{:S(2)}) %collective-permute-start.19) | collective-permute-done | bytes 229408 | tf_op jit(solution)/shard_map/ppermute | solution.py:292
  121.1 1.5 %collective-permute-done.18 = bf16[224,512]{1,0:T(8,128)(2,1)S(1)} collective-permute-done((bf16[224,512]{1,0:T(8,128)(2,1)S(1)}, bf16[224,512]{1,0:T(8,128)(2,1)S(1)}, u32[]{:S(2)}, u32[]{:S(2)}) %collective-permute-start.18) | collective-permute-done | bytes 229408 | tf_op jit(solution)/shard_map/ppermute | solution.py:292
  122.6 0.1 fusion.2
  122.8 0.1 copy.13
  122.9 16.8 %all_to_all.10 = bf16[8,48,224]{2,1,0:T(8,128)(2,1)S(1)} all-to-all(bf16[8,48,224]{2,1,0:T(8,128)(2,1)S(1)} %bitcast.49), channel_id=1, replica_groups=mesh['expert'=8,'tensor'=32] {'expert'}, dimensions={0} | all-to-all | bytes 344064 | tf_op jit(solution)/shard_map/all_to_all | solution.py:329
  139.7 1.0 fusion.5
  (17 shorter events, 0.1 us)
Async XLA Ops:
  1.9 24.1 %all-to-all-start = ((bf16[8,48,224]{2,1,0:T(8,128)(2,1)}), bf16[8,48,224]{2,1,0:T(8,128)(2,1)S(1)}, u32[]{:S(2)}, u32[]{:S(2)}) async-start(bf16[8,48,224]{2,1,0:T(8,128)(2,1)} %bitcast.56), calls=%async_computation | async-start | bytes 393216 | tf_op jit(solution)/shard_map/all_to_all | solution.py:281
  18.1 8.0 %copy-start.4 = (bf16[128,224]{0,1:T(8,128)(2,1)S(1)}, bf16[128,224]{0,1:T(8,128)(2,1)}, u32[]{:S(2)}) copy-start(bf16[128,224]{0,1:T(8,128)(2,1)} %param.10) | copy-start | bytes 172036
  26.2 13.8 %collective-permute-start.1 = (bf16[224,512]{1,0:T(8,128)(2,1)S(1)}, bf16[224,512]{1,0:T(8,128)(2,1)S(1)}, u32[]{:S(2)}, u32[]{:S(2)}) collective-permute-start(bf16[224,512]{1,0:T(8,128)(2,1)S(1)} %get-tuple-element.105), channel_id=1, source_target_pairs={{0,16},{1,5},{2,18},{3,7},{4,20},{5,1},{6,22},{7,3},{8,24},{9,13},... | collective-permute-start | bytes 688136 | tf_op jit(solution)/shard_map/ppermute | solution.py:292
  29.3 10.7 %collective-permute-start = (bf16[224,512]{1,0:T(8,128)(2,1)S(1)}, bf16[224,512]{1,0:T(8,128)(2,1)S(1)}, u32[]{:S(2)}, u32[]{:S(2)}) collective-permute-start(bf16[224,512]{1,0:T(8,128)(2,1)S(1)} %get-tuple-element.105), channel_id=1, source_target_pairs={{0,8},{1,3},{2,10},{3,5},{4,12},{5,7},{6,14},{7,1},{8,16},{9,11},{... | collective-permute-start | bytes 688136 | tf_op jit(solution)/shard_map/ppermute | solution.py:292
  29.9 10.1 %collective-permute-start.2 = (bf16[224,512]{1,0:T(8,128)(2,1)S(1)}, bf16[224,512]{1,0:T(8,128)(2,1)S(1)}, u32[]{:S(2)}, u32[]{:S(2)}) collective-permute-start(bf16[224,512]{1,0:T(8,128)(2,1)S(1)} %get-tuple-element.105), channel_id=1, source_target_pairs={{0,24},{1,7},{2,26},{3,1},{4,28},{5,3},{6,30},{7,5},{8,0},{9,15},{... | collective-permute-start | bytes 688136 | tf_op jit(solution)/shard_map/ppermute | solution.py:292
  40.1 18.6 %collective-permute-start.6 = (bf16[4,224,512]{2,1,0:T(8,128)(2,1)S(1)}, bf16[4,224,512]{2,1,0:T(8,128)(2,1)}, u32[]{:S(2)}, u32[]{:S(2)}) collective-permute-start(bf16[4,224,512]{2,1,0:T(8,128)(2,1)S(1)} %pad_maximum_fusion.refs_0_), channel_id=1, source_target_pairs={{0,1},{1,0},{2,3},{3,2},{4,5},{5,4},{6,7},{7,6},{8,9},{9,8},{10,11... | collective-permute-start | bytes 2752520 | tf_op jit(solution)/shard_map/ppermute | solution.py:39
  40.2 18.5 %collective-permute-start.5 = (bf16[4,224,512]{2,1,0:T(8,128)(2,1)S(1)}, bf16[4,224,512]{2,1,0:T(8,128)(2,1)}, u32[]{:S(2)}, u32[]{:S(2)}) collective-permute-start(bf16[4,224,512]{2,1,0:T(8,128)(2,1)S(1)} %pad_maximum_fusion.refs_0_), channel_id=1, source_target_pairs={{0,2},{1,9},{2,4},{3,11},{4,6},{5,13},{6,0},{7,15},{8,10},{9,17},{... | collective-permute-start | bytes 2752520 | tf_op jit(solution)/shard_map/ppermute | solution.py:295
  41.9 26.3 %collective-permute-start.4 = (bf16[4,224,512]{2,1,0:T(8,128)(2,1)S(1)}, bf16[4,224,512]{2,1,0:T(8,128)(2,1)S(1)}, u32[]{:S(2)}, u32[]{:S(2)}) collective-permute-start(bf16[4,224,512]{2,1,0:T(8,128)(2,1)S(1)} %pad_maximum_fusion.refs_0_), channel_id=1, source_target_pairs={{0,6},{1,25},{2,0},{3,27},{4,2},{5,29},{6,4},{7,31},{8,14},{9,1},{... | collective-permute-start | bytes 2752520 | tf_op jit(solution)/shard_map/ppermute | solution.py:295
  42.3 25.9 %collective-permute-start.3 = (bf16[4,224,512]{2,1,0:T(8,128)(2,1)S(1)}, bf16[4,224,512]{2,1,0:T(8,128)(2,1)S(1)}, u32[]{:S(2)}, u32[]{:S(2)}) collective-permute-start(bf16[4,224,512]{2,1,0:T(8,128)(2,1)S(1)} %pad_maximum_fusion.refs_0_), channel_id=1, source_target_pairs={{0,4},{1,17},{2,6},{3,19},{4,0},{5,21},{6,2},{7,23},{8,12},{9,25},... | collective-permute-start | bytes 2752520 | tf_op jit(solution)/shard_map/ppermute | solution.py:295
  52.1 2.4 %copy-start = (bf16[32,304,224]{2,1,0:T(8,128)(2,1)S(1)}, bf16[32,304,224]{2,1,0:T(8,128)(2,1)}, u32[]{:S(2)}) copy-start(bf16[32,304,224]{2,1,0:T(8,128)(2,1)} %up_weights.3.refs_2_.refs_4_.refs_5_.refs_6_.refs_7_.refs_8_) | copy-start | bytes 13074436
  54.5 2.4 %copy-start.1 = (bf16[32,304,224]{2,1,0:T(8,128)(2,1)S(1)}, bf16[32,304,224]{2,1,0:T(8,128)(2,1)}, u32[]{:S(2)}) copy-start(bf16[32,304,224]{2,1,0:T(8,128)(2,1)} %up_weights.2.refs_1_.refs_2_.refs_3_.refs_4_.refs_5_) | copy-start | bytes 13074436
  58.8 10.0 %collective-permute-start.9 = (bf16[4,224,512]{2,1,0:T(8,128)(2,1)}, bf16[4,224,512]{2,1,0:T(8,128)(2,1)S(1)}, u32[]{:S(2)}, u32[]{:S(2)}) collective-permute-start(bf16[4,224,512]{2,1,0:T(8,128)(2,1)} %collective-permute-done.5.refs_1_), channel_id=1, source_target_pairs={{0,1},{1,0},{2,3},{3,2},{4,5},{5,4},{6,7},{7,6},{8,9},{9,8},{10,11... | collective-permute-start | bytes 2752520 | tf_op jit(solution)/shard_map/ppermute | solution.py:39
  68.2 3.5 %collective-permute-start.7 = (bf16[4,224,512]{2,1,0:T(8,128)(2,1)S(1)}, bf16[4,224,512]{2,1,0:T(8,128)(2,1)S(1)}, u32[]{:S(2)}, u32[]{:S(2)}) collective-permute-start(bf16[4,224,512]{2,1,0:T(8,128)(2,1)S(1)} %collective-permute-done.3.refs_1_), channel_id=1, source_target_pairs={{0,1},{1,0},{2,3},{3,2},{4,5},{5,4},{6,7},{7,6},{8,9},{9,8},{10,11... | collective-permute-start | bytes 2752520 | tf_op jit(solution)/shard_map/ppermute | solution.py:39
  68.3 3.8 %collective-permute-start.8 = (bf16[4,224,512]{2,1,0:T(8,128)(2,1)S(1)}, bf16[4,224,512]{2,1,0:T(8,128)(2,1)S(1)}, u32[]{:S(2)}, u32[]{:S(2)}) collective-permute-start(bf16[4,224,512]{2,1,0:T(8,128)(2,1)S(1)} %collective-permute-done.4.refs_2_), channel_id=1, source_target_pairs={{0,1},{1,0},{2,3},{3,2},{4,5},{5,4},{6,7},{7,6},{8,9},{9,8},{10,11... | collective-permute-start | bytes 2752520 | tf_op jit(solution)/shard_map/ppermute | solution.py:39
  72.1 2.5 %copy-start.2 = (bf16[32,224,152]{2,1,0:T(8,128)(2,1)S(1)}, bf16[32,224,152]{2,1,0:T(8,128)(2,1)}, u32[]{:S(2)}) copy-start(bf16[32,224,152]{2,1,0:T(8,128)(2,1)} %down_weights.2.refs_1_.refs_3_) | copy-start | bytes 6537220
  72.1 3.2 %copy-start.3 = (bf16[32,224,152]{2,1,0:T(8,128)(2,1)S(1)}, bf16[32,224,152]{2,1,0:T(8,128)(2,1)}, u32[]{:S(2)}) copy-start(bf16[32,224,152]{2,1,0:T(8,128)(2,1)} %down_weights.3.refs_0_.refs_2_) | copy-start | bytes 6537220
  77.1 2.8 %collective-permute-start.11 = (bf16[4,224,512]{2,1,0:T(8,128)(2,1)S(1)}, bf16[4,224,512]{2,1,0:T(8,128)(2,1)S(1)}, u32[]{:S(2)}, u32[]{:S(2)}) collective-permute-start(bf16[4,224,512]{2,1,0:T(8,128)(2,1)S(1)} %get-tuple-element.89), channel_id=1, source_target_pairs={{0,1},{1,0},{2,3},{3,2},{4,5},{5,4},{6,7},{7,6},{8,9},{9,8},{10,11... | collective-permute-start | bytes 2752520 | tf_op jit(solution)/shard_map/ppermute | solution.py:39
  79.2 4.6 %collective-permute-start.10 = (bf16[4,224,512]{2,1,0:T(8,128)(2,1)S(1)}, bf16[4,224,512]{2,1,0:T(8,128)(2,1)S(1)}, u32[]{:S(2)}, u32[]{:S(2)}) collective-permute-start(bf16[4,224,512]{2,1,0:T(8,128)(2,1)S(1)} %get-tuple-element.87), channel_id=1, source_target_pairs={{0,1},{1,0},{2,3},{3,2},{4,5},{5,4},{6,7},{7,6},{8,9},{9,8},{10,11... | collective-permute-start | bytes 2752520 | tf_op jit(solution)/shard_map/ppermute | solution.py:39
  82.1 5.4 %collective-permute-start.15 = (bf16[4,224,512]{2,1,0:T(8,128)(2,1)S(1)}, bf16[4,224,512]{2,1,0:T(8,128)(2,1)S(1)}, u32[]{:S(2)}, u32[]{:S(2)}) collective-permute-start(bf16[4,224,512]{2,1,0:T(8,128)(2,1)S(1)} %get-tuple-element.97), channel_id=1, source_target_pairs={{0,1},{1,0},{2,3},{3,2},{4,5},{5,4},{6,7},{7,6},{8,9},{9,8},{10,11... | collective-permute-start | bytes 2752520 | tf_op jit(solution)/shard_map/ppermute | solution.py:39
  82.3 13.4 %collective-permute-start.13 = (bf16[4,224,512]{2,1,0:T(8,128)(2,1)S(1)}, bf16[4,224,512]{2,1,0:T(8,128)(2,1)S(1)}, u32[]{:S(2)}, u32[]{:S(2)}) collective-permute-start(bf16[4,224,512]{2,1,0:T(8,128)(2,1)S(1)} %convert_add_fusion.1), channel_id=1, source_target_pairs={{0,2},{1,9},{2,4},{3,11},{4,6},{5,13},{6,0},{7,15},{8,10},{9,17},{... | collective-permute-start | bytes 2752520 | tf_op jit(solution)/shard_map/ppermute | solution.py:295
  86.1 9.6 %collective-permute-start.12 = (bf16[4,224,512]{2,1,0:T(8,128)(2,1)S(1)}, bf16[4,224,512]{2,1,0:T(8,128)(2,1)S(1)}, u32[]{:S(2)}, u32[]{:S(2)}) collective-permute-start(bf16[4,224,512]{2,1,0:T(8,128)(2,1)S(1)} %get-tuple-element.93), channel_id=1, source_target_pairs={{0,1},{1,0},{2,3},{3,2},{4,5},{5,4},{6,7},{7,6},{8,9},{9,8},{10,11... | collective-permute-start | bytes 2752520 | tf_op jit(solution)/shard_map/ppermute | solution.py:39
  86.2 15.1 %collective-permute-start.14 = (bf16[4,224,512]{2,1,0:T(8,128)(2,1)S(1)}, bf16[4,224,512]{2,1,0:T(8,128)(2,1)S(1)}, u32[]{:S(2)}, u32[]{:S(2)}) collective-permute-start(bf16[4,224,512]{2,1,0:T(8,128)(2,1)S(1)} %convert_add_fusion.2), channel_id=1, source_target_pairs={{0,4},{1,17},{2,6},{3,19},{4,0},{5,21},{6,2},{7,23},{8,12},{9,25},... | collective-permute-start | bytes 2752520 | tf_op jit(solution)/shard_map/ppermute | solution.py:295
  87.9 23.2 %collective-permute-start.16 = (bf16[4,224,512]{2,1,0:T(8,128)(2,1)S(1)}, bf16[4,224,512]{2,1,0:T(8,128)(2,1)S(1)}, u32[]{:S(2)}, u32[]{:S(2)}) collective-permute-start(bf16[4,224,512]{2,1,0:T(8,128)(2,1)S(1)} %add_convert_fusion), channel_id=1, source_target_pairs={{0,6},{1,25},{2,0},{3,27},{4,2},{5,29},{6,4},{7,31},{8,14},{9,1},{... | collective-permute-start | bytes 2752520 | tf_op jit(solution)/shard_map/ppermute | solution.py:295
  111.7 28.0 %copy-start.5 = (f32[384,128]{1,0:T(8,128)S(1)}, f32[384,128]{1,0:T(8,128)}, u32[]{:S(2)}) copy-start(f32[384,128]{1,0:T(8,128)} %get-tuple-element.98) | copy-start | bytes 589828
  111.8 7.3 %collective-permute-start.17 = (bf16[224,512]{1,0:T(8,128)(2,1)S(1)}, bf16[224,512]{1,0:T(8,128)(2,1)S(1)}, u32[]{:S(2)}, u32[]{:S(2)}) collective-permute-start(bf16[224,512]{1,0:T(8,128)(2,1)S(1)} %get-tuple-element.101), channel_id=1, source_target_pairs={{0,8},{1,3},{2,10},{3,5},{4,12},{5,7},{6,14},{7,1},{8,16},{9,11},{... | collective-permute-start | bytes 688136 | tf_op jit(solution)/shard_map/ppermute | solution.py:292
  111.9 9.2 %collective-permute-start.19 = (bf16[224,512]{1,0:T(8,128)(2,1)S(1)}, bf16[224,512]{1,0:T(8,128)(2,1)S(1)}, u32[]{:S(2)}, u32[]{:S(2)}) collective-permute-start(bf16[224,512]{1,0:T(8,128)(2,1)S(1)} %get-tuple-element.102), channel_id=1, source_target_pairs={{0,24},{1,7},{2,26},{3,1},{4,28},{5,3},{6,30},{7,5},{8,0},{9,15},{... | collective-permute-start | bytes 688136 | tf_op jit(solution)/shard_map/ppermute | solution.py:292
  115.1 7.5 %collective-permute-start.18 = (bf16[224,512]{1,0:T(8,128)(2,1)S(1)}, bf16[224,512]{1,0:T(8,128)(2,1)S(1)}, u32[]{:S(2)}, u32[]{:S(2)}) collective-permute-start(bf16[224,512]{1,0:T(8,128)(2,1)S(1)} %get-tuple-element.103), channel_id=1, source_target_pairs={{0,16},{1,5},{2,18},{3,7},{4,20},{5,1},{6,22},{7,3},{8,24},{9,13},... | collective-permute-start | bytes 688136 | tf_op jit(solution)/shard_map/ppermute | solution.py:292
where the time goes:
time: 142 us; the launch traced here: 141 us
  Pallas kernels  51.1 us (36%)
  starting transfers between devices  35 us (25%)
  waiting for transfers between devices  28.6 us (20%)
  blocking collectives  16.8 us (12%)
  local copies, waits for them, and re-layouts  5.88 us (4%)
  other arithmetic  2.08 us (1%)
    ppermute x6, waiting for transfers between devices, level_two(): return lax.ppermute(value, 'tensor', hops(d, False))  20.7 us
    all_to_all x1, blocking collectives, shards(): lax.all_to_all(back, 'expert', 0, 0, tiled=True)  16.8 us
    pallas_call x2, Pallas kernels, up_weights(): pl.pallas_call(functools.partial(up_weights_kernel, cols), out_shape=jax....  15.6 us
    pallas_call x2, Pallas kernels, down_weights(): pl.pallas_call(functools.partial(down_weights_kernel, cols), out_shape=ja...  14.9 us
    pallas_call x4, Pallas kernels, arrive(): pl.pallas_call(functools.partial(arrive_kernel, dense_rows, count, start,...  11.2 us
    ppermute x6, starting transfers between devices, level_one(): return lax.ppermute(value, 'tensor', hops(d, True))  9.66 us
    ppermute x6, starting transfers between devices, level_two(): return lax.ppermute(value, 'tensor', hops(d, False))  9.64 us
    all_to_all x1, starting transfers between devices, shards(): lax.all_to_all(outgoing.reshape(experts, capacity, cols), 'expert', 0, 0,...  8.47 us
  transfers between devices with their start and end apart: 21, of which 7 were waited for; matrix products, arithmetic and copies ran while one was open for 1% of the time, Pallas kernels for 32%

commit v1 on v0

--- a/solution.py
+++ b/solution.py
@@ -87,45 +87,87 @@
     )(ids, probs, tokens)
 
 
-def up_weights_kernel(cols, gain, gate, up, out):
-    for i in range(gate.shape[1] // cols):
-        at = slice(i * cols, (i + 1) * cols)
-        both = jnp.concatenate([gate[:, at].astype(F32), up[:, at].astype(F32)], axis=0)
-        out[i] = (both * gain[:, at]).astype(BF16)
-
-
-def up_weights(gain, gate, up, cols):
-    units, width = gate.shape
-    wide = pl.BlockSpec((units, CHUNK), lambda i: (0, i))
+IN_HBM = pl.BlockSpec(memory_space=pl.ANY)
+IN_VMEM = pl.BlockSpec(memory_space=pltpu.MemorySpace.VMEM)
+
+
+def laid_out(form, cols, sources, out, held, pieces, arrived, gone):
+    each = CHUNK // cols
+    steps = pieces.shape[0] // each
+    reads = [
+        [
+            pltpu.make_async_copy(
+                source.at[:, step * CHUNK : (step + 1) * CHUNK],
+                held.at[i, :, step * CHUNK : (step + 1) * CHUNK],
+                arrived.at[i, step],
+            )
+            for i, source in enumerate(sources)
+        ]
+        for step in range(steps)
+    ]
+    writes = [
+        pltpu.make_async_copy(
+            pieces.at[step * each : (step + 1) * each],
+            out.at[step * each : (step + 1) * each],
+            gone.at[step],
+        )
+        for step in range(steps)
+    ]
+    for row in reads:
+        for copy in row:
+            copy.start()
+    for step in range(steps):
+        for copy in reads[step]:
+            copy.wait()
+        for i in range(step * each, (step + 1) * each):
+            pieces[i] = form(held, slice(i * cols, (i + 1) * cols))
+        writes[step].start()
+    for copy in writes:
+        copy.wait()
+
+
+def up_weights_kernel(cols, gain, gate, up, out, held, pieces, arrived, gone):
+    def form(held, at):
+        both = jnp.concatenate([held[0, :, at].astype(F32), held[1, :, at].astype(F32)], axis=0)
+        return (both * gain[:, at]).astype(BF16)
+
+    laid_out(form, cols, [gate, up], out, held, pieces, arrived, gone)
+
+
+def down_weights_kernel(cols, down, out, held, pieces, arrived, gone):
+    def form(held, at):
+        return held[0, :, at].astype(F32).T.astype(BF16)
+
+    laid_out(form, cols, [down], out, held, pieces, arrived, gone)
+
+
+def layout_call(kernel, name, cols, piece, sources, gain=()):
+    units, width = sources[0].shape
+    shape = (width // cols,) + piece
     return pl.pallas_call(
-        functools.partial(up_weights_kernel, cols),
-        out_shape=jax.ShapeDtypeStruct((width // cols, 2 * units, cols), BF16),
-        grid=(width // CHUNK,),
-        in_specs=[pl.BlockSpec((1, CHUNK), lambda i: (0, i)), wide, wide],
-        out_specs=pl.BlockSpec((CHUNK // cols, 2 * units, cols), lambda i: (i, 0, 0)),
+        functools.partial(kernel, cols),
+        out_shape=jax.ShapeDtypeStruct(shape, BF16),
+        in_specs=[IN_VMEM] * len(gain) + [IN_HBM] * len(sources),
+        out_specs=IN_HBM,
+        scratch_shapes=[
+            pltpu.VMEM((len(sources), units, width), BF16),
+            pltpu.VMEM(shape, BF16),
+            pltpu.SemaphoreType.DMA((len(sources), width // CHUNK)),
+            pltpu.SemaphoreType.DMA((width // CHUNK,)),
+        ],
         compiler_params=pltpu.CompilerParams(vmem_limit_bytes=MOST),
         cost_estimate=SMALL,
-        name="up_weights",
-    )(gain, gate, up)
-
-
-def down_weights_kernel(cols, down, out):
-    for i in range(down.shape[1] // cols):
-        out[i] = down[:, i * cols : (i + 1) * cols].astype(F32).T.astype(BF16)
+        name=name,
+    )(*gain, *sources)
+
+
+def up_weights(gain, gate, up, cols):
+    piece = (2 * gate.shape[0], cols)
+    return layout_call(up_weights_kernel, "up_weights", cols, piece, [gate, up], [gain])
 
 
 def down_weights(down, cols):
-    units, width = down.shape
-    return pl.pallas_call(
-        functools.partial(down_weights_kernel, cols),
-        out_shape=jax.ShapeDtypeStruct((width // cols, cols, units), BF16),
-        grid=(width // CHUNK,),
-        in_specs=[pl.BlockSpec((units, CHUNK), lambda i: (0, i))],
-        out_specs=pl.BlockSpec((CHUNK // cols, cols, units), lambda i: (i, 0, 0)),
-        compiler_params=pltpu.CompilerParams(vmem_limit_bytes=MOST),
-        cost_estimate=SMALL,
-        name="down_weights",
-    )(down)
+    return layout_call(down_weights_kernel, "down_weights", cols, (cols, down.shape[0]), [down])
 
 
 def arrive_kernel(dense_rows, count, start, last, width, place, *refs):
@@ -215,45 +257,35 @@
     )
 
 
-def down_kernel(dense_rows, place, hidden, *refs):
-    mine, others = refs[4:]
-    for out, dense, routed in ((mine, refs[0], refs[1]), (others, refs[2], refs[3])):
-        for weight, span in (
-            (dense, slice(0, dense_rows)),
-            (routed, slice(dense_rows, hidden.shape[1])),
-        ):
-            out[0, :, span] = jnp.dot(
-                weight[0], hidden[:, span], preferred_element_type=F32
-            ).astype(out.dtype)
-
-
-def down_pieces(place, hidden, weights, outer, dense_rows):
+def down_kernel(dense_rows, place, hidden, dense, routed, out):
+    for weight, span in (
+        (dense, slice(0, dense_rows)),
+        (routed, slice(dense_rows, hidden.shape[1])),
+    ):
+        out[0, :, span] = jnp.dot(
+            weight[0], hidden[:, span], preferred_element_type=F32
+        ).astype(out.dtype)
+
+
+def down_pieces(place, hidden, weights, outer, other, dense_rows):
     units, rows = hidden.shape
     cols = weights[0].shape[1]
-
-    def weight(other):
-        def index(i, place):
-            return piece_index(place, other, 1, outer, i), 0, 0
-
-        return pl.BlockSpec((1, cols, units), index)
-
-    out = pl.BlockSpec((1, cols, rows), lambda i, place: (i, 0, 0))
-    shape = (SIDE, cols, rows)
+    weight = pl.BlockSpec(
+        (1, cols, units), lambda i, place: (piece_index(place, other, 1, outer, i), 0, 0)
+    )
     return pl.pallas_call(
         functools.partial(down_kernel, dense_rows),
-        out_shape=(jax.ShapeDtypeStruct(shape, F32), jax.ShapeDtypeStruct(shape, BF16)),
+        out_shape=jax.ShapeDtypeStruct((SIDE, cols, rows), BF16 if other else F32),
         grid_spec=pltpu.PrefetchScalarGridSpec(
             num_scalar_prefetch=1,
             grid=(SIDE,),
-            in_specs=[pl.BlockSpec((units, rows), lambda i, place: (0, 0))]
-            + [weight(False)] * 2
-            + [weight(True)] * 2,
-            out_specs=(out, out),
+            in_specs=[pl.BlockSpec((units, rows), lambda i, place: (0, 0)), weight, weight],
+            out_specs=pl.BlockSpec((1, cols, rows), lambda i, place: (i, 0, 0)),
         ),
         compiler_params=pltpu.CompilerParams(vmem_limit_bytes=16 * MIB),
         cost_estimate=SMALL,
-        name=f"down_pieces_{outer}",
-    )(place, hidden, weights[0], weights[1], weights[0], weights[1])
+        name=f"down_{'other' if other else 'mine'}_{outer}",
+    )(place, hidden, weights[0], weights[1])
 
 
 def shards(
@@ -312,17 +344,25 @@
     far_other, left_other, sums = lax.optimization_barrier((far_other, left_other, sums))
     hidden = add([(far_other, 2, 0, True), (left_other, 3, 0, True)], sums=sums, last=True)
 
-    pieces = {}
-    for outer in (1, 2, 3, 0):
-        mine, others = down_pieces(place, hidden, down, outer, rows)
-        if outer > 1:
-            pieces[outer - 1], hidden = lax.optimization_barrier((pieces[outer - 1], hidden))
-        pieces[outer] = mine + sibling(others).astype(F32)
-    level = pieces[0]
-    for d in range(1, SIDE):
-        level = level + level_two(pieces[d].astype(BF16), d).astype(F32)
+    def shares(outer, other, hidden):
+        out = down_pieces(place, hidden, down, outer, other, rows)
+        return lax.optimization_barrier((out, hidden))
+
+    pieces, order = {}, (2, 1, 3)
+    for d in order:
+        pieces[d], hidden = shares(d, True, hidden)
+    pieces = {d: sibling(pieces[d]) for d in order}
+    for d in order:
+        mine, hidden = shares(d, False, hidden)
+        pieces[d] = (mine + pieces[d].astype(F32)).astype(BF16)
+    pieces, hidden = lax.optimization_barrier((pieces, hidden))
+    others, hidden = shares(0, True, hidden)
+    mine, hidden = shares(0, False, hidden)
+    level = mine + sibling(others).astype(F32)
+    for d in order:
+        level = level + level_two(pieces[d], d).astype(F32)
     total = level[0]
-    for d in range(1, SIDE):
+    for d in order:
         total = total + level_one(level[d].astype(BF16), d).astype(F32)
 
     back = total[:, rows:].astype(BF16).T.reshape(experts, capacity, cols)

time: 142 us -> 135 us (0.951)
  Pallas kernels: 51.1 us -> 45.8 us
  starting transfers between devices: 35 us -> 29.9 us
  waiting for transfers between devices: 28.6 us -> 32.7 us
    pallas_call x8 -> x12, Pallas kernels: 38 us -> 32.8 us  [the longest x4 20.6 us: layout_call(): pl.pallas_call(functools.partial(kernel, cols), out_shape=jax.ShapeDtypeS...]
    ppermute x8, starting transfers between devices: 7.23 us -> 2.08 us  [sibling(): return lax.ppermute(value, 'tensor', [(i, i ^ 1) for i in range(GROUP)])]
    ppermute x6, waiting for transfers between devices: 20.7 us -> 24.8 us  [level_two(): return lax.ppermute(value, 'tensor', hops(d, False))]
  transfers between devices with their start and end apart: 21 -> 21, of which waited for: 7 -> 8; matrix products, arithmetic and copies ran while one was open for 1% -> 1% of each run, Pallas kernels for 32% -> 29%
where the time goes in v1:
time: 135 us; the launch traced here: 134 us
  Pallas kernels  45.8 us (34%)
  waiting for transfers between devices  32.7 us (24%)
  starting transfers between devices  29.9 us (22%)
  blocking collectives  16.4 us (12%)
  local copies, waits for them, and re-layouts  5.89 us (4%)
  other arithmetic  1.98 us (1%)
    ppermute x6, waiting for transfers between devices, level_two(): return lax.ppermute(value, 'tensor', hops(d, False))  24.8 us
    pallas_call x4, Pallas kernels, layout_call(): pl.pallas_call(functools.partial(kernel, cols), out_shape=jax.ShapeDtypeS...  20.6 us
    all_to_all x1, blocking collectives, shards(): lax.all_to_all(back, 'expert', 0, 0, tiled=True)  16.4 us
    pallas_call x8, Pallas kernels, down_pieces(): pl.pallas_call(functools.partial(down_kernel, dense_rows), out_shape=jax....  12.1 us
    pallas_call x4, Pallas kernels, arrive(): pl.pallas_call(functools.partial(arrive_kernel, dense_rows, count, start,...  11.2 us
    ppermute x6, starting transfers between devices, level_two(): return lax.ppermute(value, 'tensor', hops(d, False))  10.1 us
    ppermute x6, starting transfers between devices, level_one(): return lax.ppermute(value, 'tensor', hops(d, True))  9.22 us
    all_to_all x1, starting transfers between devices, shards(): lax.all_to_all(outgoing.reshape(experts, capacity, cols), 'expert', 0, 0,...  8.47 us
  transfers between devices with their start and end apart: 21, of which 8 were waited for; matrix products, arithmetic and copies ran while one was open for 1% of the time, Pallas kernels for 29%

profile of v1, /device:TPU:8, one launch (start us, length us, event | category | flops | bytes accessed | tf_op | source)
XLA Modules:
  0.0 134.0 jit_solution(15250515975450316518)
XLA Ops:
  0.0 1.9 %dispatch.1 = (bf16[384,224]{1,0:T(8,128)(2,1)}, f32[384,128]{1,0:T(8,128)}) custom-call(s32[2,128]{1,0:T(2,128)} %bitcast.59, f32[2,128]{1,0:T(2,128)} %bitcast.60, bf16[224,128]{1,0:T(8,128)(2,1)} %bitcast.54), custom_call_target="tpu_custom_call" | custom-call | tf_op jit(solution)/shard_map/dispatch/pallas_call | solution.py:80
  1.9 8.5 %all-to-all-start = ((bf16[8,48,224]{2,1,0:T(8,128)(2,1)}), bf16[8,48,224]{2,1,0:T(8,128)(2,1)S(1)}, u32[]{:S(2)}, u32[]{:S(2)}) async-start(bf16[8,48,224]{2,1,0:T(8,128)(2,1)} %bitcast.56), calls=%async_computation | async-start | bytes 393216 | tf_op jit(solution)/shard_map/all_to_all | solution.py:313
  10.3 5.0 %up_weights.3.refs_2_.refs_4_.refs_5_.refs_6_.refs_7_.refs_8_ = bf16[32,304,224]{2,1,0:T(8,128)(2,1)} custom-call(f32[1,7168]{1,0:T(1,128)} %bitcast.57, bf16[152,7168]{1,0:T(8,128)(2,1)} %bitcast.44, bf16[152,7168]{1,0:T(8,128)(2,1)} %bitcast.45), custom_call_target="tpu_custom_call" | custom-call | flops 1048576 | bytes 1048576 | tf_op jit(solution)/shard_map/up_weights/pallas_call | solution.py:147
  15.4 0.0 copy-start.4
  15.4 5.1 %up_weights.2.refs_1_.refs_2_.refs_3_.refs_4_.refs_5_ = bf16[32,304,224]{2,1,0:T(8,128)(2,1)} custom-call(f32[1,7168]{1,0:T(1,128)} %bitcast.58, bf16[152,7168]{1,0:T(8,128)(2,1)} %gate.1, bf16[152,7168]{1,0:T(8,128)(2,1)} %up.1), custom_call_target="tpu_custom_call" | custom-call | flops 1048576 | bytes 1048576 | tf_op jit(solution)/shard_map/up_weights/pallas_call | solution.py:147
  20.5 0.4 all-to-all-done
  20.8 0.1 copy.12
  21.0 3.1 %collective-permute-start.1 = (bf16[224,512]{1,0:T(8,128)(2,1)S(1)}, bf16[224,512]{1,0:T(8,128)(2,1)S(1)}, u32[]{:S(2)}, u32[]{:S(2)}) collective-permute-start(bf16[224,512]{1,0:T(8,128)(2,1)S(1)} %get-tuple-element.119), channel_id=1, source_target_pairs={{0,16},{1,5},{2,18},{3,7},{4,20},{5,1},{6,22},{7,3},{8,24},{9,13},... | collective-permute-start | bytes 688136 | tf_op jit(solution)/shard_map/ppermute | solution.py:324
  24.1 0.6 collective-permute-start
  24.7 2.6 %collective-permute-start.2 = (bf16[224,512]{1,0:T(8,128)(2,1)S(1)}, bf16[224,512]{1,0:T(8,128)(2,1)S(1)}, u32[]{:S(2)}, u32[]{:S(2)}) collective-permute-start(bf16[224,512]{1,0:T(8,128)(2,1)S(1)} %get-tuple-element.119), channel_id=1, source_target_pairs={{0,24},{1,7},{2,26},{3,1},{4,28},{5,3},{6,30},{7,5},{8,0},{9,15},{... | collective-permute-start | bytes 688136 | tf_op jit(solution)/shard_map/ppermute | solution.py:324
  27.4 5.3 %down_weights.2.routed = bf16[32,224,152]{2,1,0:T(8,128)(2,1)} custom-call(bf16[152,7168]{1,0:T(8,128)(2,1)} %bitcast.46), custom_call_target="tpu_custom_call" | custom-call | flops 1048576 | bytes 1048576 | tf_op jit(solution)/shard_map/down_weights/pallas_call | solution.py:147
  32.6 0.0 collective-permute-done.1
  32.7 0.0 collective-permute-done
  32.7 0.1 pad_maximum_fusion.refs_0_
  32.8 0.1 collective-permute-start.6
  32.9 1.7 %collective-permute-start.5 = (bf16[4,224,512]{2,1,0:T(8,128)(2,1)S(1)}, bf16[4,224,512]{2,1,0:T(8,128)(2,1)}, u32[]{:S(2)}, u32[]{:S(2)}) collective-permute-start(bf16[4,224,512]{2,1,0:T(8,128)(2,1)S(1)} %pad_maximum_fusion.refs_0_), channel_id=1, source_target_pairs={{0,2},{1,9},{2,4},{3,11},{4,6},{5,13},{6,0},{7,15},{8,10},{9,17},{... | collective-permute-start | bytes 2752520 | tf_op jit(solution)/shard_map/ppermute | solution.py:327
  34.6 0.5 collective-permute-start.4
  35.0 2.3 %collective-permute-start.3 = (bf16[4,224,512]{2,1,0:T(8,128)(2,1)S(1)}, bf16[4,224,512]{2,1,0:T(8,128)(2,1)S(1)}, u32[]{:S(2)}, u32[]{:S(2)}) collective-permute-start(bf16[4,224,512]{2,1,0:T(8,128)(2,1)S(1)} %pad_maximum_fusion.refs_0_), channel_id=1, source_target_pairs={{0,4},{1,17},{2,6},{3,19},{4,0},{5,21},{6,2},{7,23},{8,12},{9,25},... | collective-permute-start | bytes 2752520 | tf_op jit(solution)/shard_map/ppermute | solution.py:327
  37.3 5.3 %down_weights.3.dense = bf16[32,224,152]{2,1,0:T(8,128)(2,1)} custom-call(bf16[152,7168]{1,0:T(8,128)(2,1)} %down.1), custom_call_target="tpu_custom_call" | custom-call | flops 1048576 | bytes 1048576 | tf_op jit(solution)/shard_map/down_weights/pallas_call | solution.py:147
  42.6 0.1 pad_add_fusion.place
  42.7 2.4 %copy-done = bf16[32,304,224]{2,1,0:T(8,128)(2,1)S(1)} copy-done((bf16[32,304,224]{2,1,0:T(8,128)(2,1)S(1)}, bf16[32,304,224]{2,1,0:T(8,128)(2,1)}, u32[]{:S(2)}) %copy-start) | copy-done | bytes 4358168
  45.1 2.4 %copy-done.1 = bf16[32,304,224]{2,1,0:T(8,128)(2,1)S(1)} copy-done((bf16[32,304,224]{2,1,0:T(8,128)(2,1)S(1)}, bf16[32,304,224]{2,1,0:T(8,128)(2,1)}, u32[]{:S(2)}) %copy-start.1) | copy-done | bytes 4358168
  47.5 1.8 %arrive_0_1.1 = (f32[304,128]{1,0:T(8,128)S(1)}, f32[304,384]{1,0:T(8,128)S(1)}, f32[8,512]{1,0:T(8,128)S(1)}) custom-call(s32[3]{0:T(128)S(1)} %pad_add_fusion.place, bf16[4,224,512]{2,1,0:T(8,128)(2,1)S(1)} %pad_maximum_fusion.refs_0_, bf16[32,304,224]{2,1,0:T(8,128)(2,1)S(1)} %copy-done.1, bf16[32,304,224]{2,1,0:T(8,128)(2,1)S(1)} %copy-done), custom_call_target="tpu_custom_call" | custom-call | flops 1048576 | bytes 1048576 | tf_op jit(solution)/shard_map/arrive_0_1/pallas_call | solution.py:236
  49.3 0.0 collective-permute-done.5.refs_1_
  49.3 0.1 collective-permute-start.9
  49.4 4.1 %arrive_1_2.1 = (f32[304,128]{1,0:T(8,128)S(1)}, f32[304,384]{1,0:T(8,128)S(1)}, f32[8,512]{1,0:T(8,128)S(1)}) custom-call(s32[3]{0:T(128)S(1)} %pad_add_fusion.place, bf16[4,224,512]{2,1,0:T(8,128)(2,1)} %collective-permute-done.6.refs_0_, bf16[4,224,512]{2,1,0:T(8,128)(2,1)} %collective-permute-done.5.refs_1_, bf16[32,304,224]{2,1,0:T(8,128)(2,1)S(1)} %copy-done.1, ...), custom_call_target="tpu_custom_call" | custom-call | flops 1048576 | bytes 1048576 | tf_op jit(solution)/shard_map/arrive_1_2/pallas_call | solution.py:236
  53.5 5.0 %collective-permute-done.3.refs_1_ = bf16[4,224,512]{2,1,0:T(8,128)(2,1)S(1)} collective-permute-done((bf16[4,224,512]{2,1,0:T(8,128)(2,1)S(1)}, bf16[4,224,512]{2,1,0:T(8,128)(2,1)S(1)}, u32[]{:S(2)}, u32[]{:S(2)}) %collective-permute-start.3) | collective-permute-done | bytes 917536 | tf_op jit(solution)/shard_map/ppermute | solution.py:327
  58.5 0.0 collective-permute-start.7
  58.5 0.5 collective-permute-start.8
  59.0 2.9 %arrive_3_3.1 = (f32[304,128]{1,0:T(8,128)S(1)}, f32[304,384]{1,0:T(8,128)S(1)}, f32[8,512]{1,0:T(8,128)S(1)}) custom-call(s32[3]{0:T(128)S(1)} %pad_add_fusion.place, bf16[4,224,512]{2,1,0:T(8,128)(2,1)S(1)} %collective-permute-done.9.refs_0_, bf16[4,224,512]{2,1,0:T(8,128)(2,1)S(1)} %collective-permute-done.3.refs_1_, ...), custom_call_target="tpu_custom_call" | custom-call | flops 1048576 | bytes 1048576 | tf_op jit(solution)/shard_map/arrive_3_3/pallas_call | solution.py:236
  61.9 0.4 collective-permute-done.8.refs_1_
  62.3 2.4 %arrive_3_2.1.hidden = bf16[152,512]{1,0:T(8,128)(2,1)S(1)} custom-call(s32[3]{0:T(128)S(1)} %pad_add_fusion.place, bf16[4,224,512]{2,1,0:T(8,128)(2,1)S(1)} %collective-permute-done.7.refs_0_, bf16[4,224,512]{2,1,0:T(8,128)(2,1)S(1)} %collective-permute-done.8.refs_1_, bf16[32,304,224]{2,1,0:T(8,128)(2,1)S(1)} %copy-done.1, ...), custom_call_target="tpu_custom_call" | custom-call | flops 1048576 | bytes 1048576 | tf_op jit(solution)/shard_map/arrive_3_2/pallas_call | solution.py:236
  64.8 0.7 copy-done.3
  65.4 1.5 %down_other_2.1 = bf16[4,224,512]{2,1,0:T(8,128)(2,1)S(1)} custom-call(s32[3]{0:T(128)S(1)} %pad_add_fusion.place, bf16[152,512]{1,0:T(8,128)(2,1)S(1)} %arrive_3_2.1.hidden, bf16[32,224,152]{2,1,0:T(8,128)(2,1)S(1)} %copy-done.3, bf16[32,224,152]{2,1,0:T(8,128)(2,1)S(1)} %copy-done.2), custom_call_target="tpu_custom_call" | custom-call | flops 1048576 | bytes 1048576 | tf_op jit(solution)/shard_map/down_other_2/pallas_call | solution.py:276
  67.0 0.2 collective-permute-start.11
  67.2 1.5 %down_other_1.1 = bf16[4,224,512]{2,1,0:T(8,128)(2,1)S(1)} custom-call(s32[3]{0:T(128)S(1)} %pad_add_fusion.place, bf16[152,512]{1,0:T(8,128)(2,1)S(1)} %arrive_3_2.1.hidden, bf16[32,224,152]{2,1,0:T(8,128)(2,1)S(1)} %copy-done.3, bf16[32,224,152]{2,1,0:T(8,128)(2,1)S(1)} %copy-done.2), custom_call_target="tpu_custom_call" | custom-call | flops 1048576 | bytes 1048576 | tf_op jit(solution)/shard_map/down_other_1/pallas_call | solution.py:276
  68.7 0.5 collective-permute-start.10
  69.2 1.5 %down_other_3.1 = bf16[4,224,512]{2,1,0:T(8,128)(2,1)S(1)} custom-call(s32[3]{0:T(128)S(1)} %pad_add_fusion.place, bf16[152,512]{1,0:T(8,128)(2,1)S(1)} %arrive_3_2.1.hidden, bf16[32,224,152]{2,1,0:T(8,128)(2,1)S(1)} %copy-done.3, bf16[32,224,152]{2,1,0:T(8,128)(2,1)S(1)} %copy-done.2), custom_call_target="tpu_custom_call" | custom-call | flops 1048576 | bytes 1048576 | tf_op jit(solution)/shard_map/down_other_3/pallas_call | solution.py:276
  70.7 0.2 collective-permute-start.12
  71.0 1.5 %down_mine_2.1 = f32[4,224,512]{2,1,0:T(8,128)S(1)} custom-call(s32[3]{0:T(128)S(1)} %pad_add_fusion.place, bf16[152,512]{1,0:T(8,128)(2,1)S(1)} %arrive_3_2.1.hidden, bf16[32,224,152]{2,1,0:T(8,128)(2,1)S(1)} %copy-done.3, bf16[32,224,152]{2,1,0:T(8,128)(2,1)S(1)} %copy-done.2), custom_call_target="tpu_custom_call" | custom-call | flops 1048576 | bytes 1048576 | tf_op jit(solution)/shard_map/down_mine_2/pallas_call | solution.py:276
  72.5 1.5 %down_mine_1.1 = f32[4,224,512]{2,1,0:T(8,128)S(1)} custom-call(s32[3]{0:T(128)S(1)} %pad_add_fusion.place, bf16[152,512]{1,0:T(8,128)(2,1)S(1)} %arrive_3_2.1.hidden, bf16[32,224,152]{2,1,0:T(8,128)(2,1)S(1)} %copy-done.3, bf16[32,224,152]{2,1,0:T(8,128)(2,1)S(1)} %copy-done.2), custom_call_target="tpu_custom_call" | custom-call | flops 1048576 | bytes 1048576 | tf_op jit(solution)/shard_map/down_mine_1/pallas_call | solution.py:276
  74.0 1.5 %down_mine_3.1 = f32[4,224,512]{2,1,0:T(8,128)S(1)} custom-call(s32[3]{0:T(128)S(1)} %pad_add_fusion.place, bf16[152,512]{1,0:T(8,128)(2,1)S(1)} %arrive_3_2.1.hidden, bf16[32,224,152]{2,1,0:T(8,128)(2,1)S(1)} %copy-done.3, bf16[32,224,152]{2,1,0:T(8,128)(2,1)S(1)} %copy-done.2), custom_call_target="tpu_custom_call" | custom-call | flops 1048576 | bytes 1048576 | tf_op jit(solution)/shard_map/down_mine_3/pallas_call | solution.py:276
  75.5 0.3 add_convert_fusion.1
  75.8 0.3 add_convert_fusion.2
  76.2 0.3 add_convert_fusion
  76.5 1.5 %down_other_0.1 = bf16[4,224,512]{2,1,0:T(8,128)(2,1)S(1)} custom-call(s32[3]{0:T(128)S(1)} %pad_add_fusion.place, bf16[152,512]{1,0:T(8,128)(2,1)S(1)} %arrive_3_2.1.hidden, bf16[32,224,152]{2,1,0:T(8,128)(2,1)S(1)} %copy-done.3, bf16[32,224,152]{2,1,0:T(8,128)(2,1)S(1)} %copy-done.2), custom_call_target="tpu_custom_call" | custom-call | flops 1048576 | bytes 1048576 | tf_op jit(solution)/shard_map/down_other_0/pallas_call | solution.py:276
  78.0 0.5 collective-permute-start.13
  78.5 1.5 %collective-permute-start.14 = (bf16[4,224,512]{2,1,0:T(8,128)(2,1)S(1)}, bf16[4,224,512]{2,1,0:T(8,128)(2,1)S(1)}, u32[]{:S(2)}, u32[]{:S(2)}) collective-permute-start(bf16[4,224,512]{2,1,0:T(8,128)(2,1)S(1)} %add_convert_fusion.1), channel_id=1, source_target_pairs={{0,4},{1,17},{2,6},{3,19},{4,0},{5,21},{6,2},{7,23},{8,12},{9,25},... | collective-permute-start | bytes 2752520 | tf_op jit(solution)/shard_map/ppermute | solution.py:327
  80.0 2.5 %collective-permute-start.15 = (bf16[4,224,512]{2,1,0:T(8,128)(2,1)S(1)}, bf16[4,224,512]{2,1,0:T(8,128)(2,1)S(1)}, u32[]{:S(2)}, u32[]{:S(2)}) collective-permute-start(bf16[4,224,512]{2,1,0:T(8,128)(2,1)S(1)} %add_convert_fusion.2), channel_id=1, source_target_pairs={{0,2},{1,9},{2,4},{3,11},{4,6},{5,13},{6,0},{7,15},{8,10},{9,17},{... | collective-permute-start | bytes 2752520 | tf_op jit(solution)/shard_map/ppermute | solution.py:327
  82.5 1.8 %collective-permute-start.16 = (bf16[4,224,512]{2,1,0:T(8,128)(2,1)S(1)}, bf16[4,224,512]{2,1,0:T(8,128)(2,1)S(1)}, u32[]{:S(2)}, u32[]{:S(2)}) collective-permute-start(bf16[4,224,512]{2,1,0:T(8,128)(2,1)S(1)} %add_convert_fusion), channel_id=1, source_target_pairs={{0,6},{1,25},{2,0},{3,27},{4,2},{5,29},{6,4},{7,31},{8,14},{9,1},{... | collective-permute-start | bytes 2752520 | tf_op jit(solution)/shard_map/ppermute | solution.py:327
  84.3 1.5 %down_mine_0.1 = f32[4,224,512]{2,1,0:T(8,128)S(1)} custom-call(s32[3]{0:T(128)S(1)} %pad_add_fusion.place, bf16[152,512]{1,0:T(8,128)(2,1)S(1)} %arrive_3_2.1.hidden, bf16[32,224,152]{2,1,0:T(8,128)(2,1)S(1)} %copy-done.3, bf16[32,224,152]{2,1,0:T(8,128)(2,1)S(1)} %copy-done.2), custom_call_target="tpu_custom_call" | custom-call | flops 1048576 | bytes 1048576 | tf_op jit(solution)/shard_map/down_mine_0/pallas_call | solution.py:276
  85.8 7.7 %collective-permute-done.14 = bf16[4,224,512]{2,1,0:T(8,128)(2,1)S(1)} collective-permute-done((bf16[4,224,512]{2,1,0:T(8,128)(2,1)S(1)}, bf16[4,224,512]{2,1,0:T(8,128)(2,1)S(1)}, u32[]{:S(2)}, u32[]{:S(2)}) %collective-permute-start.14) | collective-permute-done | bytes 917536 | tf_op jit(solution)/shard_map/ppermute | solution.py:327
  93.5 12.0 %collective-permute-done.15 = bf16[4,224,512]{2,1,0:T(8,128)(2,1)S(1)} collective-permute-done((bf16[4,224,512]{2,1,0:T(8,128)(2,1)S(1)}, bf16[4,224,512]{2,1,0:T(8,128)(2,1)S(1)}, u32[]{:S(2)}, u32[]{:S(2)}) %collective-permute-start.15) | collective-permute-done | bytes 917536 | tf_op jit(solution)/shard_map/ppermute | solution.py:327
  105.5 0.7 fusion.7
  106.3 0.7 collective-permute-start.17
  106.9 2.1 %collective-permute-start.19 = (bf16[224,512]{1,0:T(8,128)(2,1)S(1)}, bf16[224,512]{1,0:T(8,128)(2,1)S(1)}, u32[]{:S(2)}, u32[]{:S(2)}) collective-permute-start(bf16[224,512]{1,0:T(8,128)(2,1)S(1)} %get-tuple-element.116), channel_id=1, source_target_pairs={{0,24},{1,7},{2,26},{3,1},{4,28},{5,3},{6,30},{7,5},{8,0},{9,15},{... | collective-permute-start | bytes 688136 | tf_op jit(solution)/shard_map/ppermute | solution.py:324
  109.0 0.1 collective-permute-start.18
  109.1 4.7 %collective-permute-done.17 = bf16[224,512]{1,0:T(8,128)(2,1)S(1)} collective-permute-done((bf16[224,512]{1,0:T(8,128)(2,1)S(1)}, bf16[224,512]{1,0:T(8,128)(2,1)S(1)}, u32[]{:S(2)}, u32[]{:S(2)}) %collective-permute-start.17) | collective-permute-done | bytes 229408 | tf_op jit(solution)/shard_map/ppermute | solution.py:324
  113.9 1.7 %collective-permute-done.19 = bf16[224,512]{1,0:T(8,128)(2,1)S(1)} collective-permute-done((bf16[224,512]{1,0:T(8,128)(2,1)S(1)}, bf16[224,512]{1,0:T(8,128)(2,1)S(1)}, u32[]{:S(2)}, u32[]{:S(2)}) %collective-permute-start.19) | collective-permute-done | bytes 229408 | tf_op jit(solution)/shard_map/ppermute | solution.py:324
  115.6 0.7 collective-permute-done.18
  116.3 0.1 fusion.2
  116.5 0.1 copy.13
  116.6 16.4 %all_to_all.10 = bf16[8,48,224]{2,1,0:T(8,128)(2,1)S(1)} all-to-all(bf16[8,48,224]{2,1,0:T(8,128)(2,1)S(1)} %bitcast.49), channel_id=1, replica_groups=mesh['expert'=8,'tensor'=32] {'expert'}, dimensions={0} | all-to-all | bytes 344064 | tf_op jit(solution)/shard_map/all_to_all | solution.py:369
  133.1 1.0 fusion.5
  (21 shorter events, 0.2 us)
Async XLA Ops:
  1.9 18.9 %all-to-all-start = ((bf16[8,48,224]{2,1,0:T(8,128)(2,1)}), bf16[8,48,224]{2,1,0:T(8,128)(2,1)S(1)}, u32[]{:S(2)}, u32[]{:S(2)}) async-start(bf16[8,48,224]{2,1,0:T(8,128)(2,1)} %bitcast.56), calls=%async_computation | async-start | bytes 393216 | tf_op jit(solution)/shard_map/all_to_all | solution.py:313
  15.4 5.6 %copy-start.4 = (bf16[128,224]{0,1:T(8,128)(2,1)S(1)}, bf16[128,224]{0,1:T(8,128)(2,1)}, u32[]{:S(2)}) copy-start(bf16[128,224]{0,1:T(8,128)(2,1)} %param.10) | copy-start | bytes 172036
  21.0 11.6 %collective-permute-start.1 = (bf16[224,512]{1,0:T(8,128)(2,1)S(1)}, bf16[224,512]{1,0:T(8,128)(2,1)S(1)}, u32[]{:S(2)}, u32[]{:S(2)}) collective-permute-start(bf16[224,512]{1,0:T(8,128)(2,1)S(1)} %get-tuple-element.119), channel_id=1, source_target_pairs={{0,16},{1,5},{2,18},{3,7},{4,20},{5,1},{6,22},{7,3},{8,24},{9,13},... | collective-permute-start | bytes 688136 | tf_op jit(solution)/shard_map/ppermute | solution.py:324
  24.1 8.5 %collective-permute-start = (bf16[224,512]{1,0:T(8,128)(2,1)S(1)}, bf16[224,512]{1,0:T(8,128)(2,1)S(1)}, u32[]{:S(2)}, u32[]{:S(2)}) collective-permute-start(bf16[224,512]{1,0:T(8,128)(2,1)S(1)} %get-tuple-element.119), channel_id=1, source_target_pairs={{0,8},{1,3},{2,10},{3,5},{4,12},{5,7},{6,14},{7,1},{8,16},{9,11},{... | collective-permute-start | bytes 688136 | tf_op jit(solution)/shard_map/ppermute | solution.py:324
  24.7 7.9 %collective-permute-start.2 = (bf16[224,512]{1,0:T(8,128)(2,1)S(1)}, bf16[224,512]{1,0:T(8,128)(2,1)S(1)}, u32[]{:S(2)}, u32[]{:S(2)}) collective-permute-start(bf16[224,512]{1,0:T(8,128)(2,1)S(1)} %get-tuple-element.119), channel_id=1, source_target_pairs={{0,24},{1,7},{2,26},{3,1},{4,28},{5,3},{6,30},{7,5},{8,0},{9,15},{... | collective-permute-start | bytes 688136 | tf_op jit(solution)/shard_map/ppermute | solution.py:324
  32.8 16.5 %collective-permute-start.6 = (bf16[4,224,512]{2,1,0:T(8,128)(2,1)S(1)}, bf16[4,224,512]{2,1,0:T(8,128)(2,1)}, u32[]{:S(2)}, u32[]{:S(2)}) collective-permute-start(bf16[4,224,512]{2,1,0:T(8,128)(2,1)S(1)} %pad_maximum_fusion.refs_0_), channel_id=1, source_target_pairs={{0,1},{1,0},{2,3},{3,2},{4,5},{5,4},{6,7},{7,6},{8,9},{9,8},{10,11... | collective-permute-start | bytes 2752520 | tf_op jit(solution)/shard_map/ppermute | solution.py:39
  32.9 16.4 %collective-permute-start.5 = (bf16[4,224,512]{2,1,0:T(8,128)(2,1)S(1)}, bf16[4,224,512]{2,1,0:T(8,128)(2,1)}, u32[]{:S(2)}, u32[]{:S(2)}) collective-permute-start(bf16[4,224,512]{2,1,0:T(8,128)(2,1)S(1)} %pad_maximum_fusion.refs_0_), channel_id=1, source_target_pairs={{0,2},{1,9},{2,4},{3,11},{4,6},{5,13},{6,0},{7,15},{8,10},{9,17},{... | collective-permute-start | bytes 2752520 | tf_op jit(solution)/shard_map/ppermute | solution.py:327
  34.6 18.9 %collective-permute-start.4 = (bf16[4,224,512]{2,1,0:T(8,128)(2,1)S(1)}, bf16[4,224,512]{2,1,0:T(8,128)(2,1)S(1)}, u32[]{:S(2)}, u32[]{:S(2)}) collective-permute-start(bf16[4,224,512]{2,1,0:T(8,128)(2,1)S(1)} %pad_maximum_fusion.refs_0_), channel_id=1, source_target_pairs={{0,6},{1,25},{2,0},{3,27},{4,2},{5,29},{6,4},{7,31},{8,14},{9,1},{... | collective-permute-start | bytes 2752520 | tf_op jit(solution)/shard_map/ppermute | solution.py:327
  35.0 23.5 %collective-permute-start.3 = (bf16[4,224,512]{2,1,0:T(8,128)(2,1)S(1)}, bf16[4,224,512]{2,1,0:T(8,128)(2,1)S(1)}, u32[]{:S(2)}, u32[]{:S(2)}) collective-permute-start(bf16[4,224,512]{2,1,0:T(8,128)(2,1)S(1)} %pad_maximum_fusion.refs_0_), channel_id=1, source_target_pairs={{0,4},{1,17},{2,6},{3,19},{4,0},{5,21},{6,2},{7,23},{8,12},{9,25},... | collective-permute-start | bytes 2752520 | tf_op jit(solution)/shard_map/ppermute | solution.py:327
  42.7 2.4 %copy-start = (bf16[32,304,224]{2,1,0:T(8,128)(2,1)S(1)}, bf16[32,304,224]{2,1,0:T(8,128)(2,1)}, u32[]{:S(2)}) copy-start(bf16[32,304,224]{2,1,0:T(8,128)(2,1)} %up_weights.3.refs_2_.refs_4_.refs_5_.refs_6_.refs_7_.refs_8_) | copy-start | bytes 13074436
  45.1 2.4 %copy-start.1 = (bf16[32,304,224]{2,1,0:T(8,128)(2,1)S(1)}, bf16[32,304,224]{2,1,0:T(8,128)(2,1)}, u32[]{:S(2)}) copy-start(bf16[32,304,224]{2,1,0:T(8,128)(2,1)} %up_weights.2.refs_1_.refs_2_.refs_3_.refs_4_.refs_5_) | copy-start | bytes 13074436
  49.3 9.7 %collective-permute-start.9 = (bf16[4,224,512]{2,1,0:T(8,128)(2,1)}, bf16[4,224,512]{2,1,0:T(8,128)(2,1)S(1)}, u32[]{:S(2)}, u32[]{:S(2)}) collective-permute-start(bf16[4,224,512]{2,1,0:T(8,128)(2,1)} %collective-permute-done.5.refs_1_), channel_id=1, source_target_pairs={{0,1},{1,0},{2,3},{3,2},{4,5},{5,4},{6,7},{7,6},{8,9},{9,8},{10,11... | collective-permute-start | bytes 2752520 | tf_op jit(solution)/shard_map/ppermute | solution.py:39
  58.5 3.4 %collective-permute-start.7 = (bf16[4,224,512]{2,1,0:T(8,128)(2,1)S(1)}, bf16[4,224,512]{2,1,0:T(8,128)(2,1)S(1)}, u32[]{:S(2)}, u32[]{:S(2)}) collective-permute-start(bf16[4,224,512]{2,1,0:T(8,128)(2,1)S(1)} %collective-permute-done.3.refs_1_), channel_id=1, source_target_pairs={{0,1},{1,0},{2,3},{3,2},{4,5},{5,4},{6,7},{7,6},{8,9},{9,8},{10,11... | collective-permute-start | bytes 2752520 | tf_op jit(solution)/shard_map/ppermute | solution.py:39
  58.5 3.8 %collective-permute-start.8 = (bf16[4,224,512]{2,1,0:T(8,128)(2,1)S(1)}, bf16[4,224,512]{2,1,0:T(8,128)(2,1)S(1)}, u32[]{:S(2)}, u32[]{:S(2)}) collective-permute-start(bf16[4,224,512]{2,1,0:T(8,128)(2,1)S(1)} %collective-permute-done.4.refs_2_), channel_id=1, source_target_pairs={{0,1},{1,0},{2,3},{3,2},{4,5},{5,4},{6,7},{7,6},{8,9},{9,8},{10,11... | collective-permute-start | bytes 2752520 | tf_op jit(solution)/shard_map/ppermute | solution.py:39
  62.3 2.5 %copy-start.2 = (bf16[32,224,152]{2,1,0:T(8,128)(2,1)S(1)}, bf16[32,224,152]{2,1,0:T(8,128)(2,1)}, u32[]{:S(2)}) copy-start(bf16[32,224,152]{2,1,0:T(8,128)(2,1)} %down_weights.2.routed) | copy-start | bytes 6537220
  62.3 3.2 %copy-start.3 = (bf16[32,224,152]{2,1,0:T(8,128)(2,1)S(1)}, bf16[32,224,152]{2,1,0:T(8,128)(2,1)}, u32[]{:S(2)}) copy-start(bf16[32,224,152]{2,1,0:T(8,128)(2,1)} %down_weights.3.dense) | copy-start | bytes 6537220
  67.0 8.5 %collective-permute-start.11 = (bf16[4,224,512]{2,1,0:T(8,128)(2,1)S(1)}, bf16[4,224,512]{2,1,0:T(8,128)(2,1)S(1)}, u32[]{:S(2)}, u32[]{:S(2)}) collective-permute-start(bf16[4,224,512]{2,1,0:T(8,128)(2,1)S(1)} %down_other_2.1), channel_id=1, source_target_pairs={{0,1},{1,0},{2,3},{3,2},{4,5},{5,4},{6,7},{7,6},{8,9},{9,8},{10,11... | collective-permute-start | bytes 2752520 | tf_op jit(solution)/shard_map/ppermute | solution.py:39
  68.7 7.1 %collective-permute-start.10 = (bf16[4,224,512]{2,1,0:T(8,128)(2,1)S(1)}, bf16[4,224,512]{2,1,0:T(8,128)(2,1)S(1)}, u32[]{:S(2)}, u32[]{:S(2)}) collective-permute-start(bf16[4,224,512]{2,1,0:T(8,128)(2,1)S(1)} %down_other_1.1), channel_id=1, source_target_pairs={{0,1},{1,0},{2,3},{3,2},{4,5},{5,4},{6,7},{7,6},{8,9},{9,8},{10,11... | collective-permute-start | bytes 2752520 | tf_op jit(solution)/shard_map/ppermute | solution.py:39
  70.7 5.4 %collective-permute-start.12 = (bf16[4,224,512]{2,1,0:T(8,128)(2,1)S(1)}, bf16[4,224,512]{2,1,0:T(8,128)(2,1)S(1)}, u32[]{:S(2)}, u32[]{:S(2)}) collective-permute-start(bf16[4,224,512]{2,1,0:T(8,128)(2,1)S(1)} %down_other_3.1), channel_id=1, source_target_pairs={{0,1},{1,0},{2,3},{3,2},{4,5},{5,4},{6,7},{7,6},{8,9},{9,8},{10,11... | collective-permute-start | bytes 2752520 | tf_op jit(solution)/shard_map/ppermute | solution.py:39
  78.0 7.7 %collective-permute-start.13 = (bf16[4,224,512]{2,1,0:T(8,128)(2,1)S(1)}, bf16[4,224,512]{2,1,0:T(8,128)(2,1)S(1)}, u32[]{:S(2)}, u32[]{:S(2)}) collective-permute-start(bf16[4,224,512]{2,1,0:T(8,128)(2,1)S(1)} %down_other_0.1), channel_id=1, source_target_pairs={{0,1},{1,0},{2,3},{3,2},{4,5},{5,4},{6,7},{7,6},{8,9},{9,8},{10,11... | collective-permute-start | bytes 2752520 | tf_op jit(solution)/shard_map/ppermute | solution.py:39
  78.5 15.0 %collective-permute-start.14 = (bf16[4,224,512]{2,1,0:T(8,128)(2,1)S(1)}, bf16[4,224,512]{2,1,0:T(8,128)(2,1)S(1)}, u32[]{:S(2)}, u32[]{:S(2)}) collective-permute-start(bf16[4,224,512]{2,1,0:T(8,128)(2,1)S(1)} %add_convert_fusion.1), channel_id=1, source_target_pairs={{0,4},{1,17},{2,6},{3,19},{4,0},{5,21},{6,2},{7,23},{8,12},{9,25},... | collective-permute-start | bytes 2752520 | tf_op jit(solution)/shard_map/ppermute | solution.py:327
  80.0 25.5 %collective-permute-start.15 = (bf16[4,224,512]{2,1,0:T(8,128)(2,1)S(1)}, bf16[4,224,512]{2,1,0:T(8,128)(2,1)S(1)}, u32[]{:S(2)}, u32[]{:S(2)}) collective-permute-start(bf16[4,224,512]{2,1,0:T(8,128)(2,1)S(1)} %add_convert_fusion.2), channel_id=1, source_target_pairs={{0,2},{1,9},{2,4},{3,11},{4,6},{5,13},{6,0},{7,15},{8,10},{9,17},{... | collective-permute-start | bytes 2752520 | tf_op jit(solution)/shard_map/ppermute | solution.py:327
  82.5 23.0 %collective-permute-start.16 = (bf16[4,224,512]{2,1,0:T(8,128)(2,1)S(1)}, bf16[4,224,512]{2,1,0:T(8,128)(2,1)S(1)}, u32[]{:S(2)}, u32[]{:S(2)}) collective-permute-start(bf16[4,224,512]{2,1,0:T(8,128)(2,1)S(1)} %add_convert_fusion), channel_id=1, source_target_pairs={{0,6},{1,25},{2,0},{3,27},{4,2},{5,29},{6,4},{7,31},{8,14},{9,1},{... | collective-permute-start | bytes 2752520 | tf_op jit(solution)/shard_map/ppermute | solution.py:327
  106.2 26.9 %copy-start.5 = (f32[384,128]{1,0:T(8,128)S(1)}, f32[384,128]{1,0:T(8,128)}, u32[]{:S(2)}) copy-start(f32[384,128]{1,0:T(8,128)} %get-tuple-element.112) | copy-start | bytes 589828
  106.3 7.6 %collective-permute-start.17 = (bf16[224,512]{1,0:T(8,128)(2,1)S(1)}, bf16[224,512]{1,0:T(8,128)(2,1)S(1)}, u32[]{:S(2)}, u32[]{:S(2)}) collective-permute-start(bf16[224,512]{1,0:T(8,128)(2,1)S(1)} %get-tuple-element.115), channel_id=1, source_target_pairs={{0,16},{1,5},{2,18},{3,7},{4,20},{5,1},{6,22},{7,3},{8,24},{9,13},... | collective-permute-start | bytes 688136 | tf_op jit(solution)/shard_map/ppermute | solution.py:324
  106.9 8.7 %collective-permute-start.19 = (bf16[224,512]{1,0:T(8,128)(2,1)S(1)}, bf16[224,512]{1,0:T(8,128)(2,1)S(1)}, u32[]{:S(2)}, u32[]{:S(2)}) collective-permute-start(bf16[224,512]{1,0:T(8,128)(2,1)S(1)} %get-tuple-element.116), channel_id=1, source_target_pairs={{0,24},{1,7},{2,26},{3,1},{4,28},{5,3},{6,30},{7,5},{8,0},{9,15},{... | collective-permute-start | bytes 688136 | tf_op jit(solution)/shard_map/ppermute | solution.py:324
  109.0 7.3 %collective-permute-start.18 = (bf16[224,512]{1,0:T(8,128)(2,1)S(1)}, bf16[224,512]{1,0:T(8,128)(2,1)S(1)}, u32[]{:S(2)}, u32[]{:S(2)}) collective-permute-start(bf16[224,512]{1,0:T(8,128)(2,1)S(1)} %get-tuple-element.117), channel_id=1, source_target_pairs={{0,8},{1,3},{2,10},{3,5},{4,12},{5,7},{6,14},{7,1},{8,16},{9,11},{... | collective-permute-start | bytes 688136 | tf_op jit(solution)/shard_map/ppermute | solution.py:324

commit v2 on v1

--- a/solution.py
+++ b/solution.py
@@ -257,35 +257,45 @@
     )
 
 
-def down_kernel(dense_rows, place, hidden, dense, routed, out):
-    for weight, span in (
-        (dense, slice(0, dense_rows)),
-        (routed, slice(dense_rows, hidden.shape[1])),
-    ):
-        out[0, :, span] = jnp.dot(
-            weight[0], hidden[:, span], preferred_element_type=F32
-        ).astype(out.dtype)
-
-
-def down_pieces(place, hidden, weights, outer, other, dense_rows):
+def down_kernel(dense_rows, place, hidden, *refs):
+    mine, others = refs[4:]
+    for out, dense, routed in ((mine, refs[0], refs[1]), (others, refs[2], refs[3])):
+        for weight, span in (
+            (dense, slice(0, dense_rows)),
+            (routed, slice(dense_rows, hidden.shape[1])),
+        ):
+            out[0, :, span] = jnp.dot(
+                weight[0], hidden[:, span], preferred_element_type=F32
+            ).astype(out.dtype)
+
+
+def down_pieces(place, hidden, weights, outer, dense_rows):
     units, rows = hidden.shape
     cols = weights[0].shape[1]
-    weight = pl.BlockSpec(
-        (1, cols, units), lambda i, place: (piece_index(place, other, 1, outer, i), 0, 0)
-    )
+
+    def weight(other):
+        def index(i, place):
+            return piece_index(place, other, 1, outer, i), 0, 0
+
+        return pl.BlockSpec((1, cols, units), index)
+
+    out = pl.BlockSpec((1, cols, rows), lambda i, place: (i, 0, 0))
+    shape = (SIDE, cols, rows)
     return pl.pallas_call(
         functools.partial(down_kernel, dense_rows),
-        out_shape=jax.ShapeDtypeStruct((SIDE, cols, rows), BF16 if other else F32),
+        out_shape=(jax.ShapeDtypeStruct(shape, F32), jax.ShapeDtypeStruct(shape, BF16)),
         grid_spec=pltpu.PrefetchScalarGridSpec(
             num_scalar_prefetch=1,
             grid=(SIDE,),
-            in_specs=[pl.BlockSpec((units, rows), lambda i, place: (0, 0)), weight, weight],
-            out_specs=pl.BlockSpec((1, cols, rows), lambda i, place: (i, 0, 0)),
+            in_specs=[pl.BlockSpec((units, rows), lambda i, place: (0, 0))]
+            + [weight(False)] * 2
+            + [weight(True)] * 2,
+            out_specs=(out, out),
         ),
         compiler_params=pltpu.CompilerParams(vmem_limit_bytes=16 * MIB),
         cost_estimate=SMALL,
-        name=f"down_{'other' if other else 'mine'}_{outer}",
-    )(place, hidden, weights[0], weights[1])
+        name=f"down_pieces_{outer}",
+    )(place, hidden, weights[0], weights[1], weights[0], weights[1])
 
 
 def shards(
@@ -344,25 +354,18 @@
     far_other, left_other, sums = lax.optimization_barrier((far_other, left_other, sums))
     hidden = add([(far_other, 2, 0, True), (left_other, 3, 0, True)], sums=sums, last=True)
 
-    def shares(outer, other, hidden):
-        out = down_pieces(place, hidden, down, outer, other, rows)
-        return lax.optimization_barrier((out, hidden))
-
-    pieces, order = {}, (2, 1, 3)
-    for d in order:
-        pieces[d], hidden = shares(d, True, hidden)
-    pieces = {d: sibling(pieces[d]) for d in order}
-    for d in order:
-        mine, hidden = shares(d, False, hidden)
-        pieces[d] = (mine + pieces[d].astype(F32)).astype(BF16)
-    pieces, hidden = lax.optimization_barrier((pieces, hidden))
-    others, hidden = shares(0, True, hidden)
-    mine, hidden = shares(0, False, hidden)
-    level = mine + sibling(others).astype(F32)
-    for d in order:
-        level = level + level_two(pieces[d], d).astype(F32)
+    pieces, order = {}, (2, 1, 3, 0)
+    for i, outer in enumerate(order):
+        mine, others = down_pieces(place, hidden, down, outer, rows)
+        if i > 0:
+            before = order[i - 1]
+            pieces[before], hidden = lax.optimization_barrier((pieces[before], hidden))
+        pieces[outer] = mine + sibling(others).astype(F32)
+    level = pieces[0]
+    for d in order[:-1]:
+        level = level + level_two(pieces[d].astype(BF16), d).astype(F32)
     total = level[0]
-    for d in order:
+    for d in order[:-1]:
         total = total + level_one(level[d].astype(BF16), d).astype(F32)
 
     back = total[:, rows:].astype(BF16).T.reshape(experts, capacity, cols)

time: 135 us -> 129 us (0.956)
  Pallas kernels: 45.8 us -> 41.2 us
  waiting for transfers between devices: 32.7 us -> 31.1 us
    pallas_call x8 -> x4, Pallas kernels: 12.1 us -> 7.51 us  [down_pieces(): pl.pallas_call(functools.partial(down_kernel, dense_rows), out_shape=(jax...]
    ppermute x6, waiting for transfers between devices: 24.8 us -> 23.1 us  [level_two(): return lax.ppermute(value, 'tensor', hops(d, False))]
  transfers between devices with their start and end apart: 21 -> 21, of which waited for: 8 -> 8; matrix products, arithmetic and copies ran while one was open for 1% -> 1% of each run, Pallas kernels for 29% -> 27%
where the time goes in v2:
time: 129 us; the launch traced here: 128 us
  Pallas kernels  41.2 us (32%)
  waiting for transfers between devices  31.1 us (24%)
  starting transfers between devices  30.2 us (23%)
  blocking collectives  16.4 us (13%)
  local copies, waits for them, and re-layouts  5.89 us (5%)
  other arithmetic  2.08 us (2%)
    ppermute x6, waiting for transfers between devices, level_two(): return lax.ppermute(value, 'tensor', hops(d, False))  23.1 us
    pallas_call x4, Pallas kernels, layout_call(): pl.pallas_call(functools.partial(kernel, cols), out_shape=jax.ShapeDtypeS...  20.6 us
    all_to_all x1, blocking collectives, shards(): lax.all_to_all(back, 'expert', 0, 0, tiled=True)  16.4 us
    pallas_call x4, Pallas kernels, arrive(): pl.pallas_call(functools.partial(arrive_kernel, dense_rows, count, start,...  11.2 us
    ppermute x6, starting transfers between devices, level_two(): return lax.ppermute(value, 'tensor', hops(d, False))  10.8 us
    ppermute x6, starting transfers between devices, level_one(): return lax.ppermute(value, 'tensor', hops(d, True))  9.21 us
    all_to_all x1, starting transfers between devices, shards(): lax.all_to_all(outgoing.reshape(experts, capacity, cols), 'expert', 0, 0,...  8.47 us
    pallas_call x4, Pallas kernels, down_pieces(): pl.pallas_call(functools.partial(down_kernel, dense_rows), out_shape=(jax...  7.51 us
  transfers between devices with their start and end apart: 21, of which 8 were waited for; matrix products, arithmetic and copies ran while one was open for 1% of the time, Pallas kernels for 27%

profile of v2, /device:TPU:8, one launch (start us, length us, event | category | flops | bytes accessed | tf_op | source)
XLA Modules:
  0.0 128.1 jit_solution(7040505192092161123)
XLA Ops:
  0.0 1.9 %dispatch.1 = (bf16[384,224]{1,0:T(8,128)(2,1)}, f32[384,128]{1,0:T(8,128)}) custom-call(s32[2,128]{1,0:T(2,128)} %bitcast.59, f32[2,128]{1,0:T(2,128)} %bitcast.60, bf16[224,128]{1,0:T(8,128)(2,1)} %bitcast.54), custom_call_target="tpu_custom_call" | custom-call | tf_op jit(solution)/shard_map/dispatch/pallas_call | solution.py:80
  1.9 8.5 %all-to-all-start = ((bf16[8,48,224]{2,1,0:T(8,128)(2,1)}), bf16[8,48,224]{2,1,0:T(8,128)(2,1)S(1)}, u32[]{:S(2)}, u32[]{:S(2)}) async-start(bf16[8,48,224]{2,1,0:T(8,128)(2,1)} %bitcast.56), calls=%async_computation | async-start | bytes 393216 | tf_op jit(solution)/shard_map/all_to_all | solution.py:323
  10.4 5.0 %up_weights.3.refs_2_.refs_4_.refs_5_.refs_6_.refs_7_.refs_8_ = bf16[32,304,224]{2,1,0:T(8,128)(2,1)} custom-call(f32[1,7168]{1,0:T(1,128)} %bitcast.57, bf16[152,7168]{1,0:T(8,128)(2,1)} %bitcast.44, bf16[152,7168]{1,0:T(8,128)(2,1)} %bitcast.45), custom_call_target="tpu_custom_call" | custom-call | flops 1048576 | bytes 1048576 | tf_op jit(solution)/shard_map/up_weights/pallas_call | solution.py:147
  15.4 0.0 copy-start.4
  15.4 5.1 %up_weights.2.refs_1_.refs_2_.refs_3_.refs_4_.refs_5_ = bf16[32,304,224]{2,1,0:T(8,128)(2,1)} custom-call(f32[1,7168]{1,0:T(1,128)} %bitcast.58, bf16[152,7168]{1,0:T(8,128)(2,1)} %gate.1, bf16[152,7168]{1,0:T(8,128)(2,1)} %up.1), custom_call_target="tpu_custom_call" | custom-call | flops 1048576 | bytes 1048576 | tf_op jit(solution)/shard_map/up_weights/pallas_call | solution.py:147
  20.5 0.4 all-to-all-done
  20.8 0.1 copy.12
  21.0 3.1 %collective-permute-start.1 = (bf16[224,512]{1,0:T(8,128)(2,1)S(1)}, bf16[224,512]{1,0:T(8,128)(2,1)S(1)}, u32[]{:S(2)}, u32[]{:S(2)}) collective-permute-start(bf16[224,512]{1,0:T(8,128)(2,1)S(1)} %get-tuple-element.107), channel_id=1, source_target_pairs={{0,16},{1,5},{2,18},{3,7},{4,20},{5,1},{6,22},{7,3},{8,24},{9,13},... | collective-permute-start | bytes 688136 | tf_op jit(solution)/shard_map/ppermute | solution.py:334
  24.1 0.6 collective-permute-start
  24.7 2.6 %collective-permute-start.2 = (bf16[224,512]{1,0:T(8,128)(2,1)S(1)}, bf16[224,512]{1,0:T(8,128)(2,1)S(1)}, u32[]{:S(2)}, u32[]{:S(2)}) collective-permute-start(bf16[224,512]{1,0:T(8,128)(2,1)S(1)} %get-tuple-element.107), channel_id=1, source_target_pairs={{0,24},{1,7},{2,26},{3,1},{4,28},{5,3},{6,30},{7,5},{8,0},{9,15},{... | collective-permute-start | bytes 688136 | tf_op jit(solution)/shard_map/ppermute | solution.py:334
  27.4 5.3 %down_weights.2.refs_1_.refs_3_ = bf16[32,224,152]{2,1,0:T(8,128)(2,1)} custom-call(bf16[152,7168]{1,0:T(8,128)(2,1)} %bitcast.46), custom_call_target="tpu_custom_call" | custom-call | flops 1048576 | bytes 1048576 | tf_op jit(solution)/shard_map/down_weights/pallas_call | solution.py:147
  32.7 0.0 collective-permute-done.1
  32.7 0.0 collective-permute-done
  32.7 0.1 pad_maximum_fusion.refs_0_
  32.8 0.1 collective-permute-start.6
  32.9 1.7 %collective-permute-start.5 = (bf16[4,224,512]{2,1,0:T(8,128)(2,1)S(1)}, bf16[4,224,512]{2,1,0:T(8,128)(2,1)}, u32[]{:S(2)}, u32[]{:S(2)}) collective-permute-start(bf16[4,224,512]{2,1,0:T(8,128)(2,1)S(1)} %pad_maximum_fusion.refs_0_), channel_id=1, source_target_pairs={{0,2},{1,9},{2,4},{3,11},{4,6},{5,13},{6,0},{7,15},{8,10},{9,17},{... | collective-permute-start | bytes 2752520 | tf_op jit(solution)/shard_map/ppermute | solution.py:337
  34.6 0.5 collective-permute-start.4
  35.0 2.3 %collective-permute-start.3 = (bf16[4,224,512]{2,1,0:T(8,128)(2,1)S(1)}, bf16[4,224,512]{2,1,0:T(8,128)(2,1)S(1)}, u32[]{:S(2)}, u32[]{:S(2)}) collective-permute-start(bf16[4,224,512]{2,1,0:T(8,128)(2,1)S(1)} %pad_maximum_fusion.refs_0_), channel_id=1, source_target_pairs={{0,4},{1,17},{2,6},{3,19},{4,0},{5,21},{6,2},{7,23},{8,12},{9,25},... | collective-permute-start | bytes 2752520 | tf_op jit(solution)/shard_map/ppermute | solution.py:337
  37.3 5.3 %down_weights.3.refs_0_.refs_2_ = bf16[32,224,152]{2,1,0:T(8,128)(2,1)} custom-call(bf16[152,7168]{1,0:T(8,128)(2,1)} %down.1), custom_call_target="tpu_custom_call" | custom-call | flops 1048576 | bytes 1048576 | tf_op jit(solution)/shard_map/down_weights/pallas_call | solution.py:147
  42.6 0.1 pad_add_fusion.place
  42.7 2.4 %copy-done = bf16[32,304,224]{2,1,0:T(8,128)(2,1)S(1)} copy-done((bf16[32,304,224]{2,1,0:T(8,128)(2,1)S(1)}, bf16[32,304,224]{2,1,0:T(8,128)(2,1)}, u32[]{:S(2)}) %copy-start) | copy-done | bytes 4358168
  45.1 2.4 %copy-done.1 = bf16[32,304,224]{2,1,0:T(8,128)(2,1)S(1)} copy-done((bf16[32,304,224]{2,1,0:T(8,128)(2,1)S(1)}, bf16[32,304,224]{2,1,0:T(8,128)(2,1)}, u32[]{:S(2)}) %copy-start.1) | copy-done | bytes 4358168
  47.5 1.8 %arrive_0_1.1 = (f32[304,128]{1,0:T(8,128)S(1)}, f32[304,384]{1,0:T(8,128)S(1)}, f32[8,512]{1,0:T(8,128)S(1)}) custom-call(s32[3]{0:T(128)S(1)} %pad_add_fusion.place, bf16[4,224,512]{2,1,0:T(8,128)(2,1)S(1)} %pad_maximum_fusion.refs_0_, bf16[32,304,224]{2,1,0:T(8,128)(2,1)S(1)} %copy-done.1, bf16[32,304,224]{2,1,0:T(8,128)(2,1)S(1)} %copy-done), custom_call_target="tpu_custom_call" | custom-call | flops 1048576 | bytes 1048576 | tf_op jit(solution)/shard_map/arrive_0_1/pallas_call | solution.py:236
  49.3 0.0 collective-permute-done.5.refs_1_
  49.3 0.1 collective-permute-start.9
  49.4 4.0 %arrive_1_2.1 = (f32[304,128]{1,0:T(8,128)S(1)}, f32[304,384]{1,0:T(8,128)S(1)}, f32[8,512]{1,0:T(8,128)S(1)}) custom-call(s32[3]{0:T(128)S(1)} %pad_add_fusion.place, bf16[4,224,512]{2,1,0:T(8,128)(2,1)} %collective-permute-done.6.refs_0_, bf16[4,224,512]{2,1,0:T(8,128)(2,1)} %collective-permute-done.5.refs_1_, bf16[32,304,224]{2,1,0:T(8,128)(2,1)S(1)} %copy-done.1, ...), custom_call_target="tpu_custom_call" | custom-call | flops 1048576 | bytes 1048576 | tf_op jit(solution)/shard_map/arrive_1_2/pallas_call | solution.py:236
  53.5 0.0 collective-permute-done.4.refs_2_
  53.5 5.0 %collective-permute-done.3.refs_1_ = bf16[4,224,512]{2,1,0:T(8,128)(2,1)S(1)} collective-permute-done((bf16[4,224,512]{2,1,0:T(8,128)(2,1)S(1)}, bf16[4,224,512]{2,1,0:T(8,128)(2,1)S(1)}, u32[]{:S(2)}, u32[]{:S(2)}) %collective-permute-start.3) | collective-permute-done | bytes 917536 | tf_op jit(solution)/shard_map/ppermute | solution.py:337
  58.5 0.0 collective-permute-start.7
  58.5 0.5 collective-permute-start.8
  59.0 0.0 collective-permute-done.9.refs_0_
  59.0 2.9 %arrive_3_3.1 = (f32[304,128]{1,0:T(8,128)S(1)}, f32[304,384]{1,0:T(8,128)S(1)}, f32[8,512]{1,0:T(8,128)S(1)}) custom-call(s32[3]{0:T(128)S(1)} %pad_add_fusion.place, bf16[4,224,512]{2,1,0:T(8,128)(2,1)S(1)} %collective-permute-done.9.refs_0_, bf16[4,224,512]{2,1,0:T(8,128)(2,1)S(1)} %collective-permute-done.3.refs_1_, ...), custom_call_target="tpu_custom_call" | custom-call | flops 1048576 | bytes 1048576 | tf_op jit(solution)/shard_map/arrive_3_3/pallas_call | solution.py:236
  61.9 0.0 collective-permute-done.7.refs_0_
  61.9 0.4 collective-permute-done.8.refs_1_
  62.3 2.5 %arrive_3_2.1.hidden = bf16[152,512]{1,0:T(8,128)(2,1)S(1)} custom-call(s32[3]{0:T(128)S(1)} %pad_add_fusion.place, bf16[4,224,512]{2,1,0:T(8,128)(2,1)S(1)} %collective-permute-done.7.refs_0_, bf16[4,224,512]{2,1,0:T(8,128)(2,1)S(1)} %collective-permute-done.8.refs_1_, bf16[32,304,224]{2,1,0:T(8,128)(2,1)S(1)} %copy-done.1, ...), custom_call_target="tpu_custom_call" | custom-call | flops 1048576 | bytes 1048576 | tf_op jit(solution)/shard_map/arrive_3_2/pallas_call | solution.py:236
  64.8 0.7 copy-done.3
  65.5 1.9 %down_pieces_2.1 = (f32[4,224,512]{2,1,0:T(8,128)S(1)}, bf16[4,224,512]{2,1,0:T(8,128)(2,1)S(1)}) custom-call(s32[3]{0:T(128)S(1)} %pad_add_fusion.place, bf16[152,512]{1,0:T(8,128)(2,1)S(1)} %arrive_3_2.1.hidden, bf16[32,224,152]{2,1,0:T(8,128)(2,1)S(1)} %copy-done.3, bf16[32,224,152]{2,1,0:T(8,128)(2,1)S(1)} %copy-done.2, ...), custom_call_target="tpu_custom_call" | custom-call | flops 1048576 | bytes 1048576 | tf_op jit(solution)/shard_map/down_pieces_2/pallas_call | solution.py:284
  67.3 0.2 collective-permute-start.11
  67.6 1.9 %down_pieces_1.1 = (f32[4,224,512]{2,1,0:T(8,128)S(1)}, bf16[4,224,512]{2,1,0:T(8,128)(2,1)S(1)}) custom-call(s32[3]{0:T(128)S(1)} %pad_add_fusion.place, bf16[152,512]{1,0:T(8,128)(2,1)S(1)} %arrive_3_2.1.hidden, bf16[32,224,152]{2,1,0:T(8,128)(2,1)S(1)} %copy-done.3, bf16[32,224,152]{2,1,0:T(8,128)(2,1)S(1)} %copy-done.2, ...), custom_call_target="tpu_custom_call" | custom-call | flops 1048576 | bytes 1048576 | tf_op jit(solution)/shard_map/down_pieces_1/pallas_call | solution.py:284
  69.5 0.5 collective-permute-start.10
  69.9 0.0 collective-permute-done.11
  69.9 0.3 convert_add_fusion.2
  70.2 1.9 %down_pieces_3.1 = (f32[4,224,512]{2,1,0:T(8,128)S(1)}, bf16[4,224,512]{2,1,0:T(8,128)(2,1)S(1)}) custom-call(s32[3]{0:T(128)S(1)} %pad_add_fusion.place, bf16[152,512]{1,0:T(8,128)(2,1)S(1)} %arrive_3_2.1.hidden, bf16[32,224,152]{2,1,0:T(8,128)(2,1)S(1)} %copy-done.3, bf16[32,224,152]{2,1,0:T(8,128)(2,1)S(1)} %copy-done.2, ...), custom_call_target="tpu_custom_call" | custom-call | flops 1048576 | bytes 1048576 | tf_op jit(solution)/shard_map/down_pieces_3/pallas_call | solution.py:284
  72.1 0.2 collective-permute-start.15
  72.4 1.5 %collective-permute-start.13 = (bf16[4,224,512]{2,1,0:T(8,128)(2,1)S(1)}, bf16[4,224,512]{2,1,0:T(8,128)(2,1)S(1)}, u32[]{:S(2)}, u32[]{:S(2)}) collective-permute-start(bf16[4,224,512]{2,1,0:T(8,128)(2,1)S(1)} %convert_add_fusion.2), channel_id=1, source_target_pairs={{0,4},{1,17},{2,6},{3,19},{4,0},{5,21},{6,2},{7,23},{8,12},{9,25},... | collective-permute-start | bytes 2752520 | tf_op jit(solution)/shard_map/ppermute | solution.py:337
  73.9 0.4 convert_add_fusion.3
  74.2 1.9 %down_pieces_0.1 = (f32[4,224,512]{2,1,0:T(8,128)S(1)}, bf16[4,224,512]{2,1,0:T(8,128)(2,1)S(1)}) custom-call(s32[3]{0:T(128)S(1)} %pad_add_fusion.place, bf16[152,512]{1,0:T(8,128)(2,1)S(1)} %arrive_3_2.1.hidden, bf16[32,224,152]{2,1,0:T(8,128)(2,1)S(1)} %copy-done.3, bf16[32,224,152]{2,1,0:T(8,128)(2,1)S(1)} %copy-done.2, ...), custom_call_target="tpu_custom_call" | custom-call | flops 1048576 | bytes 1048576 | tf_op jit(solution)/shard_map/down_pieces_0/pallas_call | solution.py:284
  76.1 0.1 collective-permute-start.12
  76.2 2.8 %collective-permute-start.14 = (bf16[4,224,512]{2,1,0:T(8,128)(2,1)S(1)}, bf16[4,224,512]{2,1,0:T(8,128)(2,1)S(1)}, u32[]{:S(2)}, u32[]{:S(2)}) collective-permute-start(bf16[4,224,512]{2,1,0:T(8,128)(2,1)S(1)} %convert_add_fusion.3), channel_id=1, source_target_pairs={{0,2},{1,9},{2,4},{3,11},{4,6},{5,13},{6,0},{7,15},{8,10},{9,17},{... | collective-permute-start | bytes 2752520 | tf_op jit(solution)/shard_map/ppermute | solution.py:337
  79.1 0.4 convert_add_fusion.1
  79.4 2.1 %collective-permute-start.16 = (bf16[4,224,512]{2,1,0:T(8,128)(2,1)S(1)}, bf16[4,224,512]{2,1,0:T(8,128)(2,1)S(1)}, u32[]{:S(2)}, u32[]{:S(2)}) collective-permute-start(bf16[4,224,512]{2,1,0:T(8,128)(2,1)S(1)} %convert_add_fusion.1), channel_id=1, source_target_pairs={{0,6},{1,25},{2,0},{3,27},{4,2},{5,29},{6,4},{7,31},{8,14},{9,1},{... | collective-permute-start | bytes 2752520 | tf_op jit(solution)/shard_map/ppermute | solution.py:337
  81.5 5.9 %collective-permute-done.13 = bf16[4,224,512]{2,1,0:T(8,128)(2,1)S(1)} collective-permute-done((bf16[4,224,512]{2,1,0:T(8,128)(2,1)S(1)}, bf16[4,224,512]{2,1,0:T(8,128)(2,1)S(1)}, u32[]{:S(2)}, u32[]{:S(2)}) %collective-permute-start.13) | collective-permute-done | bytes 917536 | tf_op jit(solution)/shard_map/ppermute | solution.py:337
  87.4 12.2 %collective-permute-done.14 = bf16[4,224,512]{2,1,0:T(8,128)(2,1)S(1)} collective-permute-done((bf16[4,224,512]{2,1,0:T(8,128)(2,1)S(1)}, bf16[4,224,512]{2,1,0:T(8,128)(2,1)S(1)}, u32[]{:S(2)}, u32[]{:S(2)}) %collective-permute-start.14) | collective-permute-done | bytes 917536 | tf_op jit(solution)/shard_map/ppermute | solution.py:337
  99.6 0.7 fusion.7
  100.3 0.7 collective-permute-start.17
  101.0 2.1 %collective-permute-start.19 = (bf16[224,512]{1,0:T(8,128)(2,1)S(1)}, bf16[224,512]{1,0:T(8,128)(2,1)S(1)}, u32[]{:S(2)}, u32[]{:S(2)}) collective-permute-start(bf16[224,512]{1,0:T(8,128)(2,1)S(1)} %get-tuple-element.104), channel_id=1, source_target_pairs={{0,24},{1,7},{2,26},{3,1},{4,28},{5,3},{6,30},{7,5},{8,0},{9,15},{... | collective-permute-start | bytes 688136 | tf_op jit(solution)/shard_map/ppermute | solution.py:334
  103.1 0.1 collective-permute-start.18
  103.2 4.8 %collective-permute-done.17 = bf16[224,512]{1,0:T(8,128)(2,1)S(1)} collective-permute-done((bf16[224,512]{1,0:T(8,128)(2,1)S(1)}, bf16[224,512]{1,0:T(8,128)(2,1)S(1)}, u32[]{:S(2)}, u32[]{:S(2)}) %collective-permute-start.17) | collective-permute-done | bytes 229408 | tf_op jit(solution)/shard_map/ppermute | solution.py:334
  108.0 1.7 %collective-permute-done.19 = bf16[224,512]{1,0:T(8,128)(2,1)S(1)} collective-permute-done((bf16[224,512]{1,0:T(8,128)(2,1)S(1)}, bf16[224,512]{1,0:T(8,128)(2,1)S(1)}, u32[]{:S(2)}, u32[]{:S(2)}) %collective-permute-start.19) | collective-permute-done | bytes 229408 | tf_op jit(solution)/shard_map/ppermute | solution.py:334
  109.7 0.7 collective-permute-done.18
  110.4 0.1 fusion.2
  110.6 0.1 copy.13
  110.7 16.4 %all_to_all.10 = bf16[8,48,224]{2,1,0:T(8,128)(2,1)S(1)} all-to-all(bf16[8,48,224]{2,1,0:T(8,128)(2,1)S(1)} %bitcast.49), channel_id=1, replica_groups=mesh['expert'=8,'tensor'=32] {'expert'}, dimensions={0} | all-to-all | bytes 344064 | tf_op jit(solution)/shard_map/all_to_all | solution.py:372
  127.1 1.0 fusion.5
  (17 shorter events, 0.1 us)
Async XLA Ops:
  1.9 18.9 %all-to-all-start = ((bf16[8,48,224]{2,1,0:T(8,128)(2,1)}), bf16[8,48,224]{2,1,0:T(8,128)(2,1)S(1)}, u32[]{:S(2)}, u32[]{:S(2)}) async-start(bf16[8,48,224]{2,1,0:T(8,128)(2,1)} %bitcast.56), calls=%async_computation | async-start | bytes 393216 | tf_op jit(solution)/shard_map/all_to_all | solution.py:323
  15.4 5.6 %copy-start.4 = (bf16[128,224]{0,1:T(8,128)(2,1)S(1)}, bf16[128,224]{0,1:T(8,128)(2,1)}, u32[]{:S(2)}) copy-start(bf16[128,224]{0,1:T(8,128)(2,1)} %param.10) | copy-start | bytes 172036
  21.0 11.6 %collective-permute-start.1 = (bf16[224,512]{1,0:T(8,128)(2,1)S(1)}, bf16[224,512]{1,0:T(8,128)(2,1)S(1)}, u32[]{:S(2)}, u32[]{:S(2)}) collective-permute-start(bf16[224,512]{1,0:T(8,128)(2,1)S(1)} %get-tuple-element.107), channel_id=1, source_target_pairs={{0,16},{1,5},{2,18},{3,7},{4,20},{5,1},{6,22},{7,3},{8,24},{9,13},... | collective-permute-start | bytes 688136 | tf_op jit(solution)/shard_map/ppermute | solution.py:334
  24.1 8.5 %collective-permute-start = (bf16[224,512]{1,0:T(8,128)(2,1)S(1)}, bf16[224,512]{1,0:T(8,128)(2,1)S(1)}, u32[]{:S(2)}, u32[]{:S(2)}) collective-permute-start(bf16[224,512]{1,0:T(8,128)(2,1)S(1)} %get-tuple-element.107), channel_id=1, source_target_pairs={{0,8},{1,3},{2,10},{3,5},{4,12},{5,7},{6,14},{7,1},{8,16},{9,11},{... | collective-permute-start | bytes 688136 | tf_op jit(solution)/shard_map/ppermute | solution.py:334
  24.7 7.9 %collective-permute-start.2 = (bf16[224,512]{1,0:T(8,128)(2,1)S(1)}, bf16[224,512]{1,0:T(8,128)(2,1)S(1)}, u32[]{:S(2)}, u32[]{:S(2)}) collective-permute-start(bf16[224,512]{1,0:T(8,128)(2,1)S(1)} %get-tuple-element.107), channel_id=1, source_target_pairs={{0,24},{1,7},{2,26},{3,1},{4,28},{5,3},{6,30},{7,5},{8,0},{9,15},{... | collective-permute-start | bytes 688136 | tf_op jit(solution)/shard_map/ppermute | solution.py:334
  32.8 16.5 %collective-permute-start.6 = (bf16[4,224,512]{2,1,0:T(8,128)(2,1)S(1)}, bf16[4,224,512]{2,1,0:T(8,128)(2,1)}, u32[]{:S(2)}, u32[]{:S(2)}) collective-permute-start(bf16[4,224,512]{2,1,0:T(8,128)(2,1)S(1)} %pad_maximum_fusion.refs_0_), channel_id=1, source_target_pairs={{0,1},{1,0},{2,3},{3,2},{4,5},{5,4},{6,7},{7,6},{8,9},{9,8},{10,11... | collective-permute-start | bytes 2752520 | tf_op jit(solution)/shard_map/ppermute | solution.py:39
  32.9 16.4 %collective-permute-start.5 = (bf16[4,224,512]{2,1,0:T(8,128)(2,1)S(1)}, bf16[4,224,512]{2,1,0:T(8,128)(2,1)}, u32[]{:S(2)}, u32[]{:S(2)}) collective-permute-start(bf16[4,224,512]{2,1,0:T(8,128)(2,1)S(1)} %pad_maximum_fusion.refs_0_), channel_id=1, source_target_pairs={{0,2},{1,9},{2,4},{3,11},{4,6},{5,13},{6,0},{7,15},{8,10},{9,17},{... | collective-permute-start | bytes 2752520 | tf_op jit(solution)/shard_map/ppermute | solution.py:337
  34.6 18.9 %collective-permute-start.4 = (bf16[4,224,512]{2,1,0:T(8,128)(2,1)S(1)}, bf16[4,224,512]{2,1,0:T(8,128)(2,1)S(1)}, u32[]{:S(2)}, u32[]{:S(2)}) collective-permute-start(bf16[4,224,512]{2,1,0:T(8,128)(2,1)S(1)} %pad_maximum_fusion.refs_0_), channel_id=1, source_target_pairs={{0,6},{1,25},{2,0},{3,27},{4,2},{5,29},{6,4},{7,31},{8,14},{9,1},{... | collective-permute-start | bytes 2752520 | tf_op jit(solution)/shard_map/ppermute | solution.py:337
  35.0 23.5 %collective-permute-start.3 = (bf16[4,224,512]{2,1,0:T(8,128)(2,1)S(1)}, bf16[4,224,512]{2,1,0:T(8,128)(2,1)S(1)}, u32[]{:S(2)}, u32[]{:S(2)}) collective-permute-start(bf16[4,224,512]{2,1,0:T(8,128)(2,1)S(1)} %pad_maximum_fusion.refs_0_), channel_id=1, source_target_pairs={{0,4},{1,17},{2,6},{3,19},{4,0},{5,21},{6,2},{7,23},{8,12},{9,25},... | collective-permute-start | bytes 2752520 | tf_op jit(solution)/shard_map/ppermute | solution.py:337
  42.7 2.4 %copy-start = (bf16[32,304,224]{2,1,0:T(8,128)(2,1)S(1)}, bf16[32,304,224]{2,1,0:T(8,128)(2,1)}, u32[]{:S(2)}) copy-start(bf16[32,304,224]{2,1,0:T(8,128)(2,1)} %up_weights.3.refs_2_.refs_4_.refs_5_.refs_6_.refs_7_.refs_8_) | copy-start | bytes 13074436
  45.1 2.4 %copy-start.1 = (bf16[32,304,224]{2,1,0:T(8,128)(2,1)S(1)}, bf16[32,304,224]{2,1,0:T(8,128)(2,1)}, u32[]{:S(2)}) copy-start(bf16[32,304,224]{2,1,0:T(8,128)(2,1)} %up_weights.2.refs_1_.refs_2_.refs_3_.refs_4_.refs_5_) | copy-start | bytes 13074436
  49.3 9.7 %collective-permute-start.9 = (bf16[4,224,512]{2,1,0:T(8,128)(2,1)}, bf16[4,224,512]{2,1,0:T(8,128)(2,1)S(1)}, u32[]{:S(2)}, u32[]{:S(2)}) collective-permute-start(bf16[4,224,512]{2,1,0:T(8,128)(2,1)} %collective-permute-done.5.refs_1_), channel_id=1, source_target_pairs={{0,1},{1,0},{2,3},{3,2},{4,5},{5,4},{6,7},{7,6},{8,9},{9,8},{10,11... | collective-permute-start | bytes 2752520 | tf_op jit(solution)/shard_map/ppermute | solution.py:39
  58.5 3.4 %collective-permute-start.7 = (bf16[4,224,512]{2,1,0:T(8,128)(2,1)S(1)}, bf16[4,224,512]{2,1,0:T(8,128)(2,1)S(1)}, u32[]{:S(2)}, u32[]{:S(2)}) collective-permute-start(bf16[4,224,512]{2,1,0:T(8,128)(2,1)S(1)} %collective-permute-done.3.refs_1_), channel_id=1, source_target_pairs={{0,1},{1,0},{2,3},{3,2},{4,5},{5,4},{6,7},{7,6},{8,9},{9,8},{10,11... | collective-permute-start | bytes 2752520 | tf_op jit(solution)/shard_map/ppermute | solution.py:39
  58.5 3.8 %collective-permute-start.8 = (bf16[4,224,512]{2,1,0:T(8,128)(2,1)S(1)}, bf16[4,224,512]{2,1,0:T(8,128)(2,1)S(1)}, u32[]{:S(2)}, u32[]{:S(2)}) collective-permute-start(bf16[4,224,512]{2,1,0:T(8,128)(2,1)S(1)} %collective-permute-done.4.refs_2_), channel_id=1, source_target_pairs={{0,1},{1,0},{2,3},{3,2},{4,5},{5,4},{6,7},{7,6},{8,9},{9,8},{10,11... | collective-permute-start | bytes 2752520 | tf_op jit(solution)/shard_map/ppermute | solution.py:39
  62.3 2.5 %copy-start.2 = (bf16[32,224,152]{2,1,0:T(8,128)(2,1)S(1)}, bf16[32,224,152]{2,1,0:T(8,128)(2,1)}, u32[]{:S(2)}) copy-start(bf16[32,224,152]{2,1,0:T(8,128)(2,1)} %down_weights.2.refs_1_.refs_3_) | copy-start | bytes 6537220
  62.3 3.2 %copy-start.3 = (bf16[32,224,152]{2,1,0:T(8,128)(2,1)S(1)}, bf16[32,224,152]{2,1,0:T(8,128)(2,1)}, u32[]{:S(2)}) copy-start(bf16[32,224,152]{2,1,0:T(8,128)(2,1)} %down_weights.3.refs_0_.refs_2_) | copy-start | bytes 6537220
  67.3 2.6 %collective-permute-start.11 = (bf16[4,224,512]{2,1,0:T(8,128)(2,1)S(1)}, bf16[4,224,512]{2,1,0:T(8,128)(2,1)S(1)}, u32[]{:S(2)}, u32[]{:S(2)}) collective-permute-start(bf16[4,224,512]{2,1,0:T(8,128)(2,1)S(1)} %get-tuple-element.90), channel_id=1, source_target_pairs={{0,1},{1,0},{2,3},{3,2},{4,5},{5,4},{6,7},{7,6},{8,9},{9,8},{10,11... | collective-permute-start | bytes 2752520 | tf_op jit(solution)/shard_map/ppermute | solution.py:39
  69.5 4.4 %collective-permute-start.10 = (bf16[4,224,512]{2,1,0:T(8,128)(2,1)S(1)}, bf16[4,224,512]{2,1,0:T(8,128)(2,1)S(1)}, u32[]{:S(2)}, u32[]{:S(2)}) collective-permute-start(bf16[4,224,512]{2,1,0:T(8,128)(2,1)S(1)} %get-tuple-element.88), channel_id=1, source_target_pairs={{0,1},{1,0},{2,3},{3,2},{4,5},{5,4},{6,7},{7,6},{8,9},{9,8},{10,11... | collective-permute-start | bytes 2752520 | tf_op jit(solution)/shard_map/ppermute | solution.py:39
  72.1 6.9 %collective-permute-start.15 = (bf16[4,224,512]{2,1,0:T(8,128)(2,1)S(1)}, bf16[4,224,512]{2,1,0:T(8,128)(2,1)S(1)}, u32[]{:S(2)}, u32[]{:S(2)}) collective-permute-start(bf16[4,224,512]{2,1,0:T(8,128)(2,1)S(1)} %get-tuple-element.98), channel_id=1, source_target_pairs={{0,1},{1,0},{2,3},{3,2},{4,5},{5,4},{6,7},{7,6},{8,9},{9,8},{10,11... | collective-permute-start | bytes 2752520 | tf_op jit(solution)/shard_map/ppermute | solution.py:39
  72.4 15.0 %collective-permute-start.13 = (bf16[4,224,512]{2,1,0:T(8,128)(2,1)S(1)}, bf16[4,224,512]{2,1,0:T(8,128)(2,1)S(1)}, u32[]{:S(2)}, u32[]{:S(2)}) collective-permute-start(bf16[4,224,512]{2,1,0:T(8,128)(2,1)S(1)} %convert_add_fusion.2), channel_id=1, source_target_pairs={{0,4},{1,17},{2,6},{3,19},{4,0},{5,21},{6,2},{7,23},{8,12},{9,25},... | collective-permute-start | bytes 2752520 | tf_op jit(solution)/shard_map/ppermute | solution.py:337
  76.1 11.2 %collective-permute-start.12 = (bf16[4,224,512]{2,1,0:T(8,128)(2,1)S(1)}, bf16[4,224,512]{2,1,0:T(8,128)(2,1)S(1)}, u32[]{:S(2)}, u32[]{:S(2)}) collective-permute-start(bf16[4,224,512]{2,1,0:T(8,128)(2,1)S(1)} %get-tuple-element.94), channel_id=1, source_target_pairs={{0,1},{1,0},{2,3},{3,2},{4,5},{5,4},{6,7},{7,6},{8,9},{9,8},{10,11... | collective-permute-start | bytes 2752520 | tf_op jit(solution)/shard_map/ppermute | solution.py:39
  76.2 23.4 %collective-permute-start.14 = (bf16[4,224,512]{2,1,0:T(8,128)(2,1)S(1)}, bf16[4,224,512]{2,1,0:T(8,128)(2,1)S(1)}, u32[]{:S(2)}, u32[]{:S(2)}) collective-permute-start(bf16[4,224,512]{2,1,0:T(8,128)(2,1)S(1)} %convert_add_fusion.3), channel_id=1, source_target_pairs={{0,2},{1,9},{2,4},{3,11},{4,6},{5,13},{6,0},{7,15},{8,10},{9,17},{... | collective-permute-start | bytes 2752520 | tf_op jit(solution)/shard_map/ppermute | solution.py:337
  79.4 20.1 %collective-permute-start.16 = (bf16[4,224,512]{2,1,0:T(8,128)(2,1)S(1)}, bf16[4,224,512]{2,1,0:T(8,128)(2,1)S(1)}, u32[]{:S(2)}, u32[]{:S(2)}) collective-permute-start(bf16[4,224,512]{2,1,0:T(8,128)(2,1)S(1)} %convert_add_fusion.1), channel_id=1, source_target_pairs={{0,6},{1,25},{2,0},{3,27},{4,2},{5,29},{6,4},{7,31},{8,14},{9,1},{... | collective-permute-start | bytes 2752520 | tf_op jit(solution)/shard_map/ppermute | solution.py:337
  100.3 26.9 %copy-start.5 = (f32[384,128]{1,0:T(8,128)S(1)}, f32[384,128]{1,0:T(8,128)}, u32[]{:S(2)}) copy-start(f32[384,128]{1,0:T(8,128)} %get-tuple-element.100) | copy-start | bytes 589828
  100.3 7.6 %collective-permute-start.17 = (bf16[224,512]{1,0:T(8,128)(2,1)S(1)}, bf16[224,512]{1,0:T(8,128)(2,1)S(1)}, u32[]{:S(2)}, u32[]{:S(2)}) collective-permute-start(bf16[224,512]{1,0:T(8,128)(2,1)S(1)} %get-tuple-element.103), channel_id=1, source_target_pairs={{0,16},{1,5},{2,18},{3,7},{4,20},{5,1},{6,22},{7,3},{8,24},{9,13},... | collective-permute-start | bytes 688136 | tf_op jit(solution)/shard_map/ppermute | solution.py:334
  101.0 8.7 %collective-permute-start.19 = (bf16[224,512]{1,0:T(8,128)(2,1)S(1)}, bf16[224,512]{1,0:T(8,128)(2,1)S(1)}, u32[]{:S(2)}, u32[]{:S(2)}) collective-permute-start(bf16[224,512]{1,0:T(8,128)(2,1)S(1)} %get-tuple-element.104), channel_id=1, source_target_pairs={{0,24},{1,7},{2,26},{3,1},{4,28},{5,3},{6,30},{7,5},{8,0},{9,15},{... | collective-permute-start | bytes 688136 | tf_op jit(solution)/shard_map/ppermute | solution.py:334
  103.1 7.3 %collective-permute-start.18 = (bf16[224,512]{1,0:T(8,128)(2,1)S(1)}, bf16[224,512]{1,0:T(8,128)(2,1)S(1)}, u32[]{:S(2)}, u32[]{:S(2)}) collective-permute-start(bf16[224,512]{1,0:T(8,128)(2,1)S(1)} %get-tuple-element.105), channel_id=1, source_target_pairs={{0,8},{1,3},{2,10},{3,5},{4,12},{5,7},{6,14},{7,1},{8,16},{9,11},{... | collective-permute-start | bytes 688136 | tf_op jit(solution)/shard_map/ppermute | solution.py:334

commit v3 on v2

--- a/solution.py
+++ b/solution.py
@@ -361,17 +361,31 @@
             before = order[i - 1]
             pieces[before], hidden = lax.optimization_barrier((pieces[before], hidden))
         pieces[outer] = mine + sibling(others).astype(F32)
-    level = pieces[0]
-    for d in order[:-1]:
-        level = level + level_two(pieces[d].astype(BF16), d).astype(F32)
+    def second(parts):
+        level = parts[0]
+        for d in order[:-1]:
+            level = level + level_two(parts[d].astype(BF16), d).astype(F32)
+        return level
+
+    def first(level):
+        return [level_one(level[d].astype(BF16), d) for d in order[:-1]]
+
+    level = second({d: part[:, :, rows:] for d, part in pieces.items()})
+    dense_parts = {d: part[:, :, :rows] for d, part in pieces.items()}
+    level, dense_parts = lax.optimization_barrier((level, dense_parts))
+    arrived = first(level)
+    dense_level = second(dense_parts)
     total = level[0]
-    for d in order[:-1]:
-        total = total + level_one(level[d].astype(BF16), d).astype(F32)
-
-    back = total[:, rows:].astype(BF16).T.reshape(experts, capacity, cols)
+    for part in arrived:
+        total = total + part.astype(F32)
+    back = total.astype(BF16).T.reshape(experts, capacity, cols)
     returned = lax.all_to_all(back, "expert", 0, 0, tiled=True).reshape(experts * capacity, cols)
+    dense_total = dense_level[0]
+    for part in first(dense_level):
+        dense_total = dense_total + part.astype(F32)
+
     moe_out = jnp.dot(combine.T, returned.astype(F32), precision=lax.Precision.HIGHEST)
-    return (total[:, :rows].T + moe_out).astype(BF16)
+    return (dense_total.T + moe_out).astype(BF16)
 
 
 def solution(mesh):

time: 129 us -> 130 us (level)
  blocking collectives: 16.4 us -> 0 us
  starting transfers between devices: 30.2 us -> 41.4 us
  waiting for transfers between devices: 31.1 us -> 36.5 us
    all_to_all x1 -> x0, blocking collectives: 16.4 us -> none  [shards(): lax.all_to_all(back, 'expert', 0, 0, tiled=True)]
    all_to_all x0 -> x1, starting transfers between devices: none -> 6.91 us  [shards(): lax.all_to_all(back, 'expert', 0, 0, tiled=True)]
    all_to_all x0 -> x1, waiting for transfers between devices: none -> 6.87 us  [shards(): lax.all_to_all(back, 'expert', 0, 0, tiled=True)]
    ppermute x6 -> x9, waiting for transfers between devices: 23.1 us -> 20 us  [level_two(): return lax.ppermute(value, 'tensor', hops(d, False))]
    ppermute x6 -> x9, starting transfers between devices: 9.21 us -> 11.9 us  [level_one(): return lax.ppermute(value, 'tensor', hops(d, True))]
    ppermute x6 -> x9, waiting for transfers between devices: 7.21 us -> 8.98 us  [level_one(): return lax.ppermute(value, 'tensor', hops(d, True))]
    ppermute x6 -> x9, starting transfers between devices: 10.8 us -> 12 us  [level_two(): return lax.ppermute(value, 'tensor', hops(d, False))]
    unnamed x12 -> x14, local copies, waits for them, and re-layouts: 5.52 us -> 5.51 us
  transfers between devices with their start and end apart: 21 -> 28, of which waited for: 8 -> 9; matrix products, arithmetic and copies ran while one was open for 1% -> 2% of each run, Pallas kernels for 27% -> 27%
where the time goes in v3:
time: 130 us
  starting transfers between devices  41.4 us (32%)
  Pallas kernels  41.3 us (32%)
  waiting for transfers between devices  36.5 us (28%)
  local copies, waits for them, and re-layouts  6.9 us (5%)
  other arithmetic  2.78 us (2%)
    pallas_call x4, Pallas kernels, layout_call(): pl.pallas_call(functools.partial(kernel, cols), out_shape=jax.ShapeDtypeS...  20.7 us
    ppermute x9, waiting for transfers between devices, level_two(): return lax.ppermute(value, 'tensor', hops(d, False))  20 us
    ppermute x9, starting transfers between devices, level_two(): return lax.ppermute(value, 'tensor', hops(d, False))  12 us
    ppermute x9, starting transfers between devices, level_one(): return lax.ppermute(value, 'tensor', hops(d, True))  11.9 us
    pallas_call x4, Pallas kernels, arrive(): pl.pallas_call(functools.partial(arrive_kernel, dense_rows, count, start,...  11.2 us
    ppermute x9, waiting for transfers between devices, level_one(): return lax.ppermute(value, 'tensor', hops(d, True))  8.98 us
    all_to_all x1, starting transfers between devices, shards(): lax.all_to_all(outgoing.reshape(experts, capacity, cols), 'expert', 0, 0,...  8.47 us
    pallas_call x4, Pallas kernels, down_pieces(): pl.pallas_call(functools.partial(down_kernel, dense_rows), out_shape=(jax...  7.52 us
  transfers between devices with their start and end apart: 28, of which 9 were waited for; matrix products, arithmetic and copies ran while one was open for 2% of the time, Pallas kernels for 27%

profile of v3, /device:TPU:8, one launch (start us, length us, event | category | flops | bytes accessed | tf_op | source)
XLA Modules:
  0.0 129.8 jit_solution(10256520397260783023)
XLA Ops:
  0.0 1.9 %dispatch.1 = (bf16[384,224]{1,0:T(8,128)(2,1)}, f32[384,128]{1,0:T(8,128)}) custom-call(s32[2,128]{1,0:T(2,128)} %bitcast.80, f32[2,128]{1,0:T(2,128)} %bitcast.81, bf16[224,128]{1,0:T(8,128)(2,1)} %bitcast.75), custom_call_target="tpu_custom_call" | custom-call | tf_op jit(solution)/shard_map/dispatch/pallas_call | solution.py:80
  1.9 8.5 %all-to-all-start = ((bf16[8,48,224]{2,1,0:T(8,128)(2,1)}), bf16[8,48,224]{2,1,0:T(8,128)(2,1)S(1)}, u32[]{:S(2)}, u32[]{:S(2)}) async-start(bf16[8,48,224]{2,1,0:T(8,128)(2,1)} %bitcast.77), calls=%async_computation | async-start | bytes 393216 | tf_op jit(solution)/shard_map/all_to_all | solution.py:323
  10.4 5.1 %up_weights.3.refs_2_.refs_4_.refs_5_.refs_6_.refs_7_.refs_8_ = bf16[32,304,224]{2,1,0:T(8,128)(2,1)} custom-call(f32[1,7168]{1,0:T(1,128)} %bitcast.78, bf16[152,7168]{1,0:T(8,128)(2,1)} %bitcast.66, bf16[152,7168]{1,0:T(8,128)(2,1)} %bitcast.67), custom_call_target="tpu_custom_call" | custom-call | flops 1048576 | bytes 1048576 | tf_op jit(solution)/shard_map/up_weights/pallas_call | solution.py:147
  15.4 5.1 %up_weights.2.refs_1_.refs_2_.refs_3_.refs_4_.refs_5_ = bf16[32,304,224]{2,1,0:T(8,128)(2,1)} custom-call(f32[1,7168]{1,0:T(1,128)} %bitcast.79, bf16[152,7168]{1,0:T(8,128)(2,1)} %gate.1, bf16[152,7168]{1,0:T(8,128)(2,1)} %up.1), custom_call_target="tpu_custom_call" | custom-call | flops 1048576 | bytes 1048576 | tf_op jit(solution)/shard_map/up_weights/pallas_call | solution.py:147
  20.5 0.3 all-to-all-done
  20.8 0.1 copy.12
  21.0 3.1 %collective-permute-start.1 = (bf16[224,512]{1,0:T(8,128)(2,1)S(1)}, bf16[224,512]{1,0:T(8,128)(2,1)S(1)}, u32[]{:S(2)}, u32[]{:S(2)}) collective-permute-start(bf16[224,512]{1,0:T(8,128)(2,1)S(1)} %get-tuple-element.120), channel_id=1, source_target_pairs={{0,16},{1,5},{2,18},{3,7},{4,20},{5,1},{6,22},{7,3},{8,24},{9,13},... | collective-permute-start | bytes 688136 | tf_op jit(solution)/shard_map/ppermute | solution.py:334
  24.1 0.6 collective-permute-start
  24.7 2.6 %collective-permute-start.2 = (bf16[224,512]{1,0:T(8,128)(2,1)S(1)}, bf16[224,512]{1,0:T(8,128)(2,1)S(1)}, u32[]{:S(2)}, u32[]{:S(2)}) collective-permute-start(bf16[224,512]{1,0:T(8,128)(2,1)S(1)} %get-tuple-element.120), channel_id=1, source_target_pairs={{0,24},{1,7},{2,26},{3,1},{4,28},{5,3},{6,30},{7,5},{8,0},{9,15},{... | collective-permute-start | bytes 688136 | tf_op jit(solution)/shard_map/ppermute | solution.py:334
  27.4 5.3 %down_weights.2.refs_1_.refs_3_ = bf16[32,224,152]{2,1,0:T(8,128)(2,1)} custom-call(bf16[152,7168]{1,0:T(8,128)(2,1)} %bitcast.68), custom_call_target="tpu_custom_call" | custom-call | flops 1048576 | bytes 1048576 | tf_op jit(solution)/shard_map/down_weights/pallas_call | solution.py:147
  32.7 0.1 pad_maximum_fusion.refs_0_
  32.8 0.1 collective-permute-start.6
  32.9 1.7 %collective-permute-start.5 = (bf16[4,224,512]{2,1,0:T(8,128)(2,1)S(1)}, bf16[4,224,512]{2,1,0:T(8,128)(2,1)}, u32[]{:S(2)}, u32[]{:S(2)}) collective-permute-start(bf16[4,224,512]{2,1,0:T(8,128)(2,1)S(1)} %pad_maximum_fusion.refs_0_), channel_id=1, source_target_pairs={{0,2},{1,9},{2,4},{3,11},{4,6},{5,13},{6,0},{7,15},{8,10},{9,17},{... | collective-permute-start | bytes 2752520 | tf_op jit(solution)/shard_map/ppermute | solution.py:337
  34.6 0.5 collective-permute-start.4
  35.0 2.3 %collective-permute-start.3 = (bf16[4,224,512]{2,1,0:T(8,128)(2,1)S(1)}, bf16[4,224,512]{2,1,0:T(8,128)(2,1)S(1)}, u32[]{:S(2)}, u32[]{:S(2)}) collective-permute-start(bf16[4,224,512]{2,1,0:T(8,128)(2,1)S(1)} %pad_maximum_fusion.refs_0_), channel_id=1, source_target_pairs={{0,4},{1,17},{2,6},{3,19},{4,0},{5,21},{6,2},{7,23},{8,12},{9,25},... | collective-permute-start | bytes 2752520 | tf_op jit(solution)/shard_map/ppermute | solution.py:337
  37.3 5.3 %down_weights.3.refs_0_.refs_2_ = bf16[32,224,152]{2,1,0:T(8,128)(2,1)} custom-call(bf16[152,7168]{1,0:T(8,128)(2,1)} %down.1), custom_call_target="tpu_custom_call" | custom-call | flops 1048576 | bytes 1048576 | tf_op jit(solution)/shard_map/down_weights/pallas_call | solution.py:147
  42.6 0.1 pad_add_fusion.place
  42.7 2.4 %copy-done = bf16[32,304,224]{2,1,0:T(8,128)(2,1)S(1)} copy-done((bf16[32,304,224]{2,1,0:T(8,128)(2,1)S(1)}, bf16[32,304,224]{2,1,0:T(8,128)(2,1)}, u32[]{:S(2)}) %copy-start) | copy-done | bytes 4358168
  45.1 2.4 %copy-done.1 = bf16[32,304,224]{2,1,0:T(8,128)(2,1)S(1)} copy-done((bf16[32,304,224]{2,1,0:T(8,128)(2,1)S(1)}, bf16[32,304,224]{2,1,0:T(8,128)(2,1)}, u32[]{:S(2)}) %copy-start.1) | copy-done | bytes 4358168
  47.5 1.8 %arrive_0_1.1 = (f32[304,128]{1,0:T(8,128)S(1)}, f32[304,384]{1,0:T(8,128)S(1)}, f32[8,512]{1,0:T(8,128)S(1)}) custom-call(s32[3]{0:T(128)S(1)} %pad_add_fusion.place, bf16[4,224,512]{2,1,0:T(8,128)(2,1)S(1)} %pad_maximum_fusion.refs_0_, bf16[32,304,224]{2,1,0:T(8,128)(2,1)S(1)} %copy-done.1, bf16[32,304,224]{2,1,0:T(8,128)(2,1)S(1)} %copy-done), custom_call_target="tpu_custom_call" | custom-call | flops 1048576 | bytes 1048576 | tf_op jit(solution)/shard_map/arrive_0_1/pallas_call | solution.py:236
  49.4 0.1 collective-permute-start.9
  49.5 4.0 %arrive_1_2.1 = (f32[304,128]{1,0:T(8,128)S(1)}, f32[304,384]{1,0:T(8,128)S(1)}, f32[8,512]{1,0:T(8,128)S(1)}) custom-call(s32[3]{0:T(128)S(1)} %pad_add_fusion.place, bf16[4,224,512]{2,1,0:T(8,128)(2,1)} %collective-permute-done.6.refs_0_, bf16[4,224,512]{2,1,0:T(8,128)(2,1)} %collective-permute-done.5.refs_1_, bf16[32,304,224]{2,1,0:T(8,128)(2,1)S(1)} %copy-done.1, ...), custom_call_target="tpu_custom_call" | custom-call | flops 1048576 | bytes 1048576 | tf_op jit(solution)/shard_map/arrive_1_2/pallas_call | solution.py:236
  53.5 5.0 %collective-permute-done.3.refs_1_ = bf16[4,224,512]{2,1,0:T(8,128)(2,1)S(1)} collective-permute-done((bf16[4,224,512]{2,1,0:T(8,128)(2,1)S(1)}, bf16[4,224,512]{2,1,0:T(8,128)(2,1)S(1)}, u32[]{:S(2)}, u32[]{:S(2)}) %collective-permute-start.3) | collective-permute-done | bytes 917536 | tf_op jit(solution)/shard_map/ppermute | solution.py:337
  58.5 0.5 collective-permute-start.8
  59.1 2.9 %arrive_3_3.1 = (f32[304,128]{1,0:T(8,128)S(1)}, f32[304,384]{1,0:T(8,128)S(1)}, f32[8,512]{1,0:T(8,128)S(1)}) custom-call(s32[3]{0:T(128)S(1)} %pad_add_fusion.place, bf16[4,224,512]{2,1,0:T(8,128)(2,1)S(1)} %collective-permute-done.9.refs_0_, bf16[4,224,512]{2,1,0:T(8,128)(2,1)S(1)} %collective-permute-done.3.refs_1_, ...), custom_call_target="tpu_custom_call" | custom-call | flops 1048576 | bytes 1048576 | tf_op jit(solution)/shard_map/arrive_3_3/pallas_call | solution.py:236
  62.0 0.4 collective-permute-done.8.refs_1_
  62.3 2.5 %arrive_3_2.1.hidden = bf16[152,512]{1,0:T(8,128)(2,1)S(1)} custom-call(s32[3]{0:T(128)S(1)} %pad_add_fusion.place, bf16[4,224,512]{2,1,0:T(8,128)(2,1)S(1)} %collective-permute-done.7.refs_0_, bf16[4,224,512]{2,1,0:T(8,128)(2,1)S(1)} %collective-permute-done.8.refs_1_, bf16[32,304,224]{2,1,0:T(8,128)(2,1)S(1)} %copy-done.1, ...), custom_call_target="tpu_custom_call" | custom-call | flops 1048576 | bytes 1048576 | tf_op jit(solution)/shard_map/arrive_3_2/pallas_call | solution.py:236
  64.8 0.7 copy-done.3
  65.5 1.9 %down_pieces_2.1 = (f32[4,224,512]{2,1,0:T(8,128)S(1)}, bf16[4,224,512]{2,1,0:T(8,128)(2,1)S(1)}) custom-call(s32[3]{0:T(128)S(1)} %pad_add_fusion.place, bf16[152,512]{1,0:T(8,128)(2,1)S(1)} %arrive_3_2.1.hidden, bf16[32,224,152]{2,1,0:T(8,128)(2,1)S(1)} %copy-done.3, bf16[32,224,152]{2,1,0:T(8,128)(2,1)S(1)} %copy-done.2, ...), custom_call_target="tpu_custom_call" | custom-call | flops 1048576 | bytes 1048576 | tf_op jit(solution)/shard_map/down_pieces_2/pallas_call | solution.py:284
  67.4 0.2 collective-permute-start.11
  67.6 1.9 %down_pieces_1.1 = (f32[4,224,512]{2,1,0:T(8,128)S(1)}, bf16[4,224,512]{2,1,0:T(8,128)(2,1)S(1)}) custom-call(s32[3]{0:T(128)S(1)} %pad_add_fusion.place, bf16[152,512]{1,0:T(8,128)(2,1)S(1)} %arrive_3_2.1.hidden, bf16[32,224,152]{2,1,0:T(8,128)(2,1)S(1)} %copy-done.3, bf16[32,224,152]{2,1,0:T(8,128)(2,1)S(1)} %copy-done.2, ...), custom_call_target="tpu_custom_call" | custom-call | flops 1048576 | bytes 1048576 | tf_op jit(solution)/shard_map/down_pieces_1/pallas_call | solution.py:284
  69.5 0.5 collective-permute-start.10
  69.9 0.3 convert_add_fusion.2
  70.3 1.9 %down_pieces_3.1 = (f32[4,224,512]{2,1,0:T(8,128)S(1)}, bf16[4,224,512]{2,1,0:T(8,128)(2,1)S(1)}) custom-call(s32[3]{0:T(128)S(1)} %pad_add_fusion.place, bf16[152,512]{1,0:T(8,128)(2,1)S(1)} %arrive_3_2.1.hidden, bf16[32,224,152]{2,1,0:T(8,128)(2,1)S(1)} %copy-done.3, bf16[32,224,152]{2,1,0:T(8,128)(2,1)S(1)} %copy-done.2, ...), custom_call_target="tpu_custom_call" | custom-call | flops 1048576 | bytes 1048576 | tf_op jit(solution)/shard_map/down_pieces_3/pallas_call | solution.py:284
  72.2 0.2 collective-permute-start.15
  72.4 0.3 convert_add_fusion.3
  72.7 1.9 %down_pieces_0.1 = (f32[4,224,512]{2,1,0:T(8,128)S(1)}, bf16[4,224,512]{2,1,0:T(8,128)(2,1)S(1)}) custom-call(s32[3]{0:T(128)S(1)} %pad_add_fusion.place, bf16[152,512]{1,0:T(8,128)(2,1)S(1)} %arrive_3_2.1.hidden, bf16[32,224,152]{2,1,0:T(8,128)(2,1)S(1)} %copy-done.3, bf16[32,224,152]{2,1,0:T(8,128)(2,1)S(1)} %copy-done.2, ...), custom_call_target="tpu_custom_call" | custom-call | flops 1048576 | bytes 1048576 | tf_op jit(solution)/shard_map/down_pieces_0/pallas_call | solution.py:284
  74.6 0.5 collective-permute-start.12
  75.1 1.6 %collective-permute-start.13 = (bf16[4,224,384]{2,1,0:T(8,128)(2,1)S(1)}, bf16[4,224,384]{2,1,0:T(8,128)(2,1)S(1)}, u32[]{:S(2)}, u32[]{:S(2)}) collective-permute-start(bf16[4,224,384]{2,1,0:T(8,128)(2,1)S(1)} %slice.117), channel_id=1, source_target_pairs={{0,4},{1,17},{2,6},{3,19},{4,0},{5,21},{6,2},{7,23},{8,12},{9,25},... | collective-permute-start | bytes 2064392 | tf_op jit(solution)/shard_map/ppermute | solution.py:337
  76.8 2.5 %collective-permute-start.14 = (bf16[4,224,384]{2,1,0:T(8,128)(2,1)S(1)}, bf16[4,224,384]{2,1,0:T(8,128)(2,1)S(1)}, u32[]{:S(2)}, u32[]{:S(2)}) collective-permute-start(bf16[4,224,384]{2,1,0:T(8,128)(2,1)S(1)} %slice.116), channel_id=1, source_target_pairs={{0,2},{1,9},{2,4},{3,11},{4,6},{5,13},{6,0},{7,15},{8,10},{9,17},{... | collective-permute-start | bytes 2064392 | tf_op jit(solution)/shard_map/ppermute | solution.py:337
  79.3 0.3 convert_add_fusion
  79.7 2.1 %collective-permute-start.16 = (bf16[4,224,384]{2,1,0:T(8,128)(2,1)S(1)}, bf16[4,224,384]{2,1,0:T(8,128)(2,1)S(1)}, u32[]{:S(2)}, u32[]{:S(2)}) collective-permute-start(bf16[4,224,384]{2,1,0:T(8,128)(2,1)S(1)} %slice.115), channel_id=1, source_target_pairs={{0,6},{1,25},{2,0},{3,27},{4,2},{5,29},{6,4},{7,31},{8,14},{9,1},{... | collective-permute-start | bytes 2064392 | tf_op jit(solution)/shard_map/ppermute | solution.py:337
  82.0 0.3 convert_add_fusion.1
  82.3 5.4 %collective-permute-done.13 = bf16[4,224,384]{2,1,0:T(8,128)(2,1)S(1)} collective-permute-done((bf16[4,224,384]{2,1,0:T(8,128)(2,1)S(1)}, bf16[4,224,384]{2,1,0:T(8,128)(2,1)S(1)}, u32[]{:S(2)}, u32[]{:S(2)}) %collective-permute-start.13) | collective-permute-done | bytes 688160 | tf_op jit(solution)/shard_map/ppermute | solution.py:337
  87.8 9.5 %collective-permute-done.14 = bf16[4,224,384]{2,1,0:T(8,128)(2,1)S(1)} collective-permute-done((bf16[4,224,384]{2,1,0:T(8,128)(2,1)S(1)}, bf16[4,224,384]{2,1,0:T(8,128)(2,1)S(1)}, u32[]{:S(2)}, u32[]{:S(2)}) %collective-permute-start.14) | collective-permute-done | bytes 688160 | tf_op jit(solution)/shard_map/ppermute | solution.py:337
  97.3 0.3 fusion.1
  97.7 0.1 convert.23
  97.8 0.6 collective-permute-start.23
  98.4 2.1 %collective-permute-start.25 = (bf16[224,384]{1,0:T(8,128)(2,1)S(1)}, bf16[224,384]{1,0:T(8,128)(2,1)S(1)}, u32[]{:S(2)}, u32[]{:S(2)}) collective-permute-start(bf16[224,384]{1,0:T(8,128)(2,1)S(1)} %get-tuple-element.114), channel_id=1, source_target_pairs={{0,24},{1,7},{2,26},{3,1},{4,28},{5,3},{6,30},{7,5},{8,0},{9,15},{... | collective-permute-start | bytes 516104 | tf_op jit(solution)/shard_map/ppermute | solution.py:334
  100.5 0.1 collective-permute-start.24
  100.7 1.4 %collective-permute-start.18 = (bf16[4,224,128]{2,1,0:T(8,128)(2,1)S(1)}, bf16[4,224,128]{2,1,0:T(8,128)(2,1)S(1)}, u32[]{:S(2)}, u32[]{:S(2)}) collective-permute-start(bf16[4,224,128]{2,1,0:T(8,128)(2,1)S(1)} %slice.62), channel_id=1, source_target_pairs={{0,2},{1,9},{2,4},{3,11},{4,6},{5,13},{6,0},{7,15},{8,10},{9,17},{... | collective-permute-start | bytes 688136 | tf_op jit(solution)/shard_map/ppermute | solution.py:337
  102.1 3.5 %collective-permute-done.23 = bf16[224,384]{1,0:T(8,128)(2,1)S(1)} collective-permute-done((bf16[224,384]{1,0:T(8,128)(2,1)S(1)}, bf16[224,384]{1,0:T(8,128)(2,1)S(1)}, u32[]{:S(2)}, u32[]{:S(2)}) %collective-permute-start.23) | collective-permute-done | bytes 172064 | tf_op jit(solution)/shard_map/ppermute | solution.py:334
  105.5 3.5 %collective-permute-done.25 = bf16[224,384]{1,0:T(8,128)(2,1)S(1)} collective-permute-done((bf16[224,384]{1,0:T(8,128)(2,1)S(1)}, bf16[224,384]{1,0:T(8,128)(2,1)S(1)}, u32[]{:S(2)}, u32[]{:S(2)}) %collective-permute-start.25) | collective-permute-done | bytes 172064 | tf_op jit(solution)/shard_map/ppermute | solution.py:334
  109.1 2.0 %collective-permute-done.24 = bf16[224,384]{1,0:T(8,128)(2,1)S(1)} collective-permute-done((bf16[224,384]{1,0:T(8,128)(2,1)S(1)}, bf16[224,384]{1,0:T(8,128)(2,1)S(1)}, u32[]{:S(2)}, u32[]{:S(2)}) %collective-permute-start.24) | collective-permute-done | bytes 172064 | tf_op jit(solution)/shard_map/ppermute | solution.py:334
  111.1 0.1 fusion.5
  111.1 0.8 copy.13
  112.0 6.9 %all-to-all-start.1 = ((bf16[8,48,224]{2,1,0:T(8,128)(2,1)}), bf16[8,48,224]{2,1,0:T(8,128)(2,1)S(1)}, u32[]{:S(2)}, u32[]{:S(2)}) async-start(bf16[8,48,224]{2,1,0:T(8,128)(2,1)} %bitcast.27), calls=%async_computation.1 | async-start | bytes 393216 | tf_op jit(solution)/shard_map/all_to_all | solution.py:382
  118.9 0.1 fusion.13
  119.1 0.7 collective-permute-start.20
  119.8 1.8 %collective-permute-start.22 = (bf16[224,128]{1,0:T(8,128)(2,1)S(1)}, bf16[224,128]{1,0:T(8,128)(2,1)S(1)}, u32[]{:S(2)}, u32[]{:S(2)}) collective-permute-start(bf16[224,128]{1,0:T(8,128)(2,1)S(1)} %get-tuple-element.117), channel_id=1, source_target_pairs={{0,24},{1,7},{2,26},{3,1},{4,28},{5,3},{6,30},{7,5},{8,0},{9,15},{... | collective-permute-start | bytes 172040 | tf_op jit(solution)/shard_map/ppermute | solution.py:334
  121.6 0.2 collective-permute-start.21
  121.8 6.9 %all-to-all-done.1 = bf16[8,48,224]{2,1,0:T(8,128)(2,1)S(1)} async-done(((bf16[8,48,224]{2,1,0:T(8,128)(2,1)}), bf16[8,48,224]{2,1,0:T(8,128)(2,1)S(1)}, u32[]{:S(2)}, u32[]{:S(2)}) %all-to-all-start.1) | async-done | bytes 172064 | tf_op jit(solution)/shard_map/all_to_all | solution.py:382
  128.7 0.4 fusion.14
  129.1 0.7 fusion.11
  (44 shorter events, 0.5 us)
Async XLA Ops:
  1.9 18.9 %all-to-all-start = ((bf16[8,48,224]{2,1,0:T(8,128)(2,1)}), bf16[8,48,224]{2,1,0:T(8,128)(2,1)S(1)}, u32[]{:S(2)}, u32[]{:S(2)}) async-start(bf16[8,48,224]{2,1,0:T(8,128)(2,1)} %bitcast.77), calls=%async_computation | async-start | bytes 393216 | tf_op jit(solution)/shard_map/all_to_all | solution.py:323
  15.4 5.6 %copy-start.5 = (bf16[128,224]{0,1:T(8,128)(2,1)S(1)}, bf16[128,224]{0,1:T(8,128)(2,1)}, u32[]{:S(2)}) copy-start(bf16[128,224]{0,1:T(8,128)(2,1)} %param.10) | copy-start | bytes 172036
  21.0 11.7 %collective-permute-start.1 = (bf16[224,512]{1,0:T(8,128)(2,1)S(1)}, bf16[224,512]{1,0:T(8,128)(2,1)S(1)}, u32[]{:S(2)}, u32[]{:S(2)}) collective-permute-start(bf16[224,512]{1,0:T(8,128)(2,1)S(1)} %get-tuple-element.120), channel_id=1, source_target_pairs={{0,16},{1,5},{2,18},{3,7},{4,20},{5,1},{6,22},{7,3},{8,24},{9,13},... | collective-permute-start | bytes 688136 | tf_op jit(solution)/shard_map/ppermute | solution.py:334
  24.1 8.6 %collective-permute-start = (bf16[224,512]{1,0:T(8,128)(2,1)S(1)}, bf16[224,512]{1,0:T(8,128)(2,1)S(1)}, u32[]{:S(2)}, u32[]{:S(2)}) collective-permute-start(bf16[224,512]{1,0:T(8,128)(2,1)S(1)} %get-tuple-element.120), channel_id=1, source_target_pairs={{0,8},{1,3},{2,10},{3,5},{4,12},{5,7},{6,14},{7,1},{8,16},{9,11},{... | collective-permute-start | bytes 688136 | tf_op jit(solution)/shard_map/ppermute | solution.py:334
  24.7 8.0 %collective-permute-start.2 = (bf16[224,512]{1,0:T(8,128)(2,1)S(1)}, bf16[224,512]{1,0:T(8,128)(2,1)S(1)}, u32[]{:S(2)}, u32[]{:S(2)}) collective-permute-start(bf16[224,512]{1,0:T(8,128)(2,1)S(1)} %get-tuple-element.120), channel_id=1, source_target_pairs={{0,24},{1,7},{2,26},{3,1},{4,28},{5,3},{6,30},{7,5},{8,0},{9,15},{... | collective-permute-start | bytes 688136 | tf_op jit(solution)/shard_map/ppermute | solution.py:334
  32.8 16.5 %collective-permute-start.6 = (bf16[4,224,512]{2,1,0:T(8,128)(2,1)S(1)}, bf16[4,224,512]{2,1,0:T(8,128)(2,1)}, u32[]{:S(2)}, u32[]{:S(2)}) collective-permute-start(bf16[4,224,512]{2,1,0:T(8,128)(2,1)S(1)} %pad_maximum_fusion.refs_0_), channel_id=1, source_target_pairs={{0,1},{1,0},{2,3},{3,2},{4,5},{5,4},{6,7},{7,6},{8,9},{9,8},{10,11... | collective-permute-start | bytes 2752520 | tf_op jit(solution)/shard_map/ppermute | solution.py:39
  32.9 16.4 %collective-permute-start.5 = (bf16[4,224,512]{2,1,0:T(8,128)(2,1)S(1)}, bf16[4,224,512]{2,1,0:T(8,128)(2,1)}, u32[]{:S(2)}, u32[]{:S(2)}) collective-permute-start(bf16[4,224,512]{2,1,0:T(8,128)(2,1)S(1)} %pad_maximum_fusion.refs_0_), channel_id=1, source_target_pairs={{0,2},{1,9},{2,4},{3,11},{4,6},{5,13},{6,0},{7,15},{8,10},{9,17},{... | collective-permute-start | bytes 2752520 | tf_op jit(solution)/shard_map/ppermute | solution.py:337
  34.6 18.9 %collective-permute-start.4 = (bf16[4,224,512]{2,1,0:T(8,128)(2,1)S(1)}, bf16[4,224,512]{2,1,0:T(8,128)(2,1)S(1)}, u32[]{:S(2)}, u32[]{:S(2)}) collective-permute-start(bf16[4,224,512]{2,1,0:T(8,128)(2,1)S(1)} %pad_maximum_fusion.refs_0_), channel_id=1, source_target_pairs={{0,6},{1,25},{2,0},{3,27},{4,2},{5,29},{6,4},{7,31},{8,14},{9,1},{... | collective-permute-start | bytes 2752520 | tf_op jit(solution)/shard_map/ppermute | solution.py:337
  35.0 23.5 %collective-permute-start.3 = (bf16[4,224,512]{2,1,0:T(8,128)(2,1)S(1)}, bf16[4,224,512]{2,1,0:T(8,128)(2,1)S(1)}, u32[]{:S(2)}, u32[]{:S(2)}) collective-permute-start(bf16[4,224,512]{2,1,0:T(8,128)(2,1)S(1)} %pad_maximum_fusion.refs_0_), channel_id=1, source_target_pairs={{0,4},{1,17},{2,6},{3,19},{4,0},{5,21},{6,2},{7,23},{8,12},{9,25},... | collective-permute-start | bytes 2752520 | tf_op jit(solution)/shard_map/ppermute | solution.py:337
  42.7 2.4 %copy-start = (bf16[32,304,224]{2,1,0:T(8,128)(2,1)S(1)}, bf16[32,304,224]{2,1,0:T(8,128)(2,1)}, u32[]{:S(2)}) copy-start(bf16[32,304,224]{2,1,0:T(8,128)(2,1)} %up_weights.3.refs_2_.refs_4_.refs_5_.refs_6_.refs_7_.refs_8_) | copy-start | bytes 13074436
  45.1 2.4 %copy-start.1 = (bf16[32,304,224]{2,1,0:T(8,128)(2,1)S(1)}, bf16[32,304,224]{2,1,0:T(8,128)(2,1)}, u32[]{:S(2)}) copy-start(bf16[32,304,224]{2,1,0:T(8,128)(2,1)} %up_weights.2.refs_1_.refs_2_.refs_3_.refs_4_.refs_5_) | copy-start | bytes 13074436
  49.4 9.7 %collective-permute-start.9 = (bf16[4,224,512]{2,1,0:T(8,128)(2,1)}, bf16[4,224,512]{2,1,0:T(8,128)(2,1)S(1)}, u32[]{:S(2)}, u32[]{:S(2)}) collective-permute-start(bf16[4,224,512]{2,1,0:T(8,128)(2,1)} %collective-permute-done.5.refs_1_), channel_id=1, source_target_pairs={{0,1},{1,0},{2,3},{3,2},{4,5},{5,4},{6,7},{7,6},{8,9},{9,8},{10,11... | collective-permute-start | bytes 2752520 | tf_op jit(solution)/shard_map/ppermute | solution.py:39
  58.5 3.4 %collective-permute-start.7 = (bf16[4,224,512]{2,1,0:T(8,128)(2,1)S(1)}, bf16[4,224,512]{2,1,0:T(8,128)(2,1)S(1)}, u32[]{:S(2)}, u32[]{:S(2)}) collective-permute-start(bf16[4,224,512]{2,1,0:T(8,128)(2,1)S(1)} %collective-permute-done.3.refs_1_), channel_id=1, source_target_pairs={{0,1},{1,0},{2,3},{3,2},{4,5},{5,4},{6,7},{7,6},{8,9},{9,8},{10,11... | collective-permute-start | bytes 2752520 | tf_op jit(solution)/shard_map/ppermute | solution.py:39
  58.5 3.8 %collective-permute-start.8 = (bf16[4,224,512]{2,1,0:T(8,128)(2,1)S(1)}, bf16[4,224,512]{2,1,0:T(8,128)(2,1)S(1)}, u32[]{:S(2)}, u32[]{:S(2)}) collective-permute-start(bf16[4,224,512]{2,1,0:T(8,128)(2,1)S(1)} %collective-permute-done.4.refs_2_), channel_id=1, source_target_pairs={{0,1},{1,0},{2,3},{3,2},{4,5},{5,4},{6,7},{7,6},{8,9},{9,8},{10,11... | collective-permute-start | bytes 2752520 | tf_op jit(solution)/shard_map/ppermute | solution.py:39
  62.3 2.5 %copy-start.2 = (bf16[32,224,152]{2,1,0:T(8,128)(2,1)S(1)}, bf16[32,224,152]{2,1,0:T(8,128)(2,1)}, u32[]{:S(2)}) copy-start(bf16[32,224,152]{2,1,0:T(8,128)(2,1)} %down_weights.2.refs_1_.refs_3_) | copy-start | bytes 6537220
  62.3 3.2 %copy-start.3 = (bf16[32,224,152]{2,1,0:T(8,128)(2,1)S(1)}, bf16[32,224,152]{2,1,0:T(8,128)(2,1)}, u32[]{:S(2)}) copy-start(bf16[32,224,152]{2,1,0:T(8,128)(2,1)} %down_weights.3.refs_0_.refs_2_) | copy-start | bytes 6537220
  67.4 2.6 %collective-permute-start.11 = (bf16[4,224,512]{2,1,0:T(8,128)(2,1)S(1)}, bf16[4,224,512]{2,1,0:T(8,128)(2,1)S(1)}, u32[]{:S(2)}, u32[]{:S(2)}) collective-permute-start(bf16[4,224,512]{2,1,0:T(8,128)(2,1)S(1)} %get-tuple-element.95), channel_id=1, source_target_pairs={{0,1},{1,0},{2,3},{3,2},{4,5},{5,4},{6,7},{7,6},{8,9},{9,8},{10,11... | collective-permute-start | bytes 2752520 | tf_op jit(solution)/shard_map/ppermute | solution.py:39
  69.5 2.9 %collective-permute-start.10 = (bf16[4,224,512]{2,1,0:T(8,128)(2,1)S(1)}, bf16[4,224,512]{2,1,0:T(8,128)(2,1)S(1)}, u32[]{:S(2)}, u32[]{:S(2)}) collective-permute-start(bf16[4,224,512]{2,1,0:T(8,128)(2,1)S(1)} %get-tuple-element.93), channel_id=1, source_target_pairs={{0,1},{1,0},{2,3},{3,2},{4,5},{5,4},{6,7},{7,6},{8,9},{9,8},{10,11... | collective-permute-start | bytes 2752520 | tf_op jit(solution)/shard_map/ppermute | solution.py:39
  72.2 7.1 %collective-permute-start.15 = (bf16[4,224,512]{2,1,0:T(8,128)(2,1)S(1)}, bf16[4,224,512]{2,1,0:T(8,128)(2,1)S(1)}, u32[]{:S(2)}, u32[]{:S(2)}) collective-permute-start(bf16[4,224,512]{2,1,0:T(8,128)(2,1)S(1)} %get-tuple-element.103), channel_id=1, source_target_pairs={{0,1},{1,0},{2,3},{3,2},{4,5},{5,4},{6,7},{7,6},{8,9},{9,8},{10,11... | collective-permute-start | bytes 2752520 | tf_op jit(solution)/shard_map/ppermute | solution.py:39
  74.6 7.4 %collective-permute-start.12 = (bf16[4,224,512]{2,1,0:T(8,128)(2,1)S(1)}, bf16[4,224,512]{2,1,0:T(8,128)(2,1)S(1)}, u32[]{:S(2)}, u32[]{:S(2)}) collective-permute-start(bf16[4,224,512]{2,1,0:T(8,128)(2,1)S(1)} %get-tuple-element.99), channel_id=1, source_target_pairs={{0,1},{1,0},{2,3},{3,2},{4,5},{5,4},{6,7},{7,6},{8,9},{9,8},{10,11... | collective-permute-start | bytes 2752520 | tf_op jit(solution)/shard_map/ppermute | solution.py:39
  75.1 12.6 %collective-permute-start.13 = (bf16[4,224,384]{2,1,0:T(8,128)(2,1)S(1)}, bf16[4,224,384]{2,1,0:T(8,128)(2,1)S(1)}, u32[]{:S(2)}, u32[]{:S(2)}) collective-permute-start(bf16[4,224,384]{2,1,0:T(8,128)(2,1)S(1)} %slice.117), channel_id=1, source_target_pairs={{0,4},{1,17},{2,6},{3,19},{4,0},{5,21},{6,2},{7,23},{8,12},{9,25},... | collective-permute-start | bytes 2064392 | tf_op jit(solution)/shard_map/ppermute | solution.py:337
  76.8 20.5 %collective-permute-start.14 = (bf16[4,224,384]{2,1,0:T(8,128)(2,1)S(1)}, bf16[4,224,384]{2,1,0:T(8,128)(2,1)S(1)}, u32[]{:S(2)}, u32[]{:S(2)}) collective-permute-start(bf16[4,224,384]{2,1,0:T(8,128)(2,1)S(1)} %slice.116), channel_id=1, source_target_pairs={{0,2},{1,9},{2,4},{3,11},{4,6},{5,13},{6,0},{7,15},{8,10},{9,17},{... | collective-permute-start | bytes 2064392 | tf_op jit(solution)/shard_map/ppermute | solution.py:337
  79.7 17.6 %collective-permute-start.16 = (bf16[4,224,384]{2,1,0:T(8,128)(2,1)S(1)}, bf16[4,224,384]{2,1,0:T(8,128)(2,1)S(1)}, u32[]{:S(2)}, u32[]{:S(2)}) collective-permute-start(bf16[4,224,384]{2,1,0:T(8,128)(2,1)S(1)} %slice.115), channel_id=1, source_target_pairs={{0,6},{1,25},{2,0},{3,27},{4,2},{5,29},{6,4},{7,31},{8,14},{9,1},{... | collective-permute-start | bytes 2064392 | tf_op jit(solution)/shard_map/ppermute | solution.py:337
  82.3 15.3 %copy-start.4 = (f32[4,224,512]{2,1,0:T(8,128)}, f32[4,224,512]{2,1,0:T(8,128)S(1)}, u32[]{:S(2)}) copy-start(f32[4,224,512]{2,1,0:T(8,128)S(1)} %convert_add_fusion.1) | copy-start | bytes 5505028
  97.7 21.2 %slice-start = ((f32[4,224,512]{2,1,0:T(8,128)}), f32[4,224,128]{2,1,0:T(8,128)S(1)}, s32[]{:S(2)}) async-start(f32[4,224,512]{2,1,0:T(8,128)} %copy-done.4), calls=%async_computation.2 | async-start | bytes 917504 | tf_op jit(solution)/shard_map/slice | solution.py:374
  97.8 7.7 %collective-permute-start.23 = (bf16[224,384]{1,0:T(8,128)(2,1)S(1)}, bf16[224,384]{1,0:T(8,128)(2,1)S(1)}, u32[]{:S(2)}, u32[]{:S(2)}) collective-permute-start(bf16[224,384]{1,0:T(8,128)(2,1)S(1)} %get-tuple-element.113), channel_id=1, source_target_pairs={{0,16},{1,5},{2,18},{3,7},{4,20},{5,1},{6,22},{7,3},{8,24},{9,13},... | collective-permute-start | bytes 516104 | tf_op jit(solution)/shard_map/ppermute | solution.py:334
  98.4 10.6 %collective-permute-start.25 = (bf16[224,384]{1,0:T(8,128)(2,1)S(1)}, bf16[224,384]{1,0:T(8,128)(2,1)S(1)}, u32[]{:S(2)}, u32[]{:S(2)}) collective-permute-start(bf16[224,384]{1,0:T(8,128)(2,1)S(1)} %get-tuple-element.114), channel_id=1, source_target_pairs={{0,24},{1,7},{2,26},{3,1},{4,28},{5,3},{6,30},{7,5},{8,0},{9,15},{... | collective-permute-start | bytes 516104 | tf_op jit(solution)/shard_map/ppermute | solution.py:334
  100.5 28.1 %copy-start.6 = (f32[384,128]{1,0:T(8,128)S(1)}, f32[384,128]{1,0:T(8,128)}, u32[]{:S(2)}) copy-start(f32[384,128]{1,0:T(8,128)} %get-tuple-element.109) | copy-start | bytes 589828
  100.5 10.5 %collective-permute-start.24 = (bf16[224,384]{1,0:T(8,128)(2,1)S(1)}, bf16[224,384]{1,0:T(8,128)(2,1)S(1)}, u32[]{:S(2)}, u32[]{:S(2)}) collective-permute-start(bf16[224,384]{1,0:T(8,128)(2,1)S(1)} %get-tuple-element.115), channel_id=1, source_target_pairs={{0,8},{1,3},{2,10},{3,5},{4,12},{5,7},{6,14},{7,1},{8,16},{9,11},{... | collective-permute-start | bytes 516104 | tf_op jit(solution)/shard_map/ppermute | solution.py:334
  100.7 18.2 %collective-permute-start.17 = (bf16[4,224,128]{2,1,0:T(8,128)(2,1)S(1)}, bf16[4,224,128]{2,1,0:T(8,128)(2,1)S(1)}, u32[]{:S(2)}, u32[]{:S(2)}) collective-permute-start(bf16[4,224,128]{2,1,0:T(8,128)(2,1)S(1)} %slice.63), channel_id=1, source_target_pairs={{0,4},{1,17},{2,6},{3,19},{4,0},{5,21},{6,2},{7,23},{8,12},{9,25},... | collective-permute-start | bytes 688136 | tf_op jit(solution)/shard_map/ppermute | solution.py:337
  100.7 18.2 %collective-permute-start.18 = (bf16[4,224,128]{2,1,0:T(8,128)(2,1)S(1)}, bf16[4,224,128]{2,1,0:T(8,128)(2,1)S(1)}, u32[]{:S(2)}, u32[]{:S(2)}) collective-permute-start(bf16[4,224,128]{2,1,0:T(8,128)(2,1)S(1)} %slice.62), channel_id=1, source_target_pairs={{0,2},{1,9},{2,4},{3,11},{4,6},{5,13},{6,0},{7,15},{8,10},{9,17},{... | collective-permute-start | bytes 688136 | tf_op jit(solution)/shard_map/ppermute | solution.py:337
  105.5 13.4 %collective-permute-start.19 = (bf16[4,224,128]{2,1,0:T(8,128)(2,1)S(1)}, bf16[4,224,128]{2,1,0:T(8,128)(2,1)S(1)}, u32[]{:S(2)}, u32[]{:S(2)}) collective-permute-start(bf16[4,224,128]{2,1,0:T(8,128)(2,1)S(1)} %slice.64), channel_id=1, source_target_pairs={{0,6},{1,25},{2,0},{3,27},{4,2},{5,29},{6,4},{7,31},{8,14},{9,1},{... | collective-permute-start | bytes 688136 | tf_op jit(solution)/shard_map/ppermute | solution.py:337
  112.0 16.7 %all-to-all-start.1 = ((bf16[8,48,224]{2,1,0:T(8,128)(2,1)}), bf16[8,48,224]{2,1,0:T(8,128)(2,1)S(1)}, u32[]{:S(2)}, u32[]{:S(2)}) async-start(bf16[8,48,224]{2,1,0:T(8,128)(2,1)} %bitcast.27), calls=%async_computation.1 | async-start | bytes 393216 | tf_op jit(solution)/shard_map/all_to_all | solution.py:382
  119.1 10.0 %collective-permute-start.20 = (bf16[224,128]{1,0:T(8,128)(2,1)S(1)}, bf16[224,128]{1,0:T(8,128)(2,1)S(1)}, u32[]{:S(2)}, u32[]{:S(2)}) collective-permute-start(bf16[224,128]{1,0:T(8,128)(2,1)S(1)} %get-tuple-element.116), channel_id=1, source_target_pairs={{0,16},{1,5},{2,18},{3,7},{4,20},{5,1},{6,22},{7,3},{8,24},{9,13},... | collective-permute-start | bytes 172040 | tf_op jit(solution)/shard_map/ppermute | solution.py:334
  119.8 9.3 %collective-permute-start.22 = (bf16[224,128]{1,0:T(8,128)(2,1)S(1)}, bf16[224,128]{1,0:T(8,128)(2,1)S(1)}, u32[]{:S(2)}, u32[]{:S(2)}) collective-permute-start(bf16[224,128]{1,0:T(8,128)(2,1)S(1)} %get-tuple-element.117), channel_id=1, source_target_pairs={{0,24},{1,7},{2,26},{3,1},{4,28},{5,3},{6,30},{7,5},{8,0},{9,15},{... | collective-permute-start | bytes 172040 | tf_op jit(solution)/shard_map/ppermute | solution.py:334
  121.6 7.5 %collective-permute-start.21 = (bf16[224,128]{1,0:T(8,128)(2,1)S(1)}, bf16[224,128]{1,0:T(8,128)(2,1)S(1)}, u32[]{:S(2)}, u32[]{:S(2)}) collective-permute-start(bf16[224,128]{1,0:T(8,128)(2,1)S(1)} %get-tuple-element.118), channel_id=1, source_target_pairs={{0,8},{1,3},{2,10},{3,5},{4,12},{5,7},{6,14},{7,1},{8,16},{9,11},{... | collective-permute-start | bytes 172040 | tf_op jit(solution)/shard_map/ppermute | solution.py:334

commit v4 on v2

--- a/solution.py
+++ b/solution.py
@@ -126,14 +126,6 @@
         copy.wait()
 
 
-def up_weights_kernel(cols, gain, gate, up, out, held, pieces, arrived, gone):
-    def form(held, at):
-        both = jnp.concatenate([held[0, :, at].astype(F32), held[1, :, at].astype(F32)], axis=0)
-        return (both * gain[:, at]).astype(BF16)
-
-    laid_out(form, cols, [gate, up], out, held, pieces, arrived, gone)
-
-
 def down_weights_kernel(cols, down, out, held, pieces, arrived, gone):
     def form(held, at):
         return held[0, :, at].astype(F32).T.astype(BF16)
@@ -161,9 +153,64 @@
     )(*gain, *sources)
 
 
-def up_weights(gain, gate, up, cols):
-    piece = (2 * gate.shape[0], cols)
-    return layout_call(up_weights_kernel, "up_weights", cols, piece, [gate, up], [gain])
+def both_up_kernel(cols, gain, *refs):
+    sources, outs, held, pieces, arrived, gone = refs[:4], refs[4:6], *refs[6:]
+    each = CHUNK // cols
+    steps = held.shape[2] // CHUNK
+    reads = [
+        [
+            pltpu.make_async_copy(
+                source.at[:, step * CHUNK : (step + 1) * CHUNK],
+                held.at[i, :, step * CHUNK : (step + 1) * CHUNK],
+                arrived.at[i, step],
+            )
+            for i, source in enumerate(sources)
+        ]
+        for step in range(steps)
+    ]
+    for row in reads:
+        for copy in row:
+            copy.start()
+    writes = []
+    for step in range(steps):
+        for j, out in enumerate(outs):
+            for copy in reads[step][2 * j : 2 * j + 2]:
+                copy.wait()
+            for i in range(step * each, (step + 1) * each):
+                at = slice(i * cols, (i + 1) * cols)
+                both = jnp.concatenate(
+                    [held[2 * j, :, at].astype(F32), held[2 * j + 1, :, at].astype(F32)], axis=0
+                )
+                pieces[j, i] = (both * gain[:, at]).astype(BF16)
+            write = pltpu.make_async_copy(
+                pieces.at[j, step * each : (step + 1) * each],
+                out.at[step * each : (step + 1) * each],
+                gone.at[j, step],
+            )
+            write.start()
+            writes.append(write)
+    for copy in writes:
+        copy.wait()
+
+
+def up_weights(gain, dense_gate, dense_up, expert_gate, expert_up, cols):
+    units, width = dense_gate.shape
+    shape = (width // cols, 2 * units, cols)
+    return pl.pallas_call(
+        functools.partial(both_up_kernel, cols),
+        out_shape=[jax.ShapeDtypeStruct(shape, BF16)] * 2,
+        in_specs=[IN_VMEM] + [IN_HBM] * 4,
+        out_specs=[IN_HBM] * 2,
+        scratch_shapes=[
+            pltpu.VMEM((4, units, width), BF16),
+            pltpu.VMEM((2,) + shape, BF16),
+            pltpu.SemaphoreType.DMA((4, width // CHUNK)),
+            pltpu.SemaphoreType.DMA((2, width // CHUNK)),
+        ],
+        compiler_params=pltpu.CompilerParams(vmem_limit_bytes=MOST),
+        cost_estimate=SMALL,
+        name="up_weights",
+    )(gain, dense_gate, dense_up, expert_gate, expert_up)
 
 
 def down_weights(down, cols):
@@ -323,10 +370,7 @@
     received = lax.all_to_all(
         outgoing.reshape(experts, capacity, cols), "expert", 0, 0, tiled=True
     ).reshape(experts * capacity, cols)
-    weights = [
-        up_weights(gain, dense_gate, dense_up, cols),
-        up_weights(gain, expert_gate[0], expert_up[0], cols),
-    ]
+    weights = up_weights(gain, dense_gate, dense_up, expert_gate[0], expert_up[0], cols)
     received, weights = lax.optimization_barrier((received, weights))
     own = jnp.concatenate([tokens.T, received.T], axis=1)
 

time: 129 us -> 127 us (0.984)
  Pallas kernels: 41.2 us -> 39.6 us
  waiting for transfers between devices: 31.1 us -> 32.7 us
  blocking collectives: 16.4 us -> 14.8 us
    pallas_call x4 -> x2, Pallas kernels: 20.6 us -> 10.5 us  [layout_call(): pl.pallas_call(functools.partial(kernel, cols), out_shape=jax.ShapeDtypeS...]
    pallas_call x0 -> x1, Pallas kernels: none -> 8.47 us  [up_weights(): pl.pallas_call(functools.partial(both_up_kernel, cols), out_shape=[jax.Sh...]
    all_to_all x1, blocking collectives: 16.4 us -> 14.8 us  [shards(): lax.all_to_all(back, 'expert', 0, 0, tiled=True)]
    all_to_all x1, waiting for transfers between devices: 0.36 us -> 1.99 us  [shards(): lax.all_to_all(outgoing.reshape(experts, capacity, cols), 'expert', 0, 0,...]
  transfers between devices with their start and end apart: 21 -> 21, of which waited for: 8 -> 8; matrix products, arithmetic and copies ran while one was open for 1% -> 1% of each run, Pallas kernels for 27% -> 26%
where the time goes in v4:
time: 127 us; the launch traced here: 126 us
  Pallas kernels  39.6 us (31%)
  waiting for transfers between devices  32.7 us (26%)
  starting transfers between devices  30.2 us (24%)
  blocking collectives  14.8 us (12%)
  local copies, waits for them, and re-layouts  5.89 us (5%)
  other arithmetic  2.08 us (2%)
    ppermute x6, waiting for transfers between devices, level_two(): return lax.ppermute(value, 'tensor', hops(d, False))  23.1 us
    all_to_all x1, blocking collectives, shards(): lax.all_to_all(back, 'expert', 0, 0, tiled=True)  14.8 us
    pallas_call x4, Pallas kernels, arrive(): pl.pallas_call(functools.partial(arrive_kernel, dense_rows, count, start,...  11.2 us
    ppermute x6, starting transfers between devices, level_two(): return lax.ppermute(value, 'tensor', hops(d, False))  10.8 us
    pallas_call x2, Pallas kernels, layout_call(): pl.pallas_call(functools.partial(kernel, cols), out_shape=jax.ShapeDtypeS...  10.5 us
    ppermute x6, starting transfers between devices, level_one(): return lax.ppermute(value, 'tensor', hops(d, True))  9.21 us
    pallas_call x1, Pallas kernels, up_weights(): pl.pallas_call(functools.partial(both_up_kernel, cols), out_shape=[jax.Sh...  8.47 us
    all_to_all x1, starting transfers between devices, shards(): lax.all_to_all(outgoing.reshape(experts, capacity, cols), 'expert', 0, 0,...  8.47 us
  transfers between devices with their start and end apart: 21, of which 8 were waited for; matrix products, arithmetic and copies ran while one was open for 1% of the time, Pallas kernels for 26%

profile of v4, /device:TPU:8, one launch (start us, length us, event | category | flops | bytes accessed | tf_op | source)
XLA Modules:
  0.0 126.5 jit_solution(18106479943670124512)
XLA Ops:
  0.0 1.9 %dispatch.1 = (bf16[384,224]{1,0:T(8,128)(2,1)}, f32[384,128]{1,0:T(8,128)}) custom-call(s32[2,128]{1,0:T(2,128)} %bitcast.58, f32[2,128]{1,0:T(2,128)} %bitcast.59, bf16[224,128]{1,0:T(8,128)(2,1)} %bitcast.54), custom_call_target="tpu_custom_call" | custom-call | tf_op jit(solution)/shard_map/dispatch/pallas_call | solution.py:80
  1.9 8.5 %all-to-all-start = ((bf16[8,48,224]{2,1,0:T(8,128)(2,1)}), bf16[8,48,224]{2,1,0:T(8,128)(2,1)S(1)}, u32[]{:S(2)}, u32[]{:S(2)}) async-start(bf16[8,48,224]{2,1,0:T(8,128)(2,1)} %bitcast.56), calls=%async_computation | async-start | bytes 393216 | tf_op jit(solution)/shard_map/all_to_all | solution.py:370
  10.3 8.5 %up_weights.1 = (bf16[32,304,224]{2,1,0:T(8,128)(2,1)}, bf16[32,304,224]{2,1,0:T(8,128)(2,1)}) custom-call(f32[1,7168]{1,0:T(1,128)} %bitcast.57, bf16[152,7168]{1,0:T(8,128)(2,1)} %refs_0_.1, bf16[152,7168]{1,0:T(8,128)(2,1)} %refs_1_.1, bf16[152,7168]{1,0:T(8,128)(2,1)} %bitcast.44, bf16[152,7168]{1,0:T(8,128)(2,1)} %bitcast.45), custom_call_target="tpu_custom_call" | custom-call | flops 1048576 | bytes 1048576 | tf_op jit(solution)/shard_map/up_weights/pallas_call | solution.py:199
  18.8 2.0 %all-to-all-done = bf16[8,48,224]{2,1,0:T(8,128)(2,1)S(1)} async-done(((bf16[8,48,224]{2,1,0:T(8,128)(2,1)}), bf16[8,48,224]{2,1,0:T(8,128)(2,1)S(1)}, u32[]{:S(2)}, u32[]{:S(2)}) %all-to-all-start) | async-done | bytes 172064 | tf_op jit(solution)/shard_map/all_to_all | solution.py:370
  20.8 0.1 copy.12
  21.0 3.1 %collective-permute-start.1 = (bf16[224,512]{1,0:T(8,128)(2,1)S(1)}, bf16[224,512]{1,0:T(8,128)(2,1)S(1)}, u32[]{:S(2)}, u32[]{:S(2)}) collective-permute-start(bf16[224,512]{1,0:T(8,128)(2,1)S(1)} %get-tuple-element.111), channel_id=1, source_target_pairs={{0,16},{1,5},{2,18},{3,7},{4,20},{5,1},{6,22},{7,3},{8,24},{9,13},... | collective-permute-start | bytes 688136 | tf_op jit(solution)/shard_map/ppermute | solution.py:378
  24.1 0.6 collective-permute-start
  24.7 2.6 %collective-permute-start.2 = (bf16[224,512]{1,0:T(8,128)(2,1)S(1)}, bf16[224,512]{1,0:T(8,128)(2,1)S(1)}, u32[]{:S(2)}, u32[]{:S(2)}) collective-permute-start(bf16[224,512]{1,0:T(8,128)(2,1)S(1)} %get-tuple-element.111), channel_id=1, source_target_pairs={{0,24},{1,7},{2,26},{3,1},{4,28},{5,3},{6,30},{7,5},{8,0},{9,15},{... | collective-permute-start | bytes 688136 | tf_op jit(solution)/shard_map/ppermute | solution.py:378
  27.4 5.3 %down_weights.2.refs_1_.refs_3_ = bf16[32,224,152]{2,1,0:T(8,128)(2,1)} custom-call(bf16[152,7168]{1,0:T(8,128)(2,1)} %bitcast.46), custom_call_target="tpu_custom_call" | custom-call | flops 1048576 | bytes 1048576 | tf_op jit(solution)/shard_map/down_weights/pallas_call | solution.py:139
  32.7 0.0 collective-permute-done.1
  32.7 0.0 collective-permute-done
  32.7 0.0 collective-permute-done.2
  32.7 0.1 pad_maximum_fusion.refs_0_
  32.8 0.1 collective-permute-start.6
  32.9 1.7 %collective-permute-start.5 = (bf16[4,224,512]{2,1,0:T(8,128)(2,1)S(1)}, bf16[4,224,512]{2,1,0:T(8,128)(2,1)}, u32[]{:S(2)}, u32[]{:S(2)}) collective-permute-start(bf16[4,224,512]{2,1,0:T(8,128)(2,1)S(1)} %pad_maximum_fusion.refs_0_), channel_id=1, source_target_pairs={{0,2},{1,9},{2,4},{3,11},{4,6},{5,13},{6,0},{7,15},{8,10},{9,17},{... | collective-permute-start | bytes 2752520 | tf_op jit(solution)/shard_map/ppermute | solution.py:381
  34.6 0.5 collective-permute-start.4
  35.0 2.3 %collective-permute-start.3 = (bf16[4,224,512]{2,1,0:T(8,128)(2,1)S(1)}, bf16[4,224,512]{2,1,0:T(8,128)(2,1)S(1)}, u32[]{:S(2)}, u32[]{:S(2)}) collective-permute-start(bf16[4,224,512]{2,1,0:T(8,128)(2,1)S(1)} %pad_maximum_fusion.refs_0_), channel_id=1, source_target_pairs={{0,4},{1,17},{2,6},{3,19},{4,0},{5,21},{6,2},{7,23},{8,12},{9,25},... | collective-permute-start | bytes 2752520 | tf_op jit(solution)/shard_map/ppermute | solution.py:381
  37.3 5.3 %down_weights.3.refs_0_.refs_2_ = bf16[32,224,152]{2,1,0:T(8,128)(2,1)} custom-call(bf16[152,7168]{1,0:T(8,128)(2,1)} %down.1), custom_call_target="tpu_custom_call" | custom-call | flops 1048576 | bytes 1048576 | tf_op jit(solution)/shard_map/down_weights/pallas_call | solution.py:139
  42.6 0.1 pad_add_fusion.place
  42.7 2.4 %copy-done = bf16[32,304,224]{2,1,0:T(8,128)(2,1)S(1)} copy-done((bf16[32,304,224]{2,1,0:T(8,128)(2,1)S(1)}, bf16[32,304,224]{2,1,0:T(8,128)(2,1)}, u32[]{:S(2)}) %copy-start) | copy-done | bytes 4358168
  45.1 2.4 %copy-done.1 = bf16[32,304,224]{2,1,0:T(8,128)(2,1)S(1)} copy-done((bf16[32,304,224]{2,1,0:T(8,128)(2,1)S(1)}, bf16[32,304,224]{2,1,0:T(8,128)(2,1)}, u32[]{:S(2)}) %copy-start.1) | copy-done | bytes 4358168
  47.5 1.8 %arrive_0_1.1 = (f32[304,128]{1,0:T(8,128)S(1)}, f32[304,384]{1,0:T(8,128)S(1)}, f32[8,512]{1,0:T(8,128)S(1)}) custom-call(s32[3]{0:T(128)S(1)} %pad_add_fusion.place, bf16[4,224,512]{2,1,0:T(8,128)(2,1)S(1)} %pad_maximum_fusion.refs_0_, bf16[32,304,224]{2,1,0:T(8,128)(2,1)S(1)} %copy-done, bf16[32,304,224]{2,1,0:T(8,128)(2,1)S(1)} %copy-done.1), custom_call_target="tpu_custom_call" | custom-call | flops 1048576 | bytes 1048576 | tf_op jit(solution)/shard_map/arrive_0_1/pallas_call | solution.py:283
  49.3 0.0 collective-permute-done.6.refs_0_
  49.3 0.0 collective-permute-done.5.refs_1_
  49.3 0.1 collective-permute-start.9
  49.4 4.0 %arrive_1_2.1 = (f32[304,128]{1,0:T(8,128)S(1)}, f32[304,384]{1,0:T(8,128)S(1)}, f32[8,512]{1,0:T(8,128)S(1)}) custom-call(s32[3]{0:T(128)S(1)} %pad_add_fusion.place, bf16[4,224,512]{2,1,0:T(8,128)(2,1)} %collective-permute-done.6.refs_0_, bf16[4,224,512]{2,1,0:T(8,128)(2,1)} %collective-permute-done.5.refs_1_, bf16[32,304,224]{2,1,0:T(8,128)(2,1)S(1)} %copy-done, ...), custom_call_target="tpu_custom_call" | custom-call | flops 1048576 | bytes 1048576 | tf_op jit(solution)/shard_map/arrive_1_2/pallas_call | solution.py:283
  53.4 0.0 collective-permute-done.4.refs_2_
  53.5 5.1 %collective-permute-done.3.refs_1_ = bf16[4,224,512]{2,1,0:T(8,128)(2,1)S(1)} collective-permute-done((bf16[4,224,512]{2,1,0:T(8,128)(2,1)S(1)}, bf16[4,224,512]{2,1,0:T(8,128)(2,1)S(1)}, u32[]{:S(2)}, u32[]{:S(2)}) %collective-permute-start.3) | collective-permute-done | bytes 917536 | tf_op jit(solution)/shard_map/ppermute | solution.py:381
  58.5 0.5 collective-permute-start.8
  59.0 0.0 collective-permute-done.9.refs_0_
  59.0 2.9 %arrive_3_3.1 = (f32[304,128]{1,0:T(8,128)S(1)}, f32[304,384]{1,0:T(8,128)S(1)}, f32[8,512]{1,0:T(8,128)S(1)}) custom-call(s32[3]{0:T(128)S(1)} %pad_add_fusion.place, bf16[4,224,512]{2,1,0:T(8,128)(2,1)S(1)} %collective-permute-done.9.refs_0_, bf16[4,224,512]{2,1,0:T(8,128)(2,1)S(1)} %collective-permute-done.3.refs_1_, ...), custom_call_target="tpu_custom_call" | custom-call | flops 1048576 | bytes 1048576 | tf_op jit(solution)/shard_map/arrive_3_3/pallas_call | solution.py:283
  61.9 0.0 collective-permute-done.7.refs_0_
  61.9 0.4 collective-permute-done.8.refs_1_
  62.3 2.4 %arrive_3_2.1.hidden = bf16[152,512]{1,0:T(8,128)(2,1)S(1)} custom-call(s32[3]{0:T(128)S(1)} %pad_add_fusion.place, bf16[4,224,512]{2,1,0:T(8,128)(2,1)S(1)} %collective-permute-done.7.refs_0_, bf16[4,224,512]{2,1,0:T(8,128)(2,1)S(1)} %collective-permute-done.8.refs_1_, bf16[32,304,224]{2,1,0:T(8,128)(2,1)S(1)} %copy-done, ...), custom_call_target="tpu_custom_call" | custom-call | flops 1048576 | bytes 1048576 | tf_op jit(solution)/shard_map/arrive_3_2/pallas_call | solution.py:283
  64.8 0.7 copy-done.3
  65.5 1.9 %down_pieces_2.1 = (f32[4,224,512]{2,1,0:T(8,128)S(1)}, bf16[4,224,512]{2,1,0:T(8,128)(2,1)S(1)}) custom-call(s32[3]{0:T(128)S(1)} %pad_add_fusion.place, bf16[152,512]{1,0:T(8,128)(2,1)S(1)} %arrive_3_2.1.hidden, bf16[32,224,152]{2,1,0:T(8,128)(2,1)S(1)} %copy-done.3, bf16[32,224,152]{2,1,0:T(8,128)(2,1)S(1)} %copy-done.2, ...), custom_call_target="tpu_custom_call" | custom-call | flops 1048576 | bytes 1048576 | tf_op jit(solution)/shard_map/down_pieces_2/pallas_call | solution.py:331
  67.3 0.2 collective-permute-start.11
  67.6 1.9 %down_pieces_1.1 = (f32[4,224,512]{2,1,0:T(8,128)S(1)}, bf16[4,224,512]{2,1,0:T(8,128)(2,1)S(1)}) custom-call(s32[3]{0:T(128)S(1)} %pad_add_fusion.place, bf16[152,512]{1,0:T(8,128)(2,1)S(1)} %arrive_3_2.1.hidden, bf16[32,224,152]{2,1,0:T(8,128)(2,1)S(1)} %copy-done.3, bf16[32,224,152]{2,1,0:T(8,128)(2,1)S(1)} %copy-done.2, ...), custom_call_target="tpu_custom_call" | custom-call | flops 1048576 | bytes 1048576 | tf_op jit(solution)/shard_map/down_pieces_1/pallas_call | solution.py:331
  69.5 0.5 collective-permute-start.10
  69.9 0.3 convert_add_fusion.2
  70.2 1.9 %down_pieces_3.1 = (f32[4,224,512]{2,1,0:T(8,128)S(1)}, bf16[4,224,512]{2,1,0:T(8,128)(2,1)S(1)}) custom-call(s32[3]{0:T(128)S(1)} %pad_add_fusion.place, bf16[152,512]{1,0:T(8,128)(2,1)S(1)} %arrive_3_2.1.hidden, bf16[32,224,152]{2,1,0:T(8,128)(2,1)S(1)} %copy-done.3, bf16[32,224,152]{2,1,0:T(8,128)(2,1)S(1)} %copy-done.2, ...), custom_call_target="tpu_custom_call" | custom-call | flops 1048576 | bytes 1048576 | tf_op jit(solution)/shard_map/down_pieces_3/pallas_call | solution.py:331
  72.1 0.2 collective-permute-start.15
  72.4 1.5 %collective-permute-start.13 = (bf16[4,224,512]{2,1,0:T(8,128)(2,1)S(1)}, bf16[4,224,512]{2,1,0:T(8,128)(2,1)S(1)}, u32[]{:S(2)}, u32[]{:S(2)}) collective-permute-start(bf16[4,224,512]{2,1,0:T(8,128)(2,1)S(1)} %convert_add_fusion.2), channel_id=1, source_target_pairs={{0,4},{1,17},{2,6},{3,19},{4,0},{5,21},{6,2},{7,23},{8,12},{9,25},... | collective-permute-start | bytes 2752520 | tf_op jit(solution)/shard_map/ppermute | solution.py:381
  73.8 0.4 convert_add_fusion.3
  74.2 1.9 %down_pieces_0.1 = (f32[4,224,512]{2,1,0:T(8,128)S(1)}, bf16[4,224,512]{2,1,0:T(8,128)(2,1)S(1)}) custom-call(s32[3]{0:T(128)S(1)} %pad_add_fusion.place, bf16[152,512]{1,0:T(8,128)(2,1)S(1)} %arrive_3_2.1.hidden, bf16[32,224,152]{2,1,0:T(8,128)(2,1)S(1)} %copy-done.3, bf16[32,224,152]{2,1,0:T(8,128)(2,1)S(1)} %copy-done.2, ...), custom_call_target="tpu_custom_call" | custom-call | flops 1048576 | bytes 1048576 | tf_op jit(solution)/shard_map/down_pieces_0/pallas_call | solution.py:331
  76.1 0.1 collective-permute-start.12
  76.2 2.8 %collective-permute-start.14 = (bf16[4,224,512]{2,1,0:T(8,128)(2,1)S(1)}, bf16[4,224,512]{2,1,0:T(8,128)(2,1)S(1)}, u32[]{:S(2)}, u32[]{:S(2)}) collective-permute-start(bf16[4,224,512]{2,1,0:T(8,128)(2,1)S(1)} %convert_add_fusion.3), channel_id=1, source_target_pairs={{0,2},{1,9},{2,4},{3,11},{4,6},{5,13},{6,0},{7,15},{8,10},{9,17},{... | collective-permute-start | bytes 2752520 | tf_op jit(solution)/shard_map/ppermute | solution.py:381
  79.0 0.0 collective-permute-done.15
  79.1 0.4 convert_add_fusion.1
  79.4 2.1 %collective-permute-start.16 = (bf16[4,224,512]{2,1,0:T(8,128)(2,1)S(1)}, bf16[4,224,512]{2,1,0:T(8,128)(2,1)S(1)}, u32[]{:S(2)}, u32[]{:S(2)}) collective-permute-start(bf16[4,224,512]{2,1,0:T(8,128)(2,1)S(1)} %convert_add_fusion.1), channel_id=1, source_target_pairs={{0,6},{1,25},{2,0},{3,27},{4,2},{5,29},{6,4},{7,31},{8,14},{9,1},{... | collective-permute-start | bytes 2752520 | tf_op jit(solution)/shard_map/ppermute | solution.py:381
  81.5 5.9 %collective-permute-done.13 = bf16[4,224,512]{2,1,0:T(8,128)(2,1)S(1)} collective-permute-done((bf16[4,224,512]{2,1,0:T(8,128)(2,1)S(1)}, bf16[4,224,512]{2,1,0:T(8,128)(2,1)S(1)}, u32[]{:S(2)}, u32[]{:S(2)}) %collective-permute-start.13) | collective-permute-done | bytes 917536 | tf_op jit(solution)/shard_map/ppermute | solution.py:381
  87.4 0.0 collective-permute-done.12
  87.4 12.2 %collective-permute-done.14 = bf16[4,224,512]{2,1,0:T(8,128)(2,1)S(1)} collective-permute-done((bf16[4,224,512]{2,1,0:T(8,128)(2,1)S(1)}, bf16[4,224,512]{2,1,0:T(8,128)(2,1)S(1)}, u32[]{:S(2)}, u32[]{:S(2)}) %collective-permute-start.14) | collective-permute-done | bytes 917536 | tf_op jit(solution)/shard_map/ppermute | solution.py:381
  99.6 0.7 fusion.7
  100.3 0.7 collective-permute-start.17
  101.0 2.1 %collective-permute-start.19 = (bf16[224,512]{1,0:T(8,128)(2,1)S(1)}, bf16[224,512]{1,0:T(8,128)(2,1)S(1)}, u32[]{:S(2)}, u32[]{:S(2)}) collective-permute-start(bf16[224,512]{1,0:T(8,128)(2,1)S(1)} %get-tuple-element.108), channel_id=1, source_target_pairs={{0,24},{1,7},{2,26},{3,1},{4,28},{5,3},{6,30},{7,5},{8,0},{9,15},{... | collective-permute-start | bytes 688136 | tf_op jit(solution)/shard_map/ppermute | solution.py:378
  103.1 0.1 collective-permute-start.18
  103.2 4.8 %collective-permute-done.17 = bf16[224,512]{1,0:T(8,128)(2,1)S(1)} collective-permute-done((bf16[224,512]{1,0:T(8,128)(2,1)S(1)}, bf16[224,512]{1,0:T(8,128)(2,1)S(1)}, u32[]{:S(2)}, u32[]{:S(2)}) %collective-permute-start.17) | collective-permute-done | bytes 229408 | tf_op jit(solution)/shard_map/ppermute | solution.py:378
  107.9 1.7 %collective-permute-done.19 = bf16[224,512]{1,0:T(8,128)(2,1)S(1)} collective-permute-done((bf16[224,512]{1,0:T(8,128)(2,1)S(1)}, bf16[224,512]{1,0:T(8,128)(2,1)S(1)}, u32[]{:S(2)}, u32[]{:S(2)}) %collective-permute-start.19) | collective-permute-done | bytes 229408 | tf_op jit(solution)/shard_map/ppermute | solution.py:378
  109.7 0.7 collective-permute-done.18
  110.4 0.1 fusion.2
  110.5 0.1 copy.13
  110.7 14.8 %all_to_all.10 = bf16[8,48,224]{2,1,0:T(8,128)(2,1)S(1)} all-to-all(bf16[8,48,224]{2,1,0:T(8,128)(2,1)S(1)} %bitcast.49), channel_id=1, replica_groups=mesh['expert'=8,'tensor'=32] {'expert'}, dimensions={0} | all-to-all | bytes 344064 | tf_op jit(solution)/shard_map/all_to_all | solution.py:416
  125.5 1.0 fusion.5
  (16 shorter events, 0.1 us)
Async XLA Ops:
  1.9 18.9 %all-to-all-start = ((bf16[8,48,224]{2,1,0:T(8,128)(2,1)}), bf16[8,48,224]{2,1,0:T(8,128)(2,1)S(1)}, u32[]{:S(2)}, u32[]{:S(2)}) async-start(bf16[8,48,224]{2,1,0:T(8,128)(2,1)} %bitcast.56), calls=%async_computation | async-start | bytes 393216 | tf_op jit(solution)/shard_map/all_to_all | solution.py:370
  10.3 10.6 %copy-start.4 = (bf16[128,224]{0,1:T(8,128)(2,1)S(1)}, bf16[128,224]{0,1:T(8,128)(2,1)}, u32[]{:S(2)}) copy-start(bf16[128,224]{0,1:T(8,128)(2,1)} %param.10) | copy-start | bytes 172036
  21.0 11.6 %collective-permute-start.1 = (bf16[224,512]{1,0:T(8,128)(2,1)S(1)}, bf16[224,512]{1,0:T(8,128)(2,1)S(1)}, u32[]{:S(2)}, u32[]{:S(2)}) collective-permute-start(bf16[224,512]{1,0:T(8,128)(2,1)S(1)} %get-tuple-element.111), channel_id=1, source_target_pairs={{0,16},{1,5},{2,18},{3,7},{4,20},{5,1},{6,22},{7,3},{8,24},{9,13},... | collective-permute-start | bytes 688136 | tf_op jit(solution)/shard_map/ppermute | solution.py:378
  24.1 8.5 %collective-permute-start = (bf16[224,512]{1,0:T(8,128)(2,1)S(1)}, bf16[224,512]{1,0:T(8,128)(2,1)S(1)}, u32[]{:S(2)}, u32[]{:S(2)}) collective-permute-start(bf16[224,512]{1,0:T(8,128)(2,1)S(1)} %get-tuple-element.111), channel_id=1, source_target_pairs={{0,8},{1,3},{2,10},{3,5},{4,12},{5,7},{6,14},{7,1},{8,16},{9,11},{... | collective-permute-start | bytes 688136 | tf_op jit(solution)/shard_map/ppermute | solution.py:378
  24.7 7.9 %collective-permute-start.2 = (bf16[224,512]{1,0:T(8,128)(2,1)S(1)}, bf16[224,512]{1,0:T(8,128)(2,1)S(1)}, u32[]{:S(2)}, u32[]{:S(2)}) collective-permute-start(bf16[224,512]{1,0:T(8,128)(2,1)S(1)} %get-tuple-element.111), channel_id=1, source_target_pairs={{0,24},{1,7},{2,26},{3,1},{4,28},{5,3},{6,30},{7,5},{8,0},{9,15},{... | collective-permute-start | bytes 688136 | tf_op jit(solution)/shard_map/ppermute | solution.py:378
  32.8 16.5 %collective-permute-start.6 = (bf16[4,224,512]{2,1,0:T(8,128)(2,1)S(1)}, bf16[4,224,512]{2,1,0:T(8,128)(2,1)}, u32[]{:S(2)}, u32[]{:S(2)}) collective-permute-start(bf16[4,224,512]{2,1,0:T(8,128)(2,1)S(1)} %pad_maximum_fusion.refs_0_), channel_id=1, source_target_pairs={{0,1},{1,0},{2,3},{3,2},{4,5},{5,4},{6,7},{7,6},{8,9},{9,8},{10,11... | collective-permute-start | bytes 2752520 | tf_op jit(solution)/shard_map/ppermute | solution.py:39
  32.9 16.4 %collective-permute-start.5 = (bf16[4,224,512]{2,1,0:T(8,128)(2,1)S(1)}, bf16[4,224,512]{2,1,0:T(8,128)(2,1)}, u32[]{:S(2)}, u32[]{:S(2)}) collective-permute-start(bf16[4,224,512]{2,1,0:T(8,128)(2,1)S(1)} %pad_maximum_fusion.refs_0_), channel_id=1, source_target_pairs={{0,2},{1,9},{2,4},{3,11},{4,6},{5,13},{6,0},{7,15},{8,10},{9,17},{... | collective-permute-start | bytes 2752520 | tf_op jit(solution)/shard_map/ppermute | solution.py:381
  34.6 18.9 %collective-permute-start.4 = (bf16[4,224,512]{2,1,0:T(8,128)(2,1)S(1)}, bf16[4,224,512]{2,1,0:T(8,128)(2,1)S(1)}, u32[]{:S(2)}, u32[]{:S(2)}) collective-permute-start(bf16[4,224,512]{2,1,0:T(8,128)(2,1)S(1)} %pad_maximum_fusion.refs_0_), channel_id=1, source_target_pairs={{0,6},{1,25},{2,0},{3,27},{4,2},{5,29},{6,4},{7,31},{8,14},{9,1},{... | collective-permute-start | bytes 2752520 | tf_op jit(solution)/shard_map/ppermute | solution.py:381
  35.0 23.5 %collective-permute-start.3 = (bf16[4,224,512]{2,1,0:T(8,128)(2,1)S(1)}, bf16[4,224,512]{2,1,0:T(8,128)(2,1)S(1)}, u32[]{:S(2)}, u32[]{:S(2)}) collective-permute-start(bf16[4,224,512]{2,1,0:T(8,128)(2,1)S(1)} %pad_maximum_fusion.refs_0_), channel_id=1, source_target_pairs={{0,4},{1,17},{2,6},{3,19},{4,0},{5,21},{6,2},{7,23},{8,12},{9,25},... | collective-permute-start | bytes 2752520 | tf_op jit(solution)/shard_map/ppermute | solution.py:381
  42.7 2.4 %copy-start = (bf16[32,304,224]{2,1,0:T(8,128)(2,1)S(1)}, bf16[32,304,224]{2,1,0:T(8,128)(2,1)}, u32[]{:S(2)}) copy-start(bf16[32,304,224]{2,1,0:T(8,128)(2,1)} %get-tuple-element.62.refs_1_.refs_2_.refs_3_.refs_4_.refs_5_) | copy-start | bytes 13074436
  45.1 2.4 %copy-start.1 = (bf16[32,304,224]{2,1,0:T(8,128)(2,1)S(1)}, bf16[32,304,224]{2,1,0:T(8,128)(2,1)}, u32[]{:S(2)}) copy-start(bf16[32,304,224]{2,1,0:T(8,128)(2,1)} %get-tuple-element.63.refs_2_.refs_4_.refs_5_.refs_6_.refs_7_.refs_8_) | copy-start | bytes 13074436
  49.3 9.7 %collective-permute-start.9 = (bf16[4,224,512]{2,1,0:T(8,128)(2,1)}, bf16[4,224,512]{2,1,0:T(8,128)(2,1)S(1)}, u32[]{:S(2)}, u32[]{:S(2)}) collective-permute-start(bf16[4,224,512]{2,1,0:T(8,128)(2,1)} %collective-permute-done.5.refs_1_), channel_id=1, source_target_pairs={{0,1},{1,0},{2,3},{3,2},{4,5},{5,4},{6,7},{7,6},{8,9},{9,8},{10,11... | collective-permute-start | bytes 2752520 | tf_op jit(solution)/shard_map/ppermute | solution.py:39
  58.5 3.4 %collective-permute-start.7 = (bf16[4,224,512]{2,1,0:T(8,128)(2,1)S(1)}, bf16[4,224,512]{2,1,0:T(8,128)(2,1)S(1)}, u32[]{:S(2)}, u32[]{:S(2)}) collective-permute-start(bf16[4,224,512]{2,1,0:T(8,128)(2,1)S(1)} %collective-permute-done.3.refs_1_), channel_id=1, source_target_pairs={{0,1},{1,0},{2,3},{3,2},{4,5},{5,4},{6,7},{7,6},{8,9},{9,8},{10,11... | collective-permute-start | bytes 2752520 | tf_op jit(solution)/shard_map/ppermute | solution.py:39
  58.5 3.8 %collective-permute-start.8 = (bf16[4,224,512]{2,1,0:T(8,128)(2,1)S(1)}, bf16[4,224,512]{2,1,0:T(8,128)(2,1)S(1)}, u32[]{:S(2)}, u32[]{:S(2)}) collective-permute-start(bf16[4,224,512]{2,1,0:T(8,128)(2,1)S(1)} %collective-permute-done.4.refs_2_), channel_id=1, source_target_pairs={{0,1},{1,0},{2,3},{3,2},{4,5},{5,4},{6,7},{7,6},{8,9},{9,8},{10,11... | collective-permute-start | bytes 2752520 | tf_op jit(solution)/shard_map/ppermute | solution.py:39
  62.3 2.5 %copy-start.2 = (bf16[32,224,152]{2,1,0:T(8,128)(2,1)S(1)}, bf16[32,224,152]{2,1,0:T(8,128)(2,1)}, u32[]{:S(2)}) copy-start(bf16[32,224,152]{2,1,0:T(8,128)(2,1)} %down_weights.2.refs_1_.refs_3_) | copy-start | bytes 6537220
  62.3 3.2 %copy-start.3 = (bf16[32,224,152]{2,1,0:T(8,128)(2,1)S(1)}, bf16[32,224,152]{2,1,0:T(8,128)(2,1)}, u32[]{:S(2)}) copy-start(bf16[32,224,152]{2,1,0:T(8,128)(2,1)} %down_weights.3.refs_0_.refs_2_) | copy-start | bytes 6537220
  67.3 2.6 %collective-permute-start.11 = (bf16[4,224,512]{2,1,0:T(8,128)(2,1)S(1)}, bf16[4,224,512]{2,1,0:T(8,128)(2,1)S(1)}, u32[]{:S(2)}, u32[]{:S(2)}) collective-permute-start(bf16[4,224,512]{2,1,0:T(8,128)(2,1)S(1)} %get-tuple-element.94), channel_id=1, source_target_pairs={{0,1},{1,0},{2,3},{3,2},{4,5},{5,4},{6,7},{7,6},{8,9},{9,8},{10,11... | collective-permute-start | bytes 2752520 | tf_op jit(solution)/shard_map/ppermute | solution.py:39
  69.5 4.4 %collective-permute-start.10 = (bf16[4,224,512]{2,1,0:T(8,128)(2,1)S(1)}, bf16[4,224,512]{2,1,0:T(8,128)(2,1)S(1)}, u32[]{:S(2)}, u32[]{:S(2)}) collective-permute-start(bf16[4,224,512]{2,1,0:T(8,128)(2,1)S(1)} %get-tuple-element.92), channel_id=1, source_target_pairs={{0,1},{1,0},{2,3},{3,2},{4,5},{5,4},{6,7},{7,6},{8,9},{9,8},{10,11... | collective-permute-start | bytes 2752520 | tf_op jit(solution)/shard_map/ppermute | solution.py:39
  72.1 6.9 %collective-permute-start.15 = (bf16[4,224,512]{2,1,0:T(8,128)(2,1)S(1)}, bf16[4,224,512]{2,1,0:T(8,128)(2,1)S(1)}, u32[]{:S(2)}, u32[]{:S(2)}) collective-permute-start(bf16[4,224,512]{2,1,0:T(8,128)(2,1)S(1)} %get-tuple-element.102), channel_id=1, source_target_pairs={{0,1},{1,0},{2,3},{3,2},{4,5},{5,4},{6,7},{7,6},{8,9},{9,8},{10,11... | collective-permute-start | bytes 2752520 | tf_op jit(solution)/shard_map/ppermute | solution.py:39
  72.4 15.0 %collective-permute-start.13 = (bf16[4,224,512]{2,1,0:T(8,128)(2,1)S(1)}, bf16[4,224,512]{2,1,0:T(8,128)(2,1)S(1)}, u32[]{:S(2)}, u32[]{:S(2)}) collective-permute-start(bf16[4,224,512]{2,1,0:T(8,128)(2,1)S(1)} %convert_add_fusion.2), channel_id=1, source_target_pairs={{0,4},{1,17},{2,6},{3,19},{4,0},{5,21},{6,2},{7,23},{8,12},{9,25},... | collective-permute-start | bytes 2752520 | tf_op jit(solution)/shard_map/ppermute | solution.py:381
  76.1 11.3 %collective-permute-start.12 = (bf16[4,224,512]{2,1,0:T(8,128)(2,1)S(1)}, bf16[4,224,512]{2,1,0:T(8,128)(2,1)S(1)}, u32[]{:S(2)}, u32[]{:S(2)}) collective-permute-start(bf16[4,224,512]{2,1,0:T(8,128)(2,1)S(1)} %get-tuple-element.98), channel_id=1, source_target_pairs={{0,1},{1,0},{2,3},{3,2},{4,5},{5,4},{6,7},{7,6},{8,9},{9,8},{10,11... | collective-permute-start | bytes 2752520 | tf_op jit(solution)/shard_map/ppermute | solution.py:39
  76.2 23.4 %collective-permute-start.14 = (bf16[4,224,512]{2,1,0:T(8,128)(2,1)S(1)}, bf16[4,224,512]{2,1,0:T(8,128)(2,1)S(1)}, u32[]{:S(2)}, u32[]{:S(2)}) collective-permute-start(bf16[4,224,512]{2,1,0:T(8,128)(2,1)S(1)} %convert_add_fusion.3), channel_id=1, source_target_pairs={{0,2},{1,9},{2,4},{3,11},{4,6},{5,13},{6,0},{7,15},{8,10},{9,17},{... | collective-permute-start | bytes 2752520 | tf_op jit(solution)/shard_map/ppermute | solution.py:381
  79.4 20.1 %collective-permute-start.16 = (bf16[4,224,512]{2,1,0:T(8,128)(2,1)S(1)}, bf16[4,224,512]{2,1,0:T(8,128)(2,1)S(1)}, u32[]{:S(2)}, u32[]{:S(2)}) collective-permute-start(bf16[4,224,512]{2,1,0:T(8,128)(2,1)S(1)} %convert_add_fusion.1), channel_id=1, source_target_pairs={{0,6},{1,25},{2,0},{3,27},{4,2},{5,29},{6,4},{7,31},{8,14},{9,1},{... | collective-permute-start | bytes 2752520 | tf_op jit(solution)/shard_map/ppermute | solution.py:381
  100.3 25.2 %copy-start.5 = (f32[384,128]{1,0:T(8,128)S(1)}, f32[384,128]{1,0:T(8,128)}, u32[]{:S(2)}) copy-start(f32[384,128]{1,0:T(8,128)} %get-tuple-element.104) | copy-start | bytes 589828
  100.3 7.6 %collective-permute-start.17 = (bf16[224,512]{1,0:T(8,128)(2,1)S(1)}, bf16[224,512]{1,0:T(8,128)(2,1)S(1)}, u32[]{:S(2)}, u32[]{:S(2)}) collective-permute-start(bf16[224,512]{1,0:T(8,128)(2,1)S(1)} %get-tuple-element.107), channel_id=1, source_target_pairs={{0,16},{1,5},{2,18},{3,7},{4,20},{5,1},{6,22},{7,3},{8,24},{9,13},... | collective-permute-start | bytes 688136 | tf_op jit(solution)/shard_map/ppermute | solution.py:378
  101.0 8.7 %collective-permute-start.19 = (bf16[224,512]{1,0:T(8,128)(2,1)S(1)}, bf16[224,512]{1,0:T(8,128)(2,1)S(1)}, u32[]{:S(2)}, u32[]{:S(2)}) collective-permute-start(bf16[224,512]{1,0:T(8,128)(2,1)S(1)} %get-tuple-element.108), channel_id=1, source_target_pairs={{0,24},{1,7},{2,26},{3,1},{4,28},{5,3},{6,30},{7,5},{8,0},{9,15},{... | collective-permute-start | bytes 688136 | tf_op jit(solution)/shard_map/ppermute | solution.py:378
  103.1 7.3 %collective-permute-start.18 = (bf16[224,512]{1,0:T(8,128)(2,1)S(1)}, bf16[224,512]{1,0:T(8,128)(2,1)S(1)}, u32[]{:S(2)}, u32[]{:S(2)}) collective-permute-start(bf16[224,512]{1,0:T(8,128)(2,1)S(1)} %get-tuple-element.109), channel_id=1, source_target_pairs={{0,8},{1,3},{2,10},{3,5},{4,12},{5,7},{6,14},{7,1},{8,16},{9,11},{... | collective-permute-start | bytes 688136 | tf_op jit(solution)/shard_map/ppermute | solution.py:378
